TPU v7x, 32 devices: a whole 2x2x4 slice. The times are simulated.
32 devices in a mesh: obs: 2 (over x), chan: 16 (over z, y, core).
Axes of the slice: x: 2, y: 2, z: 4, core: 2. Of those that a mesh axis runs over, the one named last changes fastest.
Arguments:
- visibilities: bfloat16 [2, 8192, 384], P(None, ('obs', 'chan')), parts along dimension 1, may hold values from -6 to 6
- kernel: bfloat16 [4, 8192, 128], P(None, ('obs', 'chan')), parts along dimension 1, may hold values from -0.09375 to 0.09375
- weights: int32 [8192], P(('obs', 'chan')), parts along dimension 0, may hold values from 1 to 4
- counts: int32 [8192], P(('obs', 'chan')), parts along dimension 0, may hold values from 1 to 4, as said below
- blocks: int32 [4, 8192], P(None, ('obs', 'chan')), parts along dimension 1, may hold values from 0 to 15, as said below
- inv_cov: bfloat16 [384, 384], replicated, as said below
Outputs:
- delay_cube: float32 [2, 384, 4096], P(None, None, ('obs', 'chan')), parts along dimension 2
There are 2 independent parts, one for each index of `obs`. A program takes and returns all parts, laid end to end along the dimension named above; an argument that names none is the same for every part. Nothing has to cross between parts.
Inputs may be any that keep to these rules, and one draw needn't show every extreme that they name: Each sample's used blocks are the first counts of its list; the most is reached in every draw. `blocks`: row j of a sample's list is its row 0 plus j modulo 16. In each aligned group of 16 samples, row 0 holds every block number exactly once. `inv_cov`: Symmetric.
All inputs are finite; a program needn't handle non-finite values.
Results may differ from a plain program's by a relative error of at most 0.0049.
Values may be sent and summed in bfloat16 or wider, within the bound.
No kernel may reach another device: no remote copies, remote signals or barrier semaphores. Data moves between devices by JAX's collectives and lax.ppermute only.
A program may use at most 256 MiB of HBM per device.

v0:
```python
import math

import jax
import jax.numpy as jnp
from jax import lax
from jax.sharding import PartitionSpec as P

NCH = 384
MAXB = 4


def weigh_kernel(kernel, weights, counts):
    live = jnp.arange(MAXB, dtype=jnp.int32)[:, None] < counts[None, :]
    scaled = kernel.astype(jnp.float32) * weights.astype(jnp.float32)[None, :, None]
    return jnp.where(live[:, :, None], scaled, jnp.zeros_like(scaled)).astype(jnp.bfloat16)


def grid_samples(vis_rows, weighted, starts, nblocks):
    cells = weighted.shape[2]
    cell_groups = starts.shape[0] // nblocks
    labels = jnp.arange(nblocks, dtype=jnp.int32)
    place_samples = (
        starts.reshape(cell_groups, nblocks)[:, :, None] == labels[None, None, :]
    ).astype(jnp.bfloat16)
    sample_rows = vis_rows.reshape(vis_rows.shape[0], cell_groups, nblocks)
    sorted_rows = jnp.einsum(
        "xiy,iyh->xih", sample_rows, place_samples, preferred_element_type=jnp.float32
    ).astype(jnp.bfloat16)
    summed = jnp.zeros((vis_rows.shape[0], nblocks, cells), jnp.float32)
    for offset in range(weighted.shape[0]):
        grouped_visibilities = weighted[offset].reshape(cell_groups, nblocks, cells)
        sorted_kernel = jnp.einsum(
            "lun,lup->lpn", grouped_visibilities, place_samples, preferred_element_type=jnp.float32
        ).astype(jnp.bfloat16)
        placed = jnp.einsum(
            "cgt,gtk->ctk", sorted_rows, sorted_kernel, preferred_element_type=jnp.float32
        )
        summed = summed + jnp.roll(placed, offset, axis=1)
    return summed.reshape(vis_rows.shape[0], nblocks * cells)


def delay_transform(columns, inv_cov):
    filtered = jnp.einsum(
        "gh,chn->cgn", inv_cov, columns, preferred_element_type=jnp.float32
    ).astype(jnp.bfloat16)
    index = jnp.arange(NCH, dtype=jnp.int32)
    product = index[:, None] * index[None, :] % NCH
    angle = product.astype(jnp.float32) * (2.0 * math.pi / NCH)
    cosine_lookup = jnp.cos(angle).astype(jnp.bfloat16)
    sin_table = jnp.sin(angle).astype(jnp.bfloat16)
    real_part = jnp.dot(cosine_lookup, filtered[0], preferred_element_type=jnp.float32) + jnp.dot(
        sin_table, filtered[1], preferred_element_type=jnp.float32
    )
    imag_part = jnp.dot(cosine_lookup, filtered[1], preferred_element_type=jnp.float32) - jnp.dot(
        sin_table, filtered[0], preferred_element_type=jnp.float32
    )
    return jnp.stack([real_part, imag_part]) * (1.0 / math.sqrt(NCH))


def on_device(visibilities, kernel, weights, counts, blocks, inv_cov):
    nblocks = lax.axis_size("chan")
    cells_all = nblocks * kernel.shape[2]
    weighted = weigh_kernel(kernel, weights, counts)
    vis_owned = lax.all_to_all(visibilities, "chan", split_axis=2, concat_axis=1, tiled=True)
    kernel_all, blocks_all = (
        lax.all_gather(weighted, "chan", axis=1, tiled=True),
        lax.all_gather(blocks, "chan", axis=1, tiled=True),
    )
    channels = vis_owned.shape[2]
    vis_rows = vis_owned.transpose(0, 2, 1).reshape(2 * channels, vis_owned.shape[1])
    gridded_samples = grid_samples(vis_rows, kernel_all, blocks_all[0], nblocks).reshape(
        2, channels, cells_all
    )
    columns = lax.all_to_all(
        gridded_samples.astype(jnp.bfloat16), "chan", split_axis=2, concat_axis=1, tiled=True
    )
    return delay_transform(columns, inv_cov)


def solution(mesh):
    placed = (
        P(None, ("obs", "chan"), None),
        P(None, ("obs", "chan"), None),
        P(("obs", "chan")),
        P(("obs", "chan")),
        P(None, ("obs", "chan")),
        P(),
    )
    return jax.shard_map(
        on_device,
        mesh=mesh,
        in_specs=placed,
        out_specs=P(None, None, ("obs", "chan")),
        check_vma=False,
    )
```

profile of v0, /device:TPU:0, one launch (start us, length us, event | category | flops | bytes accessed | tf_op | source)
XLA Modules:
  0.0 109.9 jit_solution(14194290360095746892)
XLA Ops:
  6.5 0.0 copy-start
  6.5 0.0 copy-start.3
  6.5 0.0 all-gather.2.cloned.1.call-start
  6.5 0.7 convert_element_type.62
  7.3 0.7 iota_compare_fusion.18
  8.0 1.9 %select_convert_fusion = bf16[4,256,128]{2,1,0:T(8,128)(2,1)} fusion(bf16[4,256,128]{2,1,0:T(8,128)(2,1)} %param.7, f32[256]{0:T(256)S(1)} %convert_element_type.62, pred[4,256]{1,0:T(4,128)(4,1)S(1)} %iota_compare_fusion.18), kind=kLoop, calls=%fused_computation.44 | loop fusion | flops 524288 | bytes 526336 | tf_op jit(solution)/shard_map/convert_element_type | solution.py:15
  9.9 0.0 all-gather.2.cloned.1.call-update
  9.9 2.0 %copy.34 = bf16[2,256,384]{1,0,2:T(2,128)(2,1)} copy(bf16[2,256,384]{2,1,0:T(8,128)(2,1)} %param.6) | data formatting | bytes 786432 | tf_op args[0]
  11.9 7.4 %all-to-all-start = ((bf16[2,256,384]{1,0,2:T(2,128)(2,1)}), bf16[2,256,384]{1,0,2:T(2,128)(2,1)S(1)}, u32[]{:S(2)}, u32[]{:S(2)}) async-start(bf16[2,256,384]{1,0,2:T(2,128)(2,1)} %copy.34), calls=%async_computation | async-start | bytes 786432 | tf_op jit(solution)/shard_map/all_to_all | solution.py:64
  19.3 0.0 copy-done.3
  19.3 27.8 %all_gather.6 = s32[4,4096]{1,0:T(4,128)S(1)} all-gather(s32[4,256]{1,0:T(4,128)S(1)} %copy-done.3), channel_id=1, replica_groups=mesh['obs'=2,'chan'=16] {'chan'}, dimensions={1}, use_global_device_ids=true | all-gather | bytes 69632 | tf_op jit(solution)/shard_map/all_gather | solution.py:67
  47.1 0.1 eq.17
  47.2 0.0 all-to-all-done
  47.3 2.8 %copy.37 = bf16[2,24,4096]{1,0,2:T(2,128)(2,1)S(1)} copy(bf16[2,24,4096]{2,1,0:T(8,128)(2,1)S(1)} %bitcast.74) | data formatting | bytes 786432 | tf_op jit(solution)/shard_map/transpose | solution.py:70
  50.1 1.8 %reshape_reshape.4 = bf16[48,256,16]{0,2,1:T(8,128)(2,1)} reshape(bf16[2,24,4096]{1,0,2:T(2,128)(2,1)S(1)} %copy.37) | data formatting | bytes 786432 | tf_op jit(solution)/shard_map/reshape;reshape | solution.py:25
  51.9 1.8 %fusion.10 = bf16[48,256,16]{0,2,1:T(8,128)(2,1)S(1)} fusion(bf16[48,256,16]{0,2,1:T(8,128)(2,1)} %reshape_reshape.4, s32[256,16]{1,0:T(8,128)S(1)} %eq.17), kind=kOutput, calls=%fused_computation.11 | convolution fusion | flops 6553600 | bytes 802816 | tf_op jit(solution)/shard_map/xiy,iyh->xih/dot_general | solution.py:26
  53.6 0.8 copy.39
  54.5 14.9 %all-gather.2.cloned.1.call-done = bf16[4,4096,128]{2,1,0:T(8,128)(2,1)} async-done(((bf16[4,256,128]{2,1,0:T(8,128)(2,1)}), bf16[4,4096,128]{2,1,0:T(8,128)(2,1)}) %all-gather.2.cloned.1.call-update) | async-done | bytes 4194320 | tf_op jit(solution)/shard_map/all_gather | solution.py:66
  69.3 2.4 %fusion.47 = (bf16[1,4096,128]{2,1,0:T(8,128)(2,1)S(1)}, bf16[1,4096,128]{2,1,0:T(8,128)(2,1)S(1)}, bf16[1,4096,128]{2,1,0:T(8,128)(2,1)S(1)}, bf16[1,4096,128]{2,1,0:T(8,128)(2,1)S(1)}) fusion(bf16[4,4096,128]{2,1,0:T(8,128)(2,1)} %all-gather.2.cloned.1.call-done), kind=kLoop, calls=%fused_computation.65 | loop fusion | bytes 8388608 | tf_op jit(solution)/shard_map/slice | solution.py:31
  71.8 0.5 fusion.7
  72.3 0.4 convolution_bitcast_fusion.2
  72.7 0.0 copy-start.1
  72.7 0.5 fusion.8
  73.3 0.4 convolution_bitcast_fusion.1
  73.6 0.0 copy-done.1
  73.6 0.0 copy-start.2
  73.7 0.5 fusion.9
  74.2 0.0 slice-start
  74.2 0.0 slice-start.1
  74.2 0.4 convolution_bitcast_fusion
  74.6 0.0 copy-done.2
  74.6 0.0 slice-start.2
  74.6 0.0 slice-start.3
  74.7 0.5 fusion.5
  75.2 0.0 slice-done
  75.2 0.0 slice-done.1
  75.2 0.2 slice-done.2
  75.5 0.2 slice-done.3
  75.7 0.4 fusion.14
  76.1 0.3 copy.52
  76.4 0.4 reshape.22
  76.8 1.3 %reshape.30 = bf16[16,2,3072]{2,1,0:T(2,128)(2,1)S(1)} reshape(bf16[2048,2,24]{2,1,0:T(2,128)(2,1)S(1)} %bitcast.67) | data formatting | bytes 393216
  78.1 12.0 %all_to_all.36 = bf16[16,2,3072]{2,1,0:T(2,128)(2,1)S(1)} all-to-all(bf16[16,2,3072]{2,1,0:T(2,128)(2,1)S(1)} %reshape.30), channel_id=1, replica_groups=mesh['obs'=2,'chan'=16] {'chan'}, dimensions={0} | all-to-all | bytes 393216 | tf_op jit(solution)/shard_map/all_to_all | solution.py:74
  90.1 1.5 %reshape.31 = bf16[2048,2,24]{2,1,0:T(2,128)(2,1)S(1)} reshape(bf16[16,2,3072]{2,1,0:T(2,128)(2,1)S(1)} %all_to_all.36) | data formatting | bytes 393216
  91.6 0.7 copy.54
  92.3 0.0 copy-done
  92.3 0.3 fusion.15
  92.6 2.4 %fusion.33 = f32[384,128]{1,0:T(8,128)S(1)} fusion(bf16[2,384,128]{1,2,0:T(8,128)(2,1)S(1)} %fusion.15), kind=kOutput, calls=%fused_computation.47 | convolution fusion | flops 39223296 | bytes 294912 | tf_op jit(solution)/shard_map/dot_general | solution.py:54
  95.0 2.4 %fusion.34 = f32[384,128]{1,0:T(8,128)S(1)} fusion(bf16[2,384,128]{1,2,0:T(8,128)(2,1)S(1)} %fusion.15), kind=kOutput, calls=%fused_computation.48 | convolution fusion | flops 39223296 | bytes 294912 | tf_op jit(solution)/shard_map/dot_general | solution.py:51
  97.4 2.4 %fusion.16 = f32[1,384,128]{2,1,0:T(8,128)S(1)} fusion(f32[384,128]{1,0:T(8,128)S(1)} %fusion.33, bf16[2,384,128]{1,2,0:T(8,128)(2,1)S(1)} %fusion.15), kind=kOutput, calls=%fused_computation.23 | convolution fusion | flops 39272448 | bytes 491520 | tf_op jit(solution)/shard_map/dot_general | solution.py:54
  99.8 2.4 %fusion.17 = f32[1,384,128]{2,1,0:T(8,128)S(1)} fusion(f32[384,128]{1,0:T(8,128)S(1)} %fusion.34, bf16[2,384,128]{1,2,0:T(8,128)(2,1)S(1)} %fusion.15), kind=kOutput, calls=%fused_computation.25 | convolution fusion | flops 39272448 | bytes 491520 | tf_op jit(solution)/shard_map/dot_general | solution.py:51
  102.2 0.8 maximum_multiply_fusion
  (5 shorter events, 0.1 us)
Async XLA Ops:
  6.5 85.8 %copy-start = (bf16[384,384]{1,0:T(8,128)(2,1)S(1)}, bf16[384,384]{1,0:T(8,128)(2,1)}, u32[]{:S(2)}) copy-start(bf16[384,384]{1,0:T(8,128)(2,1)} %param.11) | copy-start | bytes 884740
  6.5 12.7 %copy-start.3 = (s32[4,256]{1,0:T(4,128)S(1)}, s32[4,256]{1,0:T(4,128)}, u32[]{:S(2)}) copy-start(s32[4,256]{1,0:T(4,128)} %param.10) | copy-start | bytes 12292
  6.5 62.8 %all-gather.2.cloned.1.call-start = ((), (), s32[]{:S(2)}) async-start(), calls=%async_computation.2 | async-start | bytes 4456448 | tf_op jit(solution)/shard_map/all_gather | solution.py:66
  11.9 35.3 %all-to-all-start = ((bf16[2,256,384]{1,0,2:T(2,128)(2,1)}), bf16[2,256,384]{1,0,2:T(2,128)(2,1)S(1)}, u32[]{:S(2)}, u32[]{:S(2)}) async-start(bf16[2,256,384]{1,0,2:T(2,128)(2,1)} %copy.34), calls=%async_computation | async-start | bytes 786432 | tf_op jit(solution)/shard_map/all_to_all | solution.py:64
  72.7 0.9 copy-start.1
  73.6 1.0 copy-start.2
  74.2 1.0 slice-start
  74.2 1.0 slice-start.1
  74.6 0.8 slice-start.2
  74.6 1.0 slice-start.3
Sparse Core Ops, SparseCore 0:
  10.0 59.2 all-gather.1
where the time goes:
time: 110 us
  blocking collectives  39.8 us (36%)
  matrix products  15.3 us (14%)
  waiting for transfers between devices  14.9 us (14%)
  local copies, waits for them, and re-layouts  14.7 us (13%)
  between operations  13.7 us (12%)
  starting transfers between devices  7.39 us (7%)
  other arithmetic  4.11 us (4%)
    all_gather x1, blocking collectives, on_device(): lax.all_gather(blocks, 'chan', axis=1, tiled=True)  27.8 us
    all_gather x1, waiting for transfers between devices, on_device(): lax.all_gather(weighted, 'chan', axis=1, tiled=True)  14.9 us
    all_to_all x1, blocking collectives, on_device(): lax.all_to_all(gridded_samples.astype(jnp.bfloat16), 'chan', split_axis=2...  12 us
    all_to_all x1, starting transfers between devices, on_device(): lax.all_to_all(visibilities, 'chan', split_axis=2, concat_axis=1, tiled=T...  7.39 us
    unnamed x11, local copies, waits for them, and re-layouts  4.8 us
    transpose x1, local copies, waits for them, and re-layouts, on_device(): vis_owned.transpose(0, 2, 1).reshape(2 * channels, vis_owned.shape[1])  2.8 us
    slice x1, local copies, waits for them, and re-layouts, grid_samples(): grouped_visibilities = weighted[offset].reshape(cell_groups, nblocks, cells)  2.44 us
    dot_general x1, matrix products, delay_transform(): jnp.dot(sin_table, filtered[1], preferred_element_type=jnp.float32)  2.4 us
  transfers between devices with their start and end apart: 2, of which 1 were waited for; matrix products, arithmetic and copies ran while one was open for 9% of the time, Pallas kernels for 0%

commit v1 on v0

v1 whole, which is shorter than its diff:
```python
import math

import jax
import jax.numpy as jnp
import numpy as np
from jax import lax
from jax.experimental import pallas as pl
from jax.experimental.pallas import tpu as pltpu
from jax.sharding import PartitionSpec as P

MAXB = 4
LABEL_ROWS = 16
CHUNK = 128
VMEM_BYTES = 48 * 1024 * 1024


def delay_tables(channels):
    index = np.arange(channels, dtype=np.int64)
    product = index[:, None] * index[None, :] % channels
    angle = product.astype(np.float32) * np.float32(2.0 * math.pi / channels)
    return jnp.asarray(np.cos(angle).astype(jnp.bfloat16)), jnp.asarray(
        np.sin(angle).astype(jnp.bfloat16)
    )


def prep_body(nblocks, nchunks, vis, kernel, weights, counts, blocks, own, core, far, *chunks):
    cells = kernel.shape[2]
    me = lax.axis_index("chan")
    start = blocks[0:1, :]
    weight = weights[...].reshape(1, -1).astype(jnp.float32)
    count = counts[...].reshape(1, -1)
    turned = [kernel[j].astype(jnp.float32).T for j in range(MAXB)]

    def pick(flip):
        residue = jnp.bitwise_xor(jnp.bitwise_and(me, MAXB - 1), flip)
        which = jnp.bitwise_and(residue - start, MAXB - 1)
        total = None
        for j in range(MAXB):
            gain = jnp.where((which == j) & (j < count), weight, 0.0)
            term = turned[j] * gain
            total = term if total is None else total + term
        label = lax.rem(start + which, nblocks) // MAXB
        return total.astype(jnp.bfloat16), jnp.broadcast_to(
            label.astype(jnp.float32), (LABEL_ROWS, start.shape[1])
        ).astype(jnp.bfloat16)

    own[:cells, :], own[cells:, :] = pick(0)
    core[:cells, :], core[cells:, :] = pick(1)
    far[:cells, :], far[2 * cells : 2 * cells + LABEL_ROWS, :] = pick(2)
    far[cells : 2 * cells, :], far[2 * cells + LABEL_ROWS :, :] = pick(3)
    for k in range(nchunks):
        for part in range(2):
            chunks[k][:, part * CHUNK : (part + 1) * CHUNK] = vis[
                part, :, k * CHUNK : (k + 1) * CHUNK
            ]


def grid_body(groups, k, own, core, far, relay, vis, vis_core, vis_far, vis_relay, send, keep, place, rows):
    samples = own.shape[1]
    cells = own.shape[0] - LABEL_ROWS
    me = lax.axis_index("chan")
    bit = jnp.bitwise_and(me // MAXB, 1).astype(jnp.float32)
    for part in range(2):
        lanes = slice(part * CHUNK, (part + 1) * CHUNK)
        rows[:samples, lanes] = vis[part, :, k * CHUNK : (k + 1) * CHUNK]
        rows[samples : 2 * samples, lanes] = vis_core[part, :, k * CHUNK : (k + 1) * CHUNK]
    rows[2 * samples : 3 * samples, :] = vis_far[...]
    rows[3 * samples :, :] = vis_relay[...]
    table = [
        (own[:cells, :], own[cells : cells + 1, :]),
        (core[:cells, :], core[cells : cells + 1, :]),
        (far[:cells, :], far[2 * cells : 2 * cells + 1, :]),
        (
            relay[cells : 2 * cells, :],
            relay[2 * cells + LABEL_ROWS : 2 * cells + LABEL_ROWS + 1, :],
        ),
    ]
    half = groups // 2
    for side in range(2):
        for p in range(half):
            wanted = 2.0 * p + (bit if side else 1.0 - bit)
            for source, (values, label) in enumerate(table):
                gain = jnp.where(label.astype(jnp.float32) == wanted, 1.0, 0.0).astype(jnp.bfloat16)
                place[
                    (side * half + p) * cells : (side * half + p + 1) * cells,
                    source * samples : (source + 1) * samples,
                ] = values * gain
        placed = jnp.dot(
            place[side * half * cells : (side + 1) * half * cells, :],
            rows[...],
            preferred_element_type=jnp.float32,
        ).reshape(half, cells, 2 * CHUNK)
        if side:
            keep[...] = placed
        else:
            send[...] = placed.astype(jnp.bfloat16)


def final_body(nchunks, *refs):
    kept, got = refs[:nchunks], refs[nchunks : 2 * nchunks]
    inv_cov, cos_table, sin_table, out = refs[2 * nchunks :]
    cells = out.shape[2]
    parts = []
    sums = [
        (kept[k][...] + got[k][...].astype(jnp.float32)).astype(jnp.bfloat16)
        for k in range(nchunks)
    ]
    for part in range(2):
        parts.append(
            jnp.concatenate(
                [s[:, part * CHUNK : (part + 1) * CHUNK] for s in sums], axis=1
            )
        )
    cube = jnp.concatenate(parts, axis=0)
    filtered = lax.dot_general(
        cube, inv_cov[...], (((1,), (1,)), ((), ())), preferred_element_type=jnp.float32
    ).astype(jnp.bfloat16)
    contract = (((1,), (1,)), ((), ()))
    cosine = lax.dot_general(cos_table[...], filtered, contract, preferred_element_type=jnp.float32)
    sine = lax.dot_general(sin_table[...], filtered, contract, preferred_element_type=jnp.float32)
    scale = 1.0 / math.sqrt(inv_cov.shape[0])
    out[0] = (cosine[:, :cells] + sine[:, cells:]) * scale
    out[1] = (cosine[:, cells:] - sine[:, :cells]) * scale


def on_device(visibilities, kernel, weights, counts, blocks, inv_cov):
    nblocks = lax.axis_size("chan")
    groups = nblocks // MAXB
    samples, channels = visibilities.shape[1:]
    cells = kernel.shape[2]
    nchunks = channels // CHUNK
    params = pltpu.CompilerParams(vmem_limit_bytes=VMEM_BYTES)
    bf16, f32 = jnp.bfloat16, jnp.float32
    shape = jax.ShapeDtypeStruct

    def swap(values, bit):
        return lax.ppermute(values, "chan", [(i, i ^ bit) for i in range(nblocks)])

    vis_core = swap(visibilities, 1)
    own, core, far, *chunks = pl.pallas_call(
        lambda *refs: prep_body(nblocks, nchunks, *refs),
        out_shape=[
            shape((cells + LABEL_ROWS, samples), bf16),
            shape((cells + LABEL_ROWS, samples), bf16),
            shape((2 * (cells + LABEL_ROWS), samples), bf16),
        ]
        + [shape((samples, 2 * CHUNK), bf16)] * nchunks,
        compiler_params=params,
        name="prep",
    )(visibilities, kernel, weights, counts, blocks)
    core = swap(core, 1)
    far = swap(far, 2)
    relay = swap(far, 1)
    me = lax.axis_index("chan")
    kept, got = [], []
    for k in range(nchunks):
        vis_far = swap(chunks[k], 2)
        vis_relay = swap(vis_far, 1)
        send, keep = pl.pallas_call(
            lambda *refs, k=k: grid_body(groups, k, *refs),
            out_shape=[
                shape((groups // 2, cells, 2 * CHUNK), bf16),
                shape((groups // 2, cells, 2 * CHUNK), f32),
            ],
            scratch_shapes=[
                pltpu.VMEM((groups * cells, MAXB * samples), bf16),
                pltpu.VMEM((MAXB * samples, 2 * CHUNK), bf16),
            ],
            compiler_params=params,
            name="grid",
        )(own, core, far, relay, visibilities, vis_core, vis_far, vis_relay)
        bit = MAXB
        while True:
            arrived = swap(send, bit)
            if keep.shape[0] == 1:
                break
            bit *= 2
            summed = (keep + arrived.astype(f32)).reshape(-1, 2, cells, 2 * CHUNK)
            upper = (me // bit) % 2 == 1
            keep = jnp.where(upper, summed[:, 1], summed[:, 0])
            send = jnp.where(upper, summed[:, 0], summed[:, 1]).astype(bf16)
        kept.append(keep[0])
        got.append(arrived[0])
    cos_table, sin_table = delay_tables(channels)
    return pl.pallas_call(
        lambda *refs: final_body(nchunks, *refs),
        out_shape=shape((2, channels, cells), f32),
        compiler_params=params,
        name="transform",
    )(*kept, *got, inv_cov, cos_table, sin_table)


def solution(mesh):
    placed = (
        P(None, ("obs", "chan"), None),
        P(None, ("obs", "chan"), None),
        P(("obs", "chan")),
        P(("obs", "chan")),
        P(None, ("obs", "chan")),
        P(),
    )
    return jax.shard_map(
        on_device,
        mesh=mesh,
        in_specs=placed,
        out_specs=P(None, None, ("obs", "chan")),
        check_vma=False,
    )
```

time: 110 us -> 43.1 us (0.39)
  blocking collectives: 39.8 us -> 0 us
  matrix products: 15.3 us -> 0 us
  between operations: 13.7 us -> 0.16 us
  local copies, waits for them, and re-layouts: 14.7 us -> 4.01 us
  starting transfers between devices: 7.39 us -> 16.1 us
  waiting for transfers between devices: 14.9 us -> 19.3 us
  other arithmetic: 4.11 us -> 0.17 us
  Pallas kernels: 0 us -> 3.08 us
    all_gather x1 -> x0, blocking collectives: 27.8 us -> none  [on_device(): lax.all_gather(blocks, 'chan', axis=1, tiled=True)]
    ppermute x0 -> x16, waiting for transfers between devices: none -> 19.3 us  [swap(): return lax.ppermute(values, 'chan', [(i, i ^ bit) for i in range(nblocks)])]
    ppermute x0 -> x16, starting transfers between devices: none -> 16.1 us  [swap(): return lax.ppermute(values, 'chan', [(i, i ^ bit) for i in range(nblocks)])]
    dot_general x14 -> x0, matrix products: 15.3 us -> none  [the longest x1 2.4 us: delay_transform(): jnp.dot(sin_table, filtered[1], preferred_element_type=jnp.float32)]
    all_gather x1 -> x0, waiting for transfers between devices: 14.9 us -> none  [on_device(): lax.all_gather(weighted, 'chan', axis=1, tiled=True)]
    all_to_all x1 -> x0, blocking collectives: 12 us -> none  [on_device(): lax.all_to_all(gridded_samples.astype(jnp.bfloat16), 'chan', split_axis=2...]
    all_to_all x1 -> x0, starting transfers between devices: 7.39 us -> none  [on_device(): lax.all_to_all(visibilities, 'chan', split_axis=2, concat_axis=1, tiled=T...]
    pallas_call x0 -> x5, Pallas kernels: none -> 3.08 us  [the longest x1 1.42 us: on_device(): pl.pallas_call(lambda *refs: final_body(nchunks, *refs), out_shape=shape(...]
  transfers between devices with their start and end apart: 2 -> 16, of which waited for: 1 -> 8; matrix products, arithmetic and copies ran while one was open for 9% -> 0% of each run, Pallas kernels for 0% -> 4%
where the time goes in v1:
time: 43.1 us; the launch traced here: 42.9 us
  waiting for transfers between devices  19.3 us (45%)
  starting transfers between devices  16.1 us (37%)
  local copies, waits for them, and re-layouts  4.01 us (9%)
  Pallas kernels  3.08 us (7%)
    ppermute x16, waiting for transfers between devices, swap(): return lax.ppermute(values, 'chan', [(i, i ^ bit) for i in range(nblocks)])  19.3 us
    ppermute x16, starting transfers between devices, swap(): return lax.ppermute(values, 'chan', [(i, i ^ bit) for i in range(nblocks)])  16.1 us
    unnamed x18, local copies, waits for them, and re-layouts  4.01 us
    pallas_call x1, Pallas kernels, on_device(): pl.pallas_call(lambda *refs: final_body(nchunks, *refs), out_shape=shape(...  1.42 us
    pallas_call x3, Pallas kernels, on_device(): pl.pallas_call(lambda *refs, k=k: grid_body(groups, k, *refs), out_shape=...  1.39 us
  transfers between devices with their start and end apart: 16, of which 8 were waited for; matrix products, arithmetic and copies ran while one was open for 0% of the time, Pallas kernels for 4%

profile of v1, /device:TPU:0, one launch (start us, length us, event | category | flops | bytes accessed | tf_op | source)
XLA Modules:
  0.0 42.9 jit_solution(11679923712603962748)
XLA Ops:
  0.0 0.5 %collective-permute-start.3 = (bf16[2,256,384]{2,1,0:T(8,128)(2,1)}, bf16[2,256,384]{2,1,0:T(8,128)(2,1)S(1)}, u32[]{:S(2)}, u32[]{:S(2)}) collective-permute-start(bf16[2,256,384]{2,1,0:T(8,128)(2,1)} %refs_4_.7), channel_id=1, source_target_pairs={{0,1},{1,0},{2,3},{3,2},{4,5},{5,4},{6,7},{7,6},{8,9},{9,8},{10,11... | collective-permute-start | bytes 1179656 | tf_op jit(solution)/shard_map/ppermute | solution.py:137
  0.5 0.0 copy-start
  0.5 1.0 %copy-done = bf16[2,256,384]{2,1,0:T(8,128)(2,1)S(1)} copy-done((bf16[2,256,384]{2,1,0:T(8,128)(2,1)S(1)}, bf16[2,256,384]{2,1,0:T(8,128)(2,1)}, u32[]{:S(2)}) %copy-start) | copy-done | bytes 393240
  1.4 0.0 copy-start.5
  1.5 0.9 %copy-done.5 = bf16[4,256,128]{2,1,0:T(8,128)(2,1)S(1)} copy-done((bf16[4,256,128]{2,1,0:T(8,128)(2,1)S(1)}, bf16[4,256,128]{2,1,0:T(8,128)(2,1)}, u32[]{:S(2)}) %copy-start.5) | copy-done | bytes 262168
  2.4 0.0 copy-start.6
  2.4 0.7 %copy-done.6 = s32[4,256]{1,0:T(4,128)S(1)} copy-done((s32[4,256]{1,0:T(4,128)S(1)}, s32[4,256]{1,0:T(4,128)}, u32[]{:S(2)}) %copy-start.6) | copy-done | bytes 4120
  3.1 0.0 copy-start.7
  3.1 0.7 %copy-done.7 = s32[256]{0:T(256)S(1)} copy-done((s32[256]{0:T(256)S(1)}, s32[256]{0:T(256)}, u32[]{:S(2)}) %copy-start.7) | copy-done | bytes 1048
  3.8 0.0 copy-start.8
  3.8 0.7 %copy-done.8 = s32[256]{0:T(256)S(1)} copy-done((s32[256]{0:T(256)S(1)}, s32[256]{0:T(256)}, u32[]{:S(2)}) %copy-start.8) | copy-done | bytes 1048
  4.4 0.3 prep.1
  4.7 2.6 %collective-permute-start.1 = (bf16[288,256]{1,0:T(8,128)(2,1)S(1)}, bf16[288,256]{1,0:T(8,128)(2,1)S(1)}, u32[]{:S(2)}, u32[]{:S(2)}) collective-permute-start(bf16[288,256]{1,0:T(8,128)(2,1)S(1)} %get-tuple-element.19), channel_id=1, source_target_pairs={{0,2},{1,3},{2,0},{3,1},{4,6},{5,7},{6,4},{7,5},{8,10},{9,11},{10,... | collective-permute-start | bytes 442376 | tf_op jit(solution)/shard_map/ppermute | solution.py:137
  7.3 0.1 collective-permute-start.10
  7.4 0.2 collective-permute-start
  7.6 4.4 %collective-permute-done.1.refs_2_ = bf16[288,256]{1,0:T(8,128)(2,1)S(1)} collective-permute-done((bf16[288,256]{1,0:T(8,128)(2,1)S(1)}, bf16[288,256]{1,0:T(8,128)(2,1)S(1)}, u32[]{:S(2)}, u32[]{:S(2)}) %collective-permute-start.1) | collective-permute-done | bytes 147488 | tf_op jit(solution)/shard_map/ppermute | solution.py:137
  12.0 0.0 collective-permute-start.2
  12.0 1.9 %collective-permute-start.7 = (bf16[256,256]{1,0:T(8,128)(2,1)S(1)}, bf16[256,256]{1,0:T(8,128)(2,1)S(1)}, u32[]{:S(2)}, u32[]{:S(2)}) collective-permute-start(bf16[256,256]{1,0:T(8,128)(2,1)S(1)} %get-tuple-element.23), channel_id=1, source_target_pairs={{0,2},{1,3},{2,0},{3,1},{4,6},{5,7},{6,4},{7,5},{8,10},{9,11},{10,... | collective-permute-start | bytes 393224 | tf_op jit(solution)/shard_map/ppermute | solution.py:137
  14.0 0.0 collective-permute-done.refs_1_
  14.0 0.1 collective-permute-start.4
  14.0 0.6 %collective-permute-done.10.refs_6_ = bf16[256,256]{1,0:T(8,128)(2,1)S(1)} collective-permute-done((bf16[256,256]{1,0:T(8,128)(2,1)S(1)}, bf16[256,256]{1,0:T(8,128)(2,1)S(1)}, u32[]{:S(2)}, u32[]{:S(2)}) %collective-permute-start.10) | collective-permute-done | bytes 131104 | tf_op jit(solution)/shard_map/ppermute | solution.py:137
  14.6 0.0 collective-permute-start.11
  14.6 3.7 %collective-permute-done.7.refs_6_ = bf16[256,256]{1,0:T(8,128)(2,1)S(1)} collective-permute-done((bf16[256,256]{1,0:T(8,128)(2,1)S(1)}, bf16[256,256]{1,0:T(8,128)(2,1)S(1)}, u32[]{:S(2)}, u32[]{:S(2)}) %collective-permute-start.7) | collective-permute-done | bytes 131104 | tf_op jit(solution)/shard_map/ppermute | solution.py:137
  18.4 0.0 collective-permute-start.8
  18.4 2.5 %collective-permute-done.4.refs_6_ = bf16[256,256]{1,0:T(8,128)(2,1)S(1)} collective-permute-done((bf16[256,256]{1,0:T(8,128)(2,1)S(1)}, bf16[256,256]{1,0:T(8,128)(2,1)S(1)}, u32[]{:S(2)}, u32[]{:S(2)}) %collective-permute-start.4) | collective-permute-done | bytes 131104 | tf_op jit(solution)/shard_map/ppermute | solution.py:137
  20.9 0.0 collective-permute-start.5
  20.9 0.0 collective-permute-done.11.refs_7_
  20.9 0.0 collective-permute-done.2.refs_3_
  20.9 0.0 collective-permute-done.3.refs_5_
  21.0 0.0 copy-start.1
  21.0 0.5 %grid.5 = (bf16[2,128,256]{2,1,0:T(8,128)(2,1)S(1)}, f32[2,128,256]{2,1,0:T(8,128)S(1)}) custom-call(bf16[144,256]{1,0:T(8,128)(2,1)S(1)} %get-tuple-element.17.refs_0_, bf16[144,256]{1,0:T(8,128)(2,1)S(1)} %collective-permute-done.refs_1_, bf16[288,256]{1,0:T(8,128)(2,1)S(1)} %collective-permute-done.1.refs_2_, ...), custom_call_target="tpu_custom_call" | custom-call | tf_op jit(solution)/shard_map/grid/pallas_call | solution.py:159
  21.4 1.9 %collective-permute-start.12 = (bf16[2,128,256]{2,1,0:T(8,128)(2,1)S(1)}, bf16[2,128,256]{2,1,0:T(8,128)(2,1)S(1)}, u32[]{:S(2)}, u32[]{:S(2)}) collective-permute-start(bf16[2,128,256]{2,1,0:T(8,128)(2,1)S(1)} %get-tuple-element.28), channel_id=1, source_target_pairs={{0,4},{1,5},{2,6},{3,7},{4,0},{5,1},{6,2},{7,3},{8,12},{9,13},{10,... | collective-permute-start | bytes 393224 | tf_op jit(solution)/shard_map/ppermute | solution.py:137
  23.3 0.0 collective-permute-done.8.refs_7_
  23.3 0.0 copy-done.1
  23.3 0.5 %grid.4 = (bf16[2,128,256]{2,1,0:T(8,128)(2,1)S(1)}, f32[2,128,256]{2,1,0:T(8,128)S(1)}) custom-call(bf16[144,256]{1,0:T(8,128)(2,1)S(1)} %get-tuple-element.17.refs_0_, bf16[144,256]{1,0:T(8,128)(2,1)S(1)} %collective-permute-done.refs_1_, bf16[288,256]{1,0:T(8,128)(2,1)S(1)} %collective-permute-done.1.refs_2_, ...), custom_call_target="tpu_custom_call" | custom-call | tf_op jit(solution)/shard_map/grid/pallas_call | solution.py:159
  23.8 0.5 %collective-permute-start.9 = (bf16[2,128,256]{2,1,0:T(8,128)(2,1)S(1)}, bf16[2,128,256]{2,1,0:T(8,128)(2,1)S(1)}, u32[]{:S(2)}, u32[]{:S(2)}) collective-permute-start(bf16[2,128,256]{2,1,0:T(8,128)(2,1)S(1)} %get-tuple-element.25), channel_id=1, source_target_pairs={{0,4},{1,5},{2,6},{3,7},{4,0},{5,1},{6,2},{7,3},{8,12},{9,13},{10,... | collective-permute-start | bytes 393224 | tf_op jit(solution)/shard_map/ppermute | solution.py:137
  24.3 0.0 collective-permute-done.5.refs_7_
  24.3 0.5 %grid.3 = (bf16[2,128,256]{2,1,0:T(8,128)(2,1)S(1)}, f32[2,128,256]{2,1,0:T(8,128)S(1)}) custom-call(bf16[144,256]{1,0:T(8,128)(2,1)S(1)} %get-tuple-element.17.refs_0_, bf16[144,256]{1,0:T(8,128)(2,1)S(1)} %collective-permute-done.refs_1_, bf16[288,256]{1,0:T(8,128)(2,1)S(1)} %collective-permute-done.1.refs_2_, ...), custom_call_target="tpu_custom_call" | custom-call | tf_op jit(solution)/shard_map/grid/pallas_call | solution.py:159
  24.8 1.7 %collective-permute-start.6 = (bf16[2,128,256]{2,1,0:T(8,128)(2,1)S(1)}, bf16[2,128,256]{2,1,0:T(8,128)(2,1)S(1)}, u32[]{:S(2)}, u32[]{:S(2)}) collective-permute-start(bf16[2,128,256]{2,1,0:T(8,128)(2,1)S(1)} %get-tuple-element.22), channel_id=1, source_target_pairs={{0,4},{1,5},{2,6},{3,7},{4,0},{5,1},{6,2},{7,3},{8,12},{9,13},{10,... | collective-permute-start | bytes 393224 | tf_op jit(solution)/shard_map/ppermute | solution.py:137
  26.4 1.4 %collective-permute-done.12 = bf16[2,128,256]{2,1,0:T(8,128)(2,1)S(1)} collective-permute-done((bf16[2,128,256]{2,1,0:T(8,128)(2,1)S(1)}, bf16[2,128,256]{2,1,0:T(8,128)(2,1)S(1)}, u32[]{:S(2)}, u32[]{:S(2)}) %collective-permute-start.12) | collective-permute-done | bytes 131104 | tf_op jit(solution)/shard_map/ppermute | solution.py:137
  27.8 2.9 %collective-permute-start.15 = (bf16[1,128,256]{2,1,0:T(8,128)(2,1)S(1)}, bf16[1,128,256]{2,1,0:T(8,128)(2,1)S(1)}, u32[]{:S(2)}, u32[]{:S(2)}) collective-permute-start(bf16[1,128,256]{2,1,0:T(8,128)(2,1)S(1)} %fusion.2), channel_id=1, source_target_pairs={{0,8},{1,9},{2,10},{3,11},{4,12},{5,13},{6,14},{7,15},{8,0},{9,1},... | collective-permute-start | bytes 196616 | tf_op jit(solution)/shard_map/ppermute | solution.py:137
  30.7 0.0 collective-permute-done.9
  30.8 2.7 %collective-permute-start.14 = (bf16[1,128,256]{2,1,0:T(8,128)(2,1)S(1)}, bf16[1,128,256]{2,1,0:T(8,128)(2,1)S(1)}, u32[]{:S(2)}, u32[]{:S(2)}) collective-permute-start(bf16[1,128,256]{2,1,0:T(8,128)(2,1)S(1)} %fusion.1), channel_id=1, source_target_pairs={{0,8},{1,9},{2,10},{3,11},{4,12},{5,13},{6,14},{7,15},{8,0},{9,1},... | collective-permute-start | bytes 196616 | tf_op jit(solution)/shard_map/ppermute | solution.py:137
  33.6 1.6 %collective-permute-done.6 = bf16[2,128,256]{2,1,0:T(8,128)(2,1)S(1)} collective-permute-done((bf16[2,128,256]{2,1,0:T(8,128)(2,1)S(1)}, bf16[2,128,256]{2,1,0:T(8,128)(2,1)S(1)}, u32[]{:S(2)}, u32[]{:S(2)}) %collective-permute-start.6) | collective-permute-done | bytes 131104 | tf_op jit(solution)/shard_map/ppermute | solution.py:137
  35.2 0.0 copy-start.4
  35.2 0.0 copy-start.2
  35.2 0.0 copy-start.3
  35.3 1.1 %collective-permute-start.13 = (bf16[1,128,256]{2,1,0:T(8,128)(2,1)S(1)}, bf16[1,128,256]{2,1,0:T(8,128)(2,1)S(1)}, u32[]{:S(2)}, u32[]{:S(2)}) collective-permute-start(bf16[1,128,256]{2,1,0:T(8,128)(2,1)S(1)} %fusion), channel_id=1, source_target_pairs={{0,8},{1,9},{2,10},{3,11},{4,12},{5,13},{6,14},{7,15},{8,0},{9,1},... | collective-permute-start | bytes 196616 | tf_op jit(solution)/shard_map/ppermute | solution.py:137
  36.4 0.0 collective-permute-done.15
  36.4 2.2 %collective-permute-done.14 = bf16[1,128,256]{2,1,0:T(8,128)(2,1)S(1)} collective-permute-done((bf16[1,128,256]{2,1,0:T(8,128)(2,1)S(1)}, bf16[1,128,256]{2,1,0:T(8,128)(2,1)S(1)}, u32[]{:S(2)}, u32[]{:S(2)}) %collective-permute-start.14) | collective-permute-done | bytes 65568 | tf_op jit(solution)/shard_map/ppermute | solution.py:137
  38.6 2.8 %collective-permute-done.13 = bf16[1,128,256]{2,1,0:T(8,128)(2,1)S(1)} collective-permute-done((bf16[1,128,256]{2,1,0:T(8,128)(2,1)S(1)}, bf16[1,128,256]{2,1,0:T(8,128)(2,1)S(1)}, u32[]{:S(2)}, u32[]{:S(2)}) %collective-permute-start.13) | collective-permute-done | bytes 65568 | tf_op jit(solution)/shard_map/ppermute | solution.py:137
  41.4 0.0 copy-done.4
  41.4 0.0 copy-done.2
  41.4 0.0 copy-done.3
  41.4 1.4 %transform.1 = f32[2,384,128]{2,1,0:T(8,128)} custom-call(f32[128,256]{1,0:T(8,128)S(1)} %select_bitcast_fusion.2.refs_0_, f32[128,256]{1,0:T(8,128)S(1)} %select_bitcast_fusion.1.refs_1_, f32[128,256]{1,0:T(8,128)S(1)} %select_bitcast_fusion.refs_2_, bf16[128,256]{1,0:T(8,128)(2,1)S(1)} %bitcast.23, bf16[128,256]{1,0:T(8,128)(2,1)S(1)} %bitcast.22, ...), custom_call_target="tpu_custom_call" | custom-call | tf_op jit(solution)/shard_map/transform/pallas_call | solution.py:185
  (9 shorter events, 0.2 us)
Async XLA Ops:
  0.0 20.9 %collective-permute-start.3 = (bf16[2,256,384]{2,1,0:T(8,128)(2,1)}, bf16[2,256,384]{2,1,0:T(8,128)(2,1)S(1)}, u32[]{:S(2)}, u32[]{:S(2)}) collective-permute-start(bf16[2,256,384]{2,1,0:T(8,128)(2,1)} %refs_4_.7), channel_id=1, source_target_pairs={{0,1},{1,0},{2,3},{3,2},{4,5},{5,4},{6,7},{7,6},{8,9},{9,8},{10,11... | collective-permute-start | bytes 1179656 | tf_op jit(solution)/shard_map/ppermute | solution.py:137
  0.5 1.0 %copy-start = (bf16[2,256,384]{2,1,0:T(8,128)(2,1)S(1)}, bf16[2,256,384]{2,1,0:T(8,128)(2,1)}, u32[]{:S(2)}) copy-start(bf16[2,256,384]{2,1,0:T(8,128)(2,1)} %refs_4_.7) | copy-start | bytes 1179652
  1.4 0.9 %copy-start.5 = (bf16[4,256,128]{2,1,0:T(8,128)(2,1)S(1)}, bf16[4,256,128]{2,1,0:T(8,128)(2,1)}, u32[]{:S(2)}) copy-start(bf16[4,256,128]{2,1,0:T(8,128)(2,1)} %refs_1_.1) | copy-start | bytes 786436
  2.4 0.7 %copy-start.6 = (s32[4,256]{1,0:T(4,128)S(1)}, s32[4,256]{1,0:T(4,128)}, u32[]{:S(2)}) copy-start(s32[4,256]{1,0:T(4,128)} %refs_4_.4) | copy-start | bytes 12292
  3.1 0.7 %copy-start.7 = (s32[256]{0:T(256)S(1)}, s32[256]{0:T(256)}, u32[]{:S(2)}) copy-start(s32[256]{0:T(256)} %refs_2_.1) | copy-start | bytes 3076
  3.8 0.7 %copy-start.8 = (s32[256]{0:T(256)S(1)}, s32[256]{0:T(256)}, u32[]{:S(2)}) copy-start(s32[256]{0:T(256)} %refs_3_.1) | copy-start | bytes 3076
  4.7 7.3 %collective-permute-start.1 = (bf16[288,256]{1,0:T(8,128)(2,1)S(1)}, bf16[288,256]{1,0:T(8,128)(2,1)S(1)}, u32[]{:S(2)}, u32[]{:S(2)}) collective-permute-start(bf16[288,256]{1,0:T(8,128)(2,1)S(1)} %get-tuple-element.19), channel_id=1, source_target_pairs={{0,2},{1,3},{2,0},{3,1},{4,6},{5,7},{6,4},{7,5},{8,10},{9,11},{10,... | collective-permute-start | bytes 442376 | tf_op jit(solution)/shard_map/ppermute | solution.py:137
  7.3 7.3 %collective-permute-start.10 = (bf16[256,256]{1,0:T(8,128)(2,1)S(1)}, bf16[256,256]{1,0:T(8,128)(2,1)S(1)}, u32[]{:S(2)}, u32[]{:S(2)}) collective-permute-start(bf16[256,256]{1,0:T(8,128)(2,1)S(1)} %get-tuple-element.26), channel_id=1, source_target_pairs={{0,2},{1,3},{2,0},{3,1},{4,6},{5,7},{6,4},{7,5},{8,10},{9,11},{10,... | collective-permute-start | bytes 393224 | tf_op jit(solution)/shard_map/ppermute | solution.py:137
  7.4 6.6 %collective-permute-start = (bf16[144,256]{1,0:T(8,128)(2,1)S(1)}, bf16[144,256]{1,0:T(8,128)(2,1)S(1)}, u32[]{:S(2)}, u32[]{:S(2)}) collective-permute-start(bf16[144,256]{1,0:T(8,128)(2,1)S(1)} %get-tuple-element.18), channel_id=1, source_target_pairs={{0,1},{1,0},{2,3},{3,2},{4,5},{5,4},{6,7},{7,6},{8,9},{9,8},{10,11... | collective-permute-start | bytes 221192 | tf_op jit(solution)/shard_map/ppermute | solution.py:137
  12.0 8.9 %collective-permute-start.2 = (bf16[288,256]{1,0:T(8,128)(2,1)S(1)}, bf16[288,256]{1,0:T(8,128)(2,1)S(1)}, u32[]{:S(2)}, u32[]{:S(2)}) collective-permute-start(bf16[288,256]{1,0:T(8,128)(2,1)S(1)} %collective-permute-done.1.refs_2_), channel_id=1, source_target_pairs={{0,1},{1,0},{2,3},{3,2},{4,5},{5,4},{6,7},{7,6},{8,9},{9,8},{10,11... | collective-permute-start | bytes 442376 | tf_op jit(solution)/shard_map/ppermute | solution.py:137
  12.0 6.4 %collective-permute-start.7 = (bf16[256,256]{1,0:T(8,128)(2,1)S(1)}, bf16[256,256]{1,0:T(8,128)(2,1)S(1)}, u32[]{:S(2)}, u32[]{:S(2)}) collective-permute-start(bf16[256,256]{1,0:T(8,128)(2,1)S(1)} %get-tuple-element.23), channel_id=1, source_target_pairs={{0,2},{1,3},{2,0},{3,1},{4,6},{5,7},{6,4},{7,5},{8,10},{9,11},{10,... | collective-permute-start | bytes 393224 | tf_op jit(solution)/shard_map/ppermute | solution.py:137
  14.0 7.0 %collective-permute-start.4 = (bf16[256,256]{1,0:T(8,128)(2,1)S(1)}, bf16[256,256]{1,0:T(8,128)(2,1)S(1)}, u32[]{:S(2)}, u32[]{:S(2)}) collective-permute-start(bf16[256,256]{1,0:T(8,128)(2,1)S(1)} %get-tuple-element.20), channel_id=1, source_target_pairs={{0,2},{1,3},{2,0},{3,1},{4,6},{5,7},{6,4},{7,5},{8,10},{9,11},{10,... | collective-permute-start | bytes 393224 | tf_op jit(solution)/shard_map/ppermute | solution.py:137
  14.6 6.3 %collective-permute-start.11 = (bf16[256,256]{1,0:T(8,128)(2,1)S(1)}, bf16[256,256]{1,0:T(8,128)(2,1)S(1)}, u32[]{:S(2)}, u32[]{:S(2)}) collective-permute-start(bf16[256,256]{1,0:T(8,128)(2,1)S(1)} %collective-permute-done.10.refs_6_), channel_id=1, source_target_pairs={{0,1},{1,0},{2,3},{3,2},{4,5},{5,4},{6,7},{7,6},{8,9},{9,8},{10,11... | collective-permute-start | bytes 393224 | tf_op jit(solution)/shard_map/ppermute | solution.py:137
  18.4 4.9 %collective-permute-start.8 = (bf16[256,256]{1,0:T(8,128)(2,1)S(1)}, bf16[256,256]{1,0:T(8,128)(2,1)S(1)}, u32[]{:S(2)}, u32[]{:S(2)}) collective-permute-start(bf16[256,256]{1,0:T(8,128)(2,1)S(1)} %collective-permute-done.7.refs_6_), channel_id=1, source_target_pairs={{0,1},{1,0},{2,3},{3,2},{4,5},{5,4},{6,7},{7,6},{8,9},{9,8},{10,11... | collective-permute-start | bytes 393224 | tf_op jit(solution)/shard_map/ppermute | solution.py:137
  20.9 3.4 %collective-permute-start.5 = (bf16[256,256]{1,0:T(8,128)(2,1)S(1)}, bf16[256,256]{1,0:T(8,128)(2,1)S(1)}, u32[]{:S(2)}, u32[]{:S(2)}) collective-permute-start(bf16[256,256]{1,0:T(8,128)(2,1)S(1)} %collective-permute-done.4.refs_6_), channel_id=1, source_target_pairs={{0,1},{1,0},{2,3},{3,2},{4,5},{5,4},{6,7},{7,6},{8,9},{9,8},{10,11... | collective-permute-start | bytes 393224 | tf_op jit(solution)/shard_map/ppermute | solution.py:137
  21.0 2.4 %copy-start.1 = (bf16[2,256,384]{2,1,0:T(8,128)(2,1)S(1)}, bf16[2,256,384]{2,1,0:T(8,128)(2,1)}, u32[]{:S(2)}) copy-start(bf16[2,256,384]{2,1,0:T(8,128)(2,1)} %refs_4_.7) | copy-start | bytes 1179652
  21.4 6.3 %collective-permute-start.12 = (bf16[2,128,256]{2,1,0:T(8,128)(2,1)S(1)}, bf16[2,128,256]{2,1,0:T(8,128)(2,1)S(1)}, u32[]{:S(2)}, u32[]{:S(2)}) collective-permute-start(bf16[2,128,256]{2,1,0:T(8,128)(2,1)S(1)} %get-tuple-element.28), channel_id=1, source_target_pairs={{0,4},{1,5},{2,6},{3,7},{4,0},{5,1},{6,2},{7,3},{8,12},{9,13},{10,... | collective-permute-start | bytes 393224 | tf_op jit(solution)/shard_map/ppermute | solution.py:137
  23.8 7.0 %collective-permute-start.9 = (bf16[2,128,256]{2,1,0:T(8,128)(2,1)S(1)}, bf16[2,128,256]{2,1,0:T(8,128)(2,1)S(1)}, u32[]{:S(2)}, u32[]{:S(2)}) collective-permute-start(bf16[2,128,256]{2,1,0:T(8,128)(2,1)S(1)} %get-tuple-element.25), channel_id=1, source_target_pairs={{0,4},{1,5},{2,6},{3,7},{4,0},{5,1},{6,2},{7,3},{8,12},{9,13},{10,... | collective-permute-start | bytes 393224 | tf_op jit(solution)/shard_map/ppermute | solution.py:137
  24.8 10.4 %collective-permute-start.6 = (bf16[2,128,256]{2,1,0:T(8,128)(2,1)S(1)}, bf16[2,128,256]{2,1,0:T(8,128)(2,1)S(1)}, u32[]{:S(2)}, u32[]{:S(2)}) collective-permute-start(bf16[2,128,256]{2,1,0:T(8,128)(2,1)S(1)} %get-tuple-element.22), channel_id=1, source_target_pairs={{0,4},{1,5},{2,6},{3,7},{4,0},{5,1},{6,2},{7,3},{8,12},{9,13},{10,... | collective-permute-start | bytes 393224 | tf_op jit(solution)/shard_map/ppermute | solution.py:137
  27.8 8.6 %collective-permute-start.15 = (bf16[1,128,256]{2,1,0:T(8,128)(2,1)S(1)}, bf16[1,128,256]{2,1,0:T(8,128)(2,1)S(1)}, u32[]{:S(2)}, u32[]{:S(2)}) collective-permute-start(bf16[1,128,256]{2,1,0:T(8,128)(2,1)S(1)} %fusion.2), channel_id=1, source_target_pairs={{0,8},{1,9},{2,10},{3,11},{4,12},{5,13},{6,14},{7,15},{8,0},{9,1},... | collective-permute-start | bytes 196616 | tf_op jit(solution)/shard_map/ppermute | solution.py:137
  30.8 7.8 %collective-permute-start.14 = (bf16[1,128,256]{2,1,0:T(8,128)(2,1)S(1)}, bf16[1,128,256]{2,1,0:T(8,128)(2,1)S(1)}, u32[]{:S(2)}, u32[]{:S(2)}) collective-permute-start(bf16[1,128,256]{2,1,0:T(8,128)(2,1)S(1)} %fusion.1), channel_id=1, source_target_pairs={{0,8},{1,9},{2,10},{3,11},{4,12},{5,13},{6,14},{7,15},{8,0},{9,1},... | collective-permute-start | bytes 196616 | tf_op jit(solution)/shard_map/ppermute | solution.py:137
  35.2 6.2 %copy-start.4 = (bf16[384,384]{1,0:T(8,128)(2,1)S(1)}, bf16[384,384]{1,0:T(8,128)(2,1)}, u32[]{:S(2)}) copy-start(bf16[384,384]{1,0:T(8,128)(2,1)} %constant.45.clone.refs_8_) | copy-start | bytes 884740
  35.2 6.2 %copy-start.2 = (bf16[384,384]{1,0:T(8,128)(2,1)S(1)}, bf16[384,384]{1,0:T(8,128)(2,1)}, u32[]{:S(2)}) copy-start(bf16[384,384]{1,0:T(8,128)(2,1)} %refs_6_.1) | copy-start | bytes 884740
  35.2 6.2 %copy-start.3 = (bf16[384,384]{1,0:T(8,128)(2,1)S(1)}, bf16[384,384]{1,0:T(8,128)(2,1)}, u32[]{:S(2)}) copy-start(bf16[384,384]{1,0:T(8,128)(2,1)} %constant.44.clone.refs_7_) | copy-start | bytes 884740
  35.3 6.2 %collective-permute-start.13 = (bf16[1,128,256]{2,1,0:T(8,128)(2,1)S(1)}, bf16[1,128,256]{2,1,0:T(8,128)(2,1)S(1)}, u32[]{:S(2)}, u32[]{:S(2)}) collective-permute-start(bf16[1,128,256]{2,1,0:T(8,128)(2,1)S(1)} %fusion), channel_id=1, source_target_pairs={{0,8},{1,9},{2,10},{3,11},{4,12},{5,13},{6,14},{7,15},{8,0},{9,1},... | collective-permute-start | bytes 196616 | tf_op jit(solution)/shard_map/ppermute | solution.py:137

commit v2 on v1

v2 whole, which is shorter than its diff:
```python
import math

import jax
import jax.numpy as jnp
import numpy as np
from jax import lax
from jax.experimental import pallas as pl
from jax.experimental.pallas import tpu as pltpu
from jax.sharding import PartitionSpec as P

MAXB = 4
LABEL_ROWS = 16
CHUNK = 128
FIRST = ()
LATER = ((0, 1), (2, 3), (4, 5))
VMEM_BYTES = 48 * 1024 * 1024


def delay_tables(channels):
    index = np.arange(channels, dtype=np.int64)
    product = index[:, None] * index[None, :] % channels
    angle = product.astype(np.float32) * np.float32(2.0 * math.pi / channels)
    return jnp.asarray(np.cos(angle).astype(jnp.bfloat16)), jnp.asarray(
        np.sin(angle).astype(jnp.bfloat16)
    )


def unit(vis, u):
    return vis.at[u % 2, :, pl.ds(u // 2 * CHUNK, CHUNK)]


def prep_body(
    nblocks, plan, vis, kernel_in, weights_in, counts_in, blocks_in, own, core, far, *refs
):
    chunks, (kernel, weights, counts, blocks, sems, cut_sems) = refs[: len(plan)], refs[len(plan) :]
    copies = [
        pltpu.make_async_copy(source, target, sems.at[i])
        for i, (source, target) in enumerate(
            [(weights_in, weights), (counts_in, counts), (blocks_in, blocks), (kernel_in, kernel)]
        )
    ]
    cuts = [
        pltpu.make_async_copy(unit(vis, u), chunk.at[:, pl.ds(i * CHUNK, CHUNK)], cut_sems.at[u])
        for units, chunk in zip(plan, chunks)
        for i, u in enumerate(units)
    ]
    for copy in copies + cuts:
        copy.start()
    for copy in copies:
        copy.wait()
    cells = kernel.shape[2]
    me = lax.axis_index("chan")
    start = blocks[0:1, :]
    weight = weights[...].reshape(1, -1).astype(jnp.float32)
    count = counts[...].reshape(1, -1)
    turned = [kernel[j].astype(jnp.float32).T for j in range(MAXB)]
    picked = []
    for flip in range(MAXB):
        residue = jnp.bitwise_xor(jnp.bitwise_and(me, MAXB - 1), flip)
        which = jnp.bitwise_and(residue - start, MAXB - 1)
        total = None
        for j in range(MAXB):
            gain = jnp.where((which == j) & (j < count), weight, 0.0)
            term = turned[j] * gain
            total = term if total is None else total + term
        label = lax.rem(start + which, nblocks) // MAXB
        picked.append(
            (
                total.astype(jnp.bfloat16),
                jnp.broadcast_to(
                    label.astype(jnp.float32), (LABEL_ROWS, start.shape[1])
                ).astype(jnp.bfloat16),
            )
        )
    for out, flips in ((own, (0, 2)), (core, (1, 3)), (far, (2, 3))):
        for i, flip in enumerate(flips):
            out[i * cells : (i + 1) * cells, :] = picked[flip][0]
            out[2 * cells + i * LABEL_ROWS : 2 * cells + (i + 1) * LABEL_ROWS, :] = picked[flip][1]
    for copy in cuts:
        copy.wait()


def listed(table, i, cells):
    row = 2 * cells + i * LABEL_ROWS
    return table[i * cells : (i + 1) * cells, :], table[row : row + 1, :].astype(jnp.float32)


def place_and_sum(classes, groups, place, rows, send, keep):
    cells = send.shape[2]
    samples = classes[0][0][0].shape[1]
    half = groups // 2
    me = lax.axis_index("chan")
    bit = jnp.bitwise_and(me // MAXB, 1).astype(jnp.float32)
    for side, out in enumerate((send, keep)):
        for c, table in enumerate(classes):
            first = (side * len(classes) + c) * half * cells
            for p in range(half):
                wanted = 2.0 * p + (bit if side else 1.0 - bit)
                for source, (values, label) in enumerate(table):
                    gain = jnp.where(label == wanted, 1.0, 0.0).astype(jnp.bfloat16)
                    place[
                        first + p * cells : first + (p + 1) * cells,
                        source * samples : (source + 1) * samples,
                    ] = values * gain
        first = side * len(classes) * half * cells
        out[...] = (
            jnp.dot(
                place[first : first + len(classes) * half * cells, :],
                rows[...],
                preferred_element_type=jnp.float32,
            )
            .reshape(out.shape)
            .astype(out.dtype)
        )


def near_body(groups, units, own, core, vis, vis_core, send, keep, place, rows):
    samples = own.shape[1]
    cells = send.shape[2]
    rows[:samples, :] = vis[...]
    for i, u in enumerate(units):
        rows[samples:, i * CHUNK : (i + 1) * CHUNK] = unit(vis_core, u)[...]
    place_and_sum(
        [[listed(own, i, cells), listed(core, i, cells)] for i in range(2)],
        groups,
        place,
        rows,
        send,
        keep,
    )


def plane_body(
    groups, units, own, core, far, relay, vis, vis_core, vis_far, *rest
):
    *vis_relay, send, keep, place, rows = rest
    samples = own.shape[1]
    cells = send.shape[2]
    rows[:samples, :] = vis[...]
    for i, u in enumerate(units):
        rows[samples : 2 * samples, i * CHUNK : (i + 1) * CHUNK] = unit(vis_core, u)[...]
    rows[2 * samples : 3 * samples, :] = vis_far[...]
    each = samples // len(vis_relay)
    for i, piece in enumerate(vis_relay):
        rows[3 * samples + i * each : 3 * samples + (i + 1) * each, :] = piece[...]
    place_and_sum(
        [
            [
                listed(own, 0, cells),
                listed(core, 0, cells),
                listed(far, 0, cells),
                listed(relay, 1, cells),
            ]
        ],
        groups,
        place,
        rows,
        send,
        keep,
    )


def final_body(plan, *refs):
    nchunks = len(plan)
    kept, got = refs[:nchunks], refs[nchunks : 2 * nchunks]
    inv_cov, cos_table, sin_table, out = refs[2 * nchunks :]
    cells = out.shape[2]
    sums = {}
    for units, mine, other in zip(plan, kept, got):
        summed = (mine[...] + other[...].astype(jnp.float32)).astype(jnp.bfloat16)
        for i, u in enumerate(units):
            sums[u] = summed[:, i * CHUNK : (i + 1) * CHUNK]
    cube = jnp.concatenate(
        [
            jnp.concatenate([sums[u] for u in range(part, len(sums), 2)], axis=1)
            for part in range(2)
        ],
        axis=0,
    )
    contract = (((1,), (1,)), ((), ()))
    filtered = lax.dot_general(
        cube, inv_cov[...], contract, preferred_element_type=jnp.float32
    ).astype(jnp.bfloat16)
    cosine = lax.dot_general(cos_table[...], filtered, contract, preferred_element_type=jnp.float32)
    sine = lax.dot_general(sin_table[...], filtered, contract, preferred_element_type=jnp.float32)
    scale = 1.0 / math.sqrt(inv_cov.shape[0])
    out[0] = (cosine[:, :cells] + sine[:, cells:]) * scale
    out[1] = (cosine[:, cells:] - sine[:, :cells]) * scale


def on_device(visibilities, kernel, weights, counts, blocks, inv_cov):
    nblocks = lax.axis_size("chan")
    groups = nblocks // MAXB
    samples, channels = visibilities.shape[1:]
    cells = kernel.shape[2]
    plan = FIRST + LATER
    bf16, f32 = jnp.bfloat16, jnp.float32
    shape = jax.ShapeDtypeStruct
    hbm, anywhere = pl.BlockSpec(memory_space=pltpu.HBM), pl.BlockSpec(memory_space=pl.ANY)
    options = dict(
        compiler_params=pltpu.CompilerParams(vmem_limit_bytes=VMEM_BYTES),
        cost_estimate=pl.CostEstimate(flops=1, bytes_accessed=1, transcendentals=0),
    )

    def swap(values, bit):
        return lax.ppermute(values, "chan", [(i, i ^ bit) for i in range(nblocks)])

    listing = shape((2 * (cells + LABEL_ROWS), samples), bf16)
    operands = (visibilities, kernel, weights, counts, blocks)
    own, core, far, *chunks = pl.pallas_call(
        lambda *refs: prep_body(nblocks, plan, *refs),
        in_specs=[hbm] * 5,
        out_specs=[pl.BlockSpec(memory_space=pltpu.VMEM)] * 3 + [anywhere] * len(plan),
        out_shape=[listing] * 3
        + [shape((samples, len(units) * CHUNK), bf16) for units in plan],
        scratch_shapes=[
            pltpu.VMEM(kernel.shape, bf16),
            pltpu.VMEM(weights.shape, jnp.int32),
            pltpu.VMEM(counts.shape, jnp.int32),
            pltpu.VMEM(blocks.shape, jnp.int32),
            pltpu.SemaphoreType.DMA((4,)),
            pltpu.SemaphoreType.DMA((2 * channels // CHUNK,)),
        ],
        name="prep",
        **options,
    )(*[pltpu.with_memory_space_constraint(x, pltpu.HBM) for x in operands])
    me = lax.axis_index("chan")
    vis_core = swap(visibilities, 1)
    core = swap(core, 1)
    far = swap(far, 2)
    relay = swap(far, 1)

    def grid(body, classes, sources, units, *operands):
        out = (classes, groups // 2, cells, len(units) * CHUNK)
        return pl.pallas_call(
            lambda *refs: body(groups, units, *refs),
            out_shape=[shape(out, bf16), shape(out, f32)],
            scratch_shapes=[
                pltpu.VMEM((classes * groups * cells, sources * samples), bf16),
                pltpu.VMEM((sources * samples, len(units) * CHUNK), bf16),
            ],
            name="grid",
            **options,
        )(*operands)

    def over_planes(send, keep):
        bit = MAXB
        while True:
            arrived = swap(send, bit)
            if keep.shape[1] == 1:
                return keep, arrived
            bit *= 2
            summed = keep + arrived.astype(f32)
            summed = summed.reshape(summed.shape[0], -1, 2, *summed.shape[2:])
            upper = (me // bit) % 2 == 1
            keep = jnp.where(upper, summed[:, :, 1], summed[:, :, 0])
            send = jnp.where(upper, summed[:, :, 0], summed[:, :, 1]).astype(bf16)

    kept, got, sent = [], [], []
    for units, chunk in zip(FIRST, chunks):
        send, keep = grid(near_body, 2, 2, units, own, core, chunk, vis_core)
        keep, arrived = over_planes(send, keep)
        summed = keep[:, 0] + arrived[:, 0].astype(f32)
        kept.append(summed[0])
        got.append(swap(summed[1].astype(bf16), 2))
    for units, chunk in zip(LATER, chunks[len(FIRST) :]):
        vis_far = swap(chunk, 2)
        if sent:
            vis_far, _ = lax.optimization_barrier((vis_far, sent[-1]))
        rows_each = samples // 2
        vis_relay = [swap(vis_far[i * rows_each : (i + 1) * rows_each], 1) for i in range(2)]
        send, keep = grid(
            plane_body, 1, 4, units, own, core, far, relay, chunk, vis_core, vis_far, *vis_relay
        )
        sent.append(send)
        keep, arrived = over_planes(send, keep)
        kept.append(keep[0, 0])
        got.append(arrived[0, 0])
    cos_table, sin_table = delay_tables(channels)
    return pl.pallas_call(
        lambda *refs: final_body(plan, *refs),
        out_shape=shape((2, channels, cells), f32),
        name="transform",
        **options,
    )(*kept, *got, inv_cov, cos_table, sin_table)


def solution(mesh):
    placed = (
        P(None, ("obs", "chan"), None),
        P(None, ("obs", "chan"), None),
        P(("obs", "chan")),
        P(("obs", "chan")),
        P(None, ("obs", "chan")),
        P(),
    )
    return jax.shard_map(
        on_device,
        mesh=mesh,
        in_specs=placed,
        out_specs=P(None, None, ("obs", "chan")),
        check_vma=False,
    )
```

time: 43.1 us -> 38 us (0.88)
  waiting for transfers between devices: 19.3 us -> 12.4 us
  starting transfers between devices: 16.1 us -> 20.8 us
  local copies, waits for them, and re-layouts: 4.01 us -> 0.05 us
  Pallas kernels: 3.08 us -> 4.28 us
    ppermute x16 -> x19, waiting for transfers between devices: 19.3 us -> 12.4 us  [swap(): return lax.ppermute(values, 'chan', [(i, i ^ bit) for i in range(nblocks)])]
    ppermute x16 -> x19, starting transfers between devices: 16.1 us -> 20.8 us  [swap(): return lax.ppermute(values, 'chan', [(i, i ^ bit) for i in range(nblocks)])]
    unnamed x18 -> x8, local copies, waits for them, and re-layouts: 4.01 us -> 0.02 us
    pallas_call x5, Pallas kernels: 3.08 us -> 4.28 us  [the longest x1 1.53 us: on_device(): pl.pallas_call(lambda *refs: prep_body(nblocks, plan, *refs), in_specs=[h...]
  transfers between devices with their start and end apart: 16 -> 19, of which waited for: 8 -> 8; matrix products, arithmetic and copies ran while one was open for 0% -> 1% of each run, Pallas kernels for 4% -> 3%
where the time goes in v2:
time: 38 us; the launch traced here: 37.9 us
  starting transfers between devices  20.8 us (55%)
  waiting for transfers between devices  12.4 us (33%)
  Pallas kernels  4.28 us (11%)
    ppermute x19, starting transfers between devices, swap(): return lax.ppermute(values, 'chan', [(i, i ^ bit) for i in range(nblocks)])  20.8 us
    ppermute x19, waiting for transfers between devices, swap(): return lax.ppermute(values, 'chan', [(i, i ^ bit) for i in range(nblocks)])  12.4 us
    pallas_call x1, Pallas kernels, on_device(): pl.pallas_call(lambda *refs: prep_body(nblocks, plan, *refs), in_specs=[h...  1.53 us
    pallas_call x1, Pallas kernels, on_device(): pl.pallas_call(lambda *refs: final_body(plan, *refs), out_shape=shape((2,...  1.42 us
    pallas_call x3, Pallas kernels, grid(): pl.pallas_call(lambda *refs: body(groups, units, *refs), out_shape=[shape...  1.32 us
  transfers between devices with their start and end apart: 19, of which 8 were waited for; matrix products, arithmetic and copies ran while one was open for 1% of the time, Pallas kernels for 3%

profile of v2, /device:TPU:0, one launch (start us, length us, event | category | flops | bytes accessed | tf_op | source)
XLA Modules:
  0.0 37.9 jit_solution(16072866205663719247)
XLA Ops:
  0.0 0.0 copy-start.3
  0.0 1.5 %prep.1 = (bf16[288,256]{1,0:T(8,128)(2,1)S(1)}, bf16[288,256]{1,0:T(8,128)(2,1)S(1)}, bf16[288,256]{1,0:T(8,128)(2,1)S(1)}, bf16[256,256]{1,0:T(8,128)(2,1)S(1)...) custom-call(bf16[2,256,384]{2,1,0:T(8,128)(2,1)} %refs_0_.1, bf16[4,256,128]{2,1,0:T(8,128)(2,1)} %refs_1_.1, ...), custom_call_target="tpu_custom_call" | custom-call | flops 1 | bytes 1 | tf_op jit(solution)/shard_map/prep/pallas_call | solution.py:210
  1.5 3.0 %collective-permute-start.1 = (bf16[288,256]{1,0:T(8,128)(2,1)S(1)}, bf16[288,256]{1,0:T(8,128)(2,1)S(1)}, u32[]{:S(2)}, u32[]{:S(2)}) collective-permute-start(bf16[288,256]{1,0:T(8,128)(2,1)S(1)} %get-tuple-element.21), channel_id=1, source_target_pairs={{0,2},{1,3},{2,0},{3,1},{4,6},{5,7},{6,4},{7,5},{8,10},{9,11},{10,... | collective-permute-start | bytes 442376 | tf_op jit(solution)/shard_map/ppermute | solution.py:206
  4.6 0.1 collective-permute-start.4
  4.7 0.0 copy-done.3
  4.7 0.0 collective-permute-start.3
  4.7 0.5 %collective-permute-start = (bf16[288,256]{1,0:T(8,128)(2,1)S(1)}, bf16[288,256]{1,0:T(8,128)(2,1)S(1)}, u32[]{:S(2)}, u32[]{:S(2)}) collective-permute-start(bf16[288,256]{1,0:T(8,128)(2,1)S(1)} %get-tuple-element.20), channel_id=1, source_target_pairs={{0,1},{1,0},{2,3},{3,2},{4,5},{5,4},{6,7},{7,6},{8,9},{9,8},{10,11... | collective-permute-start | bytes 442376 | tf_op jit(solution)/shard_map/ppermute | solution.py:206
  5.2 1.9 %collective-permute-start.8 = (bf16[256,256]{1,0:T(8,128)(2,1)S(1)}, bf16[256,256]{1,0:T(8,128)(2,1)S(1)}, u32[]{:S(2)}, u32[]{:S(2)}) collective-permute-start(bf16[256,256]{1,0:T(8,128)(2,1)S(1)} %get-tuple-element.25.refs_4_), channel_id=1, source_target_pairs={{0,2},{1,3},{2,0},{3,1},{4,6},{5,7},{6,4},{7,5},{8,10},{9,11},{10,... | collective-permute-start | bytes 393224 | tf_op jit(solution)/shard_map/ppermute | solution.py:206
  7.1 2.1 %collective-permute-done.1.refs_2_ = bf16[288,256]{1,0:T(8,128)(2,1)S(1)} collective-permute-done((bf16[288,256]{1,0:T(8,128)(2,1)S(1)}, bf16[288,256]{1,0:T(8,128)(2,1)S(1)}, u32[]{:S(2)}, u32[]{:S(2)}) %collective-permute-start.1) | collective-permute-done | bytes 147488 | tf_op jit(solution)/shard_map/ppermute | solution.py:206
  9.3 0.0 collective-permute-start.2
  9.3 2.8 %collective-permute-done.4.refs_6_ = bf16[256,256]{1,0:T(8,128)(2,1)S(1)} collective-permute-done((bf16[256,256]{1,0:T(8,128)(2,1)S(1)}, bf16[256,256]{1,0:T(8,128)(2,1)S(1)}, u32[]{:S(2)}, u32[]{:S(2)}) %collective-permute-start.4) | collective-permute-done | bytes 131104 | tf_op jit(solution)/shard_map/ppermute | solution.py:206
  12.1 0.1 collective-permute-start.5
  12.2 0.0 collective-permute-done.refs_1_
  12.2 0.5 %collective-permute-start.6 = (bf16[128,256]{1,0:T(8,128)(2,1)S(1)}, bf16[128,256]{1,0:T(8,128)(2,1)S(1)}, u32[]{:S(2)}, u32[]{:S(2)}) collective-permute-start(bf16[128,256]{1,0:T(8,128)(2,1)S(1)} %get-tuple-element.37), channel_id=1, source_target_pairs={{0,1},{1,0},{2,3},{3,2},{4,5},{5,4},{6,7},{7,6},{8,9},{9,8},{10,11... | collective-permute-start | bytes 196616 | tf_op jit(solution)/shard_map/ppermute | solution.py:206
  12.7 0.7 %collective-permute-done.5.refs_7_ = bf16[128,256]{1,0:T(8,128)(2,1)S(1)} collective-permute-done((bf16[128,256]{1,0:T(8,128)(2,1)S(1)}, bf16[128,256]{1,0:T(8,128)(2,1)S(1)}, u32[]{:S(2)}, u32[]{:S(2)}) %collective-permute-start.5) | collective-permute-done | bytes 65568 | tf_op jit(solution)/shard_map/ppermute | solution.py:206
  13.4 2.1 %collective-permute-start.12 = (bf16[256,256]{1,0:T(8,128)(2,1)S(1)}, bf16[256,256]{1,0:T(8,128)(2,1)S(1)}, u32[]{:S(2)}, u32[]{:S(2)}) collective-permute-start(bf16[256,256]{1,0:T(8,128)(2,1)S(1)} %get-tuple-element.29.refs_4_), channel_id=1, source_target_pairs={{0,2},{1,3},{2,0},{3,1},{4,6},{5,7},{6,4},{7,5},{8,10},{9,11},{10,... | collective-permute-start | bytes 393224 | tf_op jit(solution)/shard_map/ppermute | solution.py:206
  15.5 0.0 collective-permute-done.6.refs_8_
  15.5 0.0 collective-permute-done.2.refs_3_
  15.5 0.0 collective-permute-done.3.refs_5_
  15.5 0.4 %grid.3 = (bf16[1,2,128,256]{3,2,1,0:T(8,128)(2,1)S(1)}, f32[1,2,128,256]{3,2,1,0:T(8,128)S(1)}) custom-call(bf16[288,256]{1,0:T(8,128)(2,1)S(1)} %get-tuple-element.19.refs_0_, bf16[288,256]{1,0:T(8,128)(2,1)S(1)} %collective-permute-done.refs_1_, bf16[288,256]{1,0:T(8,128)(2,1)S(1)} %collective-permute-done.1.refs_2_, ...), custom_call_target="tpu_custom_call" | custom-call | flops 1 | bytes 1 | tf_op jit(solution)/shard_map/grid/pallas_call | solution.py:235
  15.9 0.0 collective-permute-done.8.refs_6_
  15.9 0.1 collective-permute-start.10
  16.0 0.5 %collective-permute-start.9 = (bf16[128,256]{1,0:T(8,128)(2,1)S(1)}, bf16[128,256]{1,0:T(8,128)(2,1)S(1)}, u32[]{:S(2)}, u32[]{:S(2)}) collective-permute-start(bf16[128,256]{1,0:T(8,128)(2,1)S(1)} %get-tuple-element.36), channel_id=1, source_target_pairs={{0,1},{1,0},{2,3},{3,2},{4,5},{5,4},{6,7},{7,6},{8,9},{9,8},{10,11... | collective-permute-start | bytes 196616 | tf_op jit(solution)/shard_map/ppermute | solution.py:206
  16.5 1.6 %collective-permute-start.7 = (bf16[1,2,128,256]{3,2,1,0:T(8,128)(2,1)S(1)}, bf16[1,2,128,256]{3,2,1,0:T(8,128)(2,1)S(1)}, u32[]{:S(2)}, u32[]{:S(2)}) collective-permute-start(bf16[1,2,128,256]{3,2,1,0:T(8,128)(2,1)S(1)} %get-tuple-element.24), channel_id=1, source_target_pairs={{0,4},{1,5},{2,6},{3,7},{4,0},{5,1},{6,2},{7,3},{8,12},{9,13},{10,... | collective-permute-start | bytes 393224 | tf_op jit(solution)/shard_map/ppermute | solution.py:206
  18.1 0.0 collective-permute-done.10.refs_8_
  18.1 0.0 collective-permute-done.9.refs_7_
  18.1 0.4 %grid.4 = (bf16[1,2,128,256]{3,2,1,0:T(8,128)(2,1)S(1)}, f32[1,2,128,256]{3,2,1,0:T(8,128)S(1)}) custom-call(bf16[288,256]{1,0:T(8,128)(2,1)S(1)} %get-tuple-element.19.refs_0_, bf16[288,256]{1,0:T(8,128)(2,1)S(1)} %collective-permute-done.refs_1_, bf16[288,256]{1,0:T(8,128)(2,1)S(1)} %collective-permute-done.1.refs_2_, ...), custom_call_target="tpu_custom_call" | custom-call | flops 1 | bytes 1 | tf_op jit(solution)/shard_map/grid/pallas_call | solution.py:235
  18.6 0.7 %collective-permute-done.12.refs_6_ = bf16[256,256]{1,0:T(8,128)(2,1)S(1)} collective-permute-done((bf16[256,256]{1,0:T(8,128)(2,1)S(1)}, bf16[256,256]{1,0:T(8,128)(2,1)S(1)}, u32[]{:S(2)}, u32[]{:S(2)}) %collective-permute-start.12) | collective-permute-done | bytes 131104 | tf_op jit(solution)/shard_map/ppermute | solution.py:206
  19.3 0.1 collective-permute-start.13
  19.4 0.5 %collective-permute-start.14 = (bf16[128,256]{1,0:T(8,128)(2,1)S(1)}, bf16[128,256]{1,0:T(8,128)(2,1)S(1)}, u32[]{:S(2)}, u32[]{:S(2)}) collective-permute-start(bf16[128,256]{1,0:T(8,128)(2,1)S(1)} %get-tuple-element.33), channel_id=1, source_target_pairs={{0,1},{1,0},{2,3},{3,2},{4,5},{5,4},{6,7},{7,6},{8,9},{9,8},{10,11... | collective-permute-start | bytes 196616 | tf_op jit(solution)/shard_map/ppermute | solution.py:206
  19.9 1.8 %collective-permute-start.11 = (bf16[1,2,128,256]{3,2,1,0:T(8,128)(2,1)S(1)}, bf16[1,2,128,256]{3,2,1,0:T(8,128)(2,1)S(1)}, u32[]{:S(2)}, u32[]{:S(2)}) collective-permute-start(bf16[1,2,128,256]{3,2,1,0:T(8,128)(2,1)S(1)} %get-tuple-element.28), channel_id=1, source_target_pairs={{0,4},{1,5},{2,6},{3,7},{4,0},{5,1},{6,2},{7,3},{8,12},{9,13},{10,... | collective-permute-start | bytes 393224 | tf_op jit(solution)/shard_map/ppermute | solution.py:206
  21.7 0.0 collective-permute-done.13.refs_7_
  21.7 0.0 collective-permute-done.14.refs_8_
  21.7 0.4 %grid.5 = (bf16[1,2,128,256]{3,2,1,0:T(8,128)(2,1)S(1)}, f32[1,2,128,256]{3,2,1,0:T(8,128)S(1)}) custom-call(bf16[288,256]{1,0:T(8,128)(2,1)S(1)} %get-tuple-element.19.refs_0_, bf16[288,256]{1,0:T(8,128)(2,1)S(1)} %collective-permute-done.refs_1_, bf16[288,256]{1,0:T(8,128)(2,1)S(1)} %collective-permute-done.1.refs_2_, ...), custom_call_target="tpu_custom_call" | custom-call | flops 1 | bytes 1 | tf_op jit(solution)/shard_map/grid/pallas_call | solution.py:235
  22.1 1.0 %collective-permute-start.15 = (bf16[1,2,128,256]{3,2,1,0:T(8,128)(2,1)S(1)}, bf16[1,2,128,256]{3,2,1,0:T(8,128)(2,1)S(1)}, u32[]{:S(2)}, u32[]{:S(2)}) collective-permute-start(bf16[1,2,128,256]{3,2,1,0:T(8,128)(2,1)S(1)} %get-tuple-element.32), channel_id=1, source_target_pairs={{0,4},{1,5},{2,6},{3,7},{4,0},{5,1},{6,2},{7,3},{8,12},{9,13},{10,... | collective-permute-start | bytes 393224 | tf_op jit(solution)/shard_map/ppermute | solution.py:206
  23.1 0.0 collective-permute-done.7
  23.1 2.7 %collective-permute-start.16 = (bf16[1,1,128,256]{3,2,1,0:T(8,128)(2,1)S(1)}, bf16[1,1,128,256]{3,2,1,0:T(8,128)(2,1)S(1)}, u32[]{:S(2)}, u32[]{:S(2)}) collective-permute-start(bf16[1,1,128,256]{3,2,1,0:T(8,128)(2,1)S(1)} %fusion), channel_id=1, source_target_pairs={{0,8},{1,9},{2,10},{3,11},{4,12},{5,13},{6,14},{7,15},{8,0},{9,1},... | collective-permute-start | bytes 196616 | tf_op jit(solution)/shard_map/ppermute | solution.py:206
  25.8 0.4 %collective-permute-done.11 = bf16[1,2,128,256]{3,2,1,0:T(8,128)(2,1)S(1)} collective-permute-done((bf16[1,2,128,256]{3,2,1,0:T(8,128)(2,1)S(1)}, bf16[1,2,128,256]{3,2,1,0:T(8,128)(2,1)S(1)}, u32[]{:S(2)}, u32[]{:S(2)}) %collective-permute-start.11) | collective-permute-done | bytes 131104 | tf_op jit(solution)/shard_map/ppermute | solution.py:206
  26.3 2.9 %collective-permute-start.17 = (bf16[1,1,128,256]{3,2,1,0:T(8,128)(2,1)S(1)}, bf16[1,1,128,256]{3,2,1,0:T(8,128)(2,1)S(1)}, u32[]{:S(2)}, u32[]{:S(2)}) collective-permute-start(bf16[1,1,128,256]{3,2,1,0:T(8,128)(2,1)S(1)} %fusion.1), channel_id=1, source_target_pairs={{0,8},{1,9},{2,10},{3,11},{4,12},{5,13},{6,14},{7,15},{8,0},{9,1},... | collective-permute-start | bytes 196616 | tf_op jit(solution)/shard_map/ppermute | solution.py:206
  29.2 1.1 %collective-permute-done.15 = bf16[1,2,128,256]{3,2,1,0:T(8,128)(2,1)S(1)} collective-permute-done((bf16[1,2,128,256]{3,2,1,0:T(8,128)(2,1)S(1)}, bf16[1,2,128,256]{3,2,1,0:T(8,128)(2,1)S(1)}, u32[]{:S(2)}, u32[]{:S(2)}) %collective-permute-start.15) | collective-permute-done | bytes 131104 | tf_op jit(solution)/shard_map/ppermute | solution.py:206
  30.3 0.0 copy-start.2
  30.3 0.0 copy-start
  30.3 0.0 copy-start.1
  30.4 1.6 %collective-permute-start.18 = (bf16[1,1,128,256]{3,2,1,0:T(8,128)(2,1)S(1)}, bf16[1,1,128,256]{3,2,1,0:T(8,128)(2,1)S(1)}, u32[]{:S(2)}, u32[]{:S(2)}) collective-permute-start(bf16[1,1,128,256]{3,2,1,0:T(8,128)(2,1)S(1)} %fusion.2), channel_id=1, source_target_pairs={{0,8},{1,9},{2,10},{3,11},{4,12},{5,13},{6,14},{7,15},{8,0},{9,1},... | collective-permute-start | bytes 196616 | tf_op jit(solution)/shard_map/ppermute | solution.py:206
  32.0 0.0 collective-permute-done.16
  32.0 2.0 %collective-permute-done.17 = bf16[1,1,128,256]{3,2,1,0:T(8,128)(2,1)S(1)} collective-permute-done((bf16[1,1,128,256]{3,2,1,0:T(8,128)(2,1)S(1)}, bf16[1,1,128,256]{3,2,1,0:T(8,128)(2,1)S(1)}, u32[]{:S(2)}, u32[]{:S(2)}) %collective-permute-start.17) | collective-permute-done | bytes 65568 | tf_op jit(solution)/shard_map/ppermute | solution.py:206
  34.0 2.4 %collective-permute-done.18 = bf16[1,1,128,256]{3,2,1,0:T(8,128)(2,1)S(1)} collective-permute-done((bf16[1,1,128,256]{3,2,1,0:T(8,128)(2,1)S(1)}, bf16[1,1,128,256]{3,2,1,0:T(8,128)(2,1)S(1)}, u32[]{:S(2)}, u32[]{:S(2)}) %collective-permute-start.18) | collective-permute-done | bytes 65568 | tf_op jit(solution)/shard_map/ppermute | solution.py:206
  36.5 0.0 copy-done.2
  36.5 0.0 copy-done
  36.5 0.0 copy-done.1
  36.5 1.4 %transform.1 = f32[2,384,128]{2,1,0:T(8,128)} custom-call(f32[128,256]{1,0:T(8,128)S(1)} %select_bitcast_fusion.2.refs_0_, f32[128,256]{1,0:T(8,128)S(1)} %select_bitcast_fusion.1.refs_1_, f32[128,256]{1,0:T(8,128)S(1)} %select_bitcast_fusion.refs_2_, bf16[128,256]{1,0:T(8,128)(2,1)S(1)} %bitcast.21, bf16[128,256]{1,0:T(8,128)(2,1)S(1)} %bitcast.22, ...), custom_call_target="tpu_custom_call" | custom-call | flops 1 | bytes 1 | tf_op jit(solution)/shard_map/transform/pallas_call | solution.py:280
  (12 shorter events, 0.2 us)
Async XLA Ops:
  0.0 4.7 %copy-start.3 = (bf16[2,256,384]{2,1,0:T(8,128)(2,1)S(1)}, bf16[2,256,384]{2,1,0:T(8,128)(2,1)}, u32[]{:S(2)}) copy-start(bf16[2,256,384]{2,1,0:T(8,128)(2,1)} %refs_0_.1) | copy-start | bytes 1179652
  1.5 7.7 %collective-permute-start.1 = (bf16[288,256]{1,0:T(8,128)(2,1)S(1)}, bf16[288,256]{1,0:T(8,128)(2,1)S(1)}, u32[]{:S(2)}, u32[]{:S(2)}) collective-permute-start(bf16[288,256]{1,0:T(8,128)(2,1)S(1)} %get-tuple-element.21), channel_id=1, source_target_pairs={{0,2},{1,3},{2,0},{3,1},{4,6},{5,7},{6,4},{7,5},{8,10},{9,11},{10,... | collective-permute-start | bytes 442376 | tf_op jit(solution)/shard_map/ppermute | solution.py:206
  4.6 7.5 %collective-permute-start.4 = (bf16[256,256]{1,0:T(8,128)(2,1)S(1)}, bf16[256,256]{1,0:T(8,128)(2,1)S(1)}, u32[]{:S(2)}, u32[]{:S(2)}) collective-permute-start(bf16[256,256]{1,0:T(8,128)(2,1)S(1)} %get-tuple-element.22.refs_4_), channel_id=1, source_target_pairs={{0,2},{1,3},{2,0},{3,1},{4,6},{5,7},{6,4},{7,5},{8,10},{9,11},{10,... | collective-permute-start | bytes 393224 | tf_op jit(solution)/shard_map/ppermute | solution.py:206
  4.7 10.8 %collective-permute-start.3 = (bf16[2,256,384]{2,1,0:T(8,128)(2,1)S(1)}, bf16[2,256,384]{2,1,0:T(8,128)(2,1)S(1)}, u32[]{:S(2)}, u32[]{:S(2)}) collective-permute-start(bf16[2,256,384]{2,1,0:T(8,128)(2,1)S(1)} %copy-done.3), channel_id=1, source_target_pairs={{0,1},{1,0},{2,3},{3,2},{4,5},{5,4},{6,7},{7,6},{8,9},{9,8},{10,11... | collective-permute-start | bytes 1179656 | tf_op jit(solution)/shard_map/ppermute | solution.py:206
  4.7 7.5 %collective-permute-start = (bf16[288,256]{1,0:T(8,128)(2,1)S(1)}, bf16[288,256]{1,0:T(8,128)(2,1)S(1)}, u32[]{:S(2)}, u32[]{:S(2)}) collective-permute-start(bf16[288,256]{1,0:T(8,128)(2,1)S(1)} %get-tuple-element.20), channel_id=1, source_target_pairs={{0,1},{1,0},{2,3},{3,2},{4,5},{5,4},{6,7},{7,6},{8,9},{9,8},{10,11... | collective-permute-start | bytes 442376 | tf_op jit(solution)/shard_map/ppermute | solution.py:206
  5.2 10.7 %collective-permute-start.8 = (bf16[256,256]{1,0:T(8,128)(2,1)S(1)}, bf16[256,256]{1,0:T(8,128)(2,1)S(1)}, u32[]{:S(2)}, u32[]{:S(2)}) collective-permute-start(bf16[256,256]{1,0:T(8,128)(2,1)S(1)} %get-tuple-element.25.refs_4_), channel_id=1, source_target_pairs={{0,2},{1,3},{2,0},{3,1},{4,6},{5,7},{6,4},{7,5},{8,10},{9,11},{10,... | collective-permute-start | bytes 393224 | tf_op jit(solution)/shard_map/ppermute | solution.py:206
  9.3 6.2 %collective-permute-start.2 = (bf16[288,256]{1,0:T(8,128)(2,1)S(1)}, bf16[288,256]{1,0:T(8,128)(2,1)S(1)}, u32[]{:S(2)}, u32[]{:S(2)}) collective-permute-start(bf16[288,256]{1,0:T(8,128)(2,1)S(1)} %collective-permute-done.1.refs_2_), channel_id=1, source_target_pairs={{0,1},{1,0},{2,3},{3,2},{4,5},{5,4},{6,7},{7,6},{8,9},{9,8},{10,11... | collective-permute-start | bytes 442376 | tf_op jit(solution)/shard_map/ppermute | solution.py:206
  12.1 1.3 %collective-permute-start.5 = (bf16[128,256]{1,0:T(8,128)(2,1)S(1)}, bf16[128,256]{1,0:T(8,128)(2,1)S(1)}, u32[]{:S(2)}, u32[]{:S(2)}) collective-permute-start(bf16[128,256]{1,0:T(8,128)(2,1)S(1)} %get-tuple-element.38), channel_id=1, source_target_pairs={{0,1},{1,0},{2,3},{3,2},{4,5},{5,4},{6,7},{7,6},{8,9},{9,8},{10,11... | collective-permute-start | bytes 196616 | tf_op jit(solution)/shard_map/ppermute | solution.py:206
  12.2 3.3 %collective-permute-start.6 = (bf16[128,256]{1,0:T(8,128)(2,1)S(1)}, bf16[128,256]{1,0:T(8,128)(2,1)S(1)}, u32[]{:S(2)}, u32[]{:S(2)}) collective-permute-start(bf16[128,256]{1,0:T(8,128)(2,1)S(1)} %get-tuple-element.37), channel_id=1, source_target_pairs={{0,1},{1,0},{2,3},{3,2},{4,5},{5,4},{6,7},{7,6},{8,9},{9,8},{10,11... | collective-permute-start | bytes 196616 | tf_op jit(solution)/shard_map/ppermute | solution.py:206
  13.4 5.9 %collective-permute-start.12 = (bf16[256,256]{1,0:T(8,128)(2,1)S(1)}, bf16[256,256]{1,0:T(8,128)(2,1)S(1)}, u32[]{:S(2)}, u32[]{:S(2)}) collective-permute-start(bf16[256,256]{1,0:T(8,128)(2,1)S(1)} %get-tuple-element.29.refs_4_), channel_id=1, source_target_pairs={{0,2},{1,3},{2,0},{3,1},{4,6},{5,7},{6,4},{7,5},{8,10},{9,11},{10,... | collective-permute-start | bytes 393224 | tf_op jit(solution)/shard_map/ppermute | solution.py:206
  15.9 2.2 %collective-permute-start.10 = (bf16[128,256]{1,0:T(8,128)(2,1)S(1)}, bf16[128,256]{1,0:T(8,128)(2,1)S(1)}, u32[]{:S(2)}, u32[]{:S(2)}) collective-permute-start(bf16[128,256]{1,0:T(8,128)(2,1)S(1)} %get-tuple-element.35), channel_id=1, source_target_pairs={{0,1},{1,0},{2,3},{3,2},{4,5},{5,4},{6,7},{7,6},{8,9},{9,8},{10,11... | collective-permute-start | bytes 196616 | tf_op jit(solution)/shard_map/ppermute | solution.py:206
  16.0 2.1 %collective-permute-start.9 = (bf16[128,256]{1,0:T(8,128)(2,1)S(1)}, bf16[128,256]{1,0:T(8,128)(2,1)S(1)}, u32[]{:S(2)}, u32[]{:S(2)}) collective-permute-start(bf16[128,256]{1,0:T(8,128)(2,1)S(1)} %get-tuple-element.36), channel_id=1, source_target_pairs={{0,1},{1,0},{2,3},{3,2},{4,5},{5,4},{6,7},{7,6},{8,9},{9,8},{10,11... | collective-permute-start | bytes 196616 | tf_op jit(solution)/shard_map/ppermute | solution.py:206
  16.5 6.6 %collective-permute-start.7 = (bf16[1,2,128,256]{3,2,1,0:T(8,128)(2,1)S(1)}, bf16[1,2,128,256]{3,2,1,0:T(8,128)(2,1)S(1)}, u32[]{:S(2)}, u32[]{:S(2)}) collective-permute-start(bf16[1,2,128,256]{3,2,1,0:T(8,128)(2,1)S(1)} %get-tuple-element.24), channel_id=1, source_target_pairs={{0,4},{1,5},{2,6},{3,7},{4,0},{5,1},{6,2},{7,3},{8,12},{9,13},{10,... | collective-permute-start | bytes 393224 | tf_op jit(solution)/shard_map/ppermute | solution.py:206
  19.3 2.4 %collective-permute-start.13 = (bf16[128,256]{1,0:T(8,128)(2,1)S(1)}, bf16[128,256]{1,0:T(8,128)(2,1)S(1)}, u32[]{:S(2)}, u32[]{:S(2)}) collective-permute-start(bf16[128,256]{1,0:T(8,128)(2,1)S(1)} %get-tuple-element.34), channel_id=1, source_target_pairs={{0,1},{1,0},{2,3},{3,2},{4,5},{5,4},{6,7},{7,6},{8,9},{9,8},{10,11... | collective-permute-start | bytes 196616 | tf_op jit(solution)/shard_map/ppermute | solution.py:206
  19.4 2.3 %collective-permute-start.14 = (bf16[128,256]{1,0:T(8,128)(2,1)S(1)}, bf16[128,256]{1,0:T(8,128)(2,1)S(1)}, u32[]{:S(2)}, u32[]{:S(2)}) collective-permute-start(bf16[128,256]{1,0:T(8,128)(2,1)S(1)} %get-tuple-element.33), channel_id=1, source_target_pairs={{0,1},{1,0},{2,3},{3,2},{4,5},{5,4},{6,7},{7,6},{8,9},{9,8},{10,11... | collective-permute-start | bytes 196616 | tf_op jit(solution)/shard_map/ppermute | solution.py:206
  19.9 6.3 %collective-permute-start.11 = (bf16[1,2,128,256]{3,2,1,0:T(8,128)(2,1)S(1)}, bf16[1,2,128,256]{3,2,1,0:T(8,128)(2,1)S(1)}, u32[]{:S(2)}, u32[]{:S(2)}) collective-permute-start(bf16[1,2,128,256]{3,2,1,0:T(8,128)(2,1)S(1)} %get-tuple-element.28), channel_id=1, source_target_pairs={{0,4},{1,5},{2,6},{3,7},{4,0},{5,1},{6,2},{7,3},{8,12},{9,13},{10,... | collective-permute-start | bytes 393224 | tf_op jit(solution)/shard_map/ppermute | solution.py:206
  22.1 8.2 %collective-permute-start.15 = (bf16[1,2,128,256]{3,2,1,0:T(8,128)(2,1)S(1)}, bf16[1,2,128,256]{3,2,1,0:T(8,128)(2,1)S(1)}, u32[]{:S(2)}, u32[]{:S(2)}) collective-permute-start(bf16[1,2,128,256]{3,2,1,0:T(8,128)(2,1)S(1)} %get-tuple-element.32), channel_id=1, source_target_pairs={{0,4},{1,5},{2,6},{3,7},{4,0},{5,1},{6,2},{7,3},{8,12},{9,13},{10,... | collective-permute-start | bytes 393224 | tf_op jit(solution)/shard_map/ppermute | solution.py:206
  23.1 8.9 %collective-permute-start.16 = (bf16[1,1,128,256]{3,2,1,0:T(8,128)(2,1)S(1)}, bf16[1,1,128,256]{3,2,1,0:T(8,128)(2,1)S(1)}, u32[]{:S(2)}, u32[]{:S(2)}) collective-permute-start(bf16[1,1,128,256]{3,2,1,0:T(8,128)(2,1)S(1)} %fusion), channel_id=1, source_target_pairs={{0,8},{1,9},{2,10},{3,11},{4,12},{5,13},{6,14},{7,15},{8,0},{9,1},... | collective-permute-start | bytes 196616 | tf_op jit(solution)/shard_map/ppermute | solution.py:206
  26.3 7.8 %collective-permute-start.17 = (bf16[1,1,128,256]{3,2,1,0:T(8,128)(2,1)S(1)}, bf16[1,1,128,256]{3,2,1,0:T(8,128)(2,1)S(1)}, u32[]{:S(2)}, u32[]{:S(2)}) collective-permute-start(bf16[1,1,128,256]{3,2,1,0:T(8,128)(2,1)S(1)} %fusion.1), channel_id=1, source_target_pairs={{0,8},{1,9},{2,10},{3,11},{4,12},{5,13},{6,14},{7,15},{8,0},{9,1},... | collective-permute-start | bytes 196616 | tf_op jit(solution)/shard_map/ppermute | solution.py:206
  30.3 6.2 %copy-start.2 = (bf16[384,384]{1,0:T(8,128)(2,1)S(1)}, bf16[384,384]{1,0:T(8,128)(2,1)}, u32[]{:S(2)}) copy-start(bf16[384,384]{1,0:T(8,128)(2,1)} %constant.45.clone.refs_8_) | copy-start | bytes 884740
  30.3 6.2 %copy-start = (bf16[384,384]{1,0:T(8,128)(2,1)S(1)}, bf16[384,384]{1,0:T(8,128)(2,1)}, u32[]{:S(2)}) copy-start(bf16[384,384]{1,0:T(8,128)(2,1)} %refs_6_.1) | copy-start | bytes 884740
  30.3 6.1 %copy-start.1 = (bf16[384,384]{1,0:T(8,128)(2,1)S(1)}, bf16[384,384]{1,0:T(8,128)(2,1)}, u32[]{:S(2)}) copy-start(bf16[384,384]{1,0:T(8,128)(2,1)} %constant.44.clone.refs_7_) | copy-start | bytes 884740
  30.4 6.1 %collective-permute-start.18 = (bf16[1,1,128,256]{3,2,1,0:T(8,128)(2,1)S(1)}, bf16[1,1,128,256]{3,2,1,0:T(8,128)(2,1)S(1)}, u32[]{:S(2)}, u32[]{:S(2)}) collective-permute-start(bf16[1,1,128,256]{3,2,1,0:T(8,128)(2,1)S(1)} %fusion.2), channel_id=1, source_target_pairs={{0,8},{1,9},{2,10},{3,11},{4,12},{5,13},{6,14},{7,15},{8,0},{9,1},... | collective-permute-start | bytes 196616 | tf_op jit(solution)/shard_map/ppermute | solution.py:206

commit v3 on v2

v3 whole, which is shorter than its diff:
```python
import math

import jax
import jax.numpy as jnp
import numpy as np
from jax import lax
from jax.experimental import pallas as pl
from jax.experimental.pallas import tpu as pltpu
from jax.sharding import PartitionSpec as P

MAXB = 4
LABEL_ROWS = 16
CHUNK = 128
VMEM_BYTES = 48 * 1024 * 1024
PLAN = ((0,), (1, 2, 3), (4, 5))
NEAR = (0,)
DIRECT = (0,)
PIECES = 1
SECOND = (1, 0, 2)
LAST = (2,)
AFTER = {'relay': ['grid0'], 'relay1': ['grid0'], 'relay2': ['grid1'], 'third0': ['grid1', 'grid2', 'second1'], 'second2': ['second0']}


def delay_tables(channels):
    index = np.arange(channels, dtype=np.int64)
    product = index[:, None] * index[None, :] % channels
    angle = product.astype(np.float32) * np.float32(2.0 * math.pi / channels)
    table = np.concatenate([np.cos(angle), np.sin(angle)])
    return jnp.asarray(table.astype(jnp.bfloat16))


def unit(vis, u):
    return vis.at[u % 2, :, pl.ds(u // 2 * CHUNK, CHUNK)]


def prep_body(
    nblocks, vis, kernel_in, weights_in, counts_in, blocks_in, own, core, far, *refs
):
    chunks, (kernel, weights, counts, blocks, sems, cut_sems) = refs[: len(PLAN)], refs[len(PLAN) :]
    copies = [
        pltpu.make_async_copy(source, target, sems.at[i])
        for i, (source, target) in enumerate(
            [(weights_in, weights), (counts_in, counts), (blocks_in, blocks), (kernel_in, kernel)]
        )
    ]
    cuts = [
        pltpu.make_async_copy(unit(vis, u), chunk.at[:, pl.ds(i * CHUNK, CHUNK)], cut_sems.at[u])
        for units, chunk in zip(PLAN, chunks)
        for i, u in enumerate(units)
    ]
    for copy in copies + cuts:
        copy.start()
    for copy in copies:
        copy.wait()
    cells = kernel.shape[2]
    me = lax.axis_index("chan")
    start = blocks[0:1, :]
    weight = weights[...].reshape(1, -1).astype(jnp.float32)
    count = counts[...].reshape(1, -1)
    turned = [kernel[j].astype(jnp.float32).T for j in range(MAXB)]
    picked = []
    for flip in range(MAXB):
        residue = jnp.bitwise_xor(jnp.bitwise_and(me, MAXB - 1), flip)
        which = jnp.bitwise_and(residue - start, MAXB - 1)
        total = None
        for j in range(MAXB):
            gain = jnp.where((which == j) & (j < count), weight, 0.0)
            term = turned[j] * gain
            total = term if total is None else total + term
        label = lax.rem(start + which, nblocks) // MAXB
        picked.append(
            (
                total.astype(jnp.bfloat16),
                jnp.broadcast_to(
                    label.astype(jnp.float32), (LABEL_ROWS, start.shape[1])
                ).astype(jnp.bfloat16),
            )
        )
    for out, flips in ((own, (0, 2)), (core, (1, 3)), (far, (2, 3))):
        for i, flip in enumerate(flips):
            out[i * cells : (i + 1) * cells, :] = picked[flip][0]
            out[2 * cells + i * LABEL_ROWS : 2 * cells + (i + 1) * LABEL_ROWS, :] = picked[flip][1]
    for copy in cuts:
        copy.wait()


def listed(table, i, cells):
    row = 2 * cells + i * LABEL_ROWS
    return table[i * cells : (i + 1) * cells, :], table[row : row + 1, :].astype(jnp.float32)


def grid_body(groups, n, *refs):
    units, near, direct = PLAN[n], n in NEAR, n in DIRECT
    sources = 2 if near else 4
    count = groups if direct else 2
    refs, (place, rows) = refs[:-2], refs[-2:]
    refs, outs = refs[:-count], refs[-count:]
    cells = outs[0].shape[2]
    if near:
        own, core, vis, vis_core = refs
        classes = [[listed(own, i, cells), listed(core, i, cells)] for i in range(2)]
    else:
        own, core, far, relay, vis, vis_core, vis_far, *vis_relay = refs
        classes = [[listed(table, int(i == 3), cells) for i, table in enumerate((own, core, far, relay))]]
    samples = own.shape[1]
    rows[:samples, :] = vis[...]
    for i, u in enumerate(units):
        rows[samples : 2 * samples, i * CHUNK : (i + 1) * CHUNK] = unit(vis_core, u)[...]
    if not near:
        rows[2 * samples : 3 * samples, :] = vis_far[...]
        each = samples // len(vis_relay)
        for i, piece in enumerate(vis_relay):
            rows[3 * samples + i * each : 3 * samples + (i + 1) * each, :] = piece[...]
    plane = lax.axis_index("chan") // MAXB
    if direct:
        wanted = [[jnp.bitwise_xor(plane, away)] for away in range(groups)]
    else:
        bit = jnp.bitwise_and(plane, 1)
        wanted = [[2 * p + side for p in range(groups // 2)] for side in (bit, 1 - bit)]
    first = 0
    for out, blocks in zip(outs, wanted):
        top = first
        for table in classes:
            for block in blocks:
                for source, (values, label) in enumerate(table):
                    gain = jnp.where(label == block.astype(jnp.float32), 1.0, 0.0)
                    place[first : first + cells, source * samples : (source + 1) * samples] = (
                        values * gain.astype(jnp.bfloat16)
                    )
                first += cells
        summed = jnp.dot(place[top:first, :], rows[...], preferred_element_type=jnp.float32)
        out[...] = summed.reshape(out.shape).astype(out.dtype)


def fold_body(tables, inv_cov, folded):
    folded[...] = lax.dot_general(
        tables[...], inv_cov[...], (((1,), (0,)), ((), ())), preferred_element_type=jnp.float32
    ).astype(folded.dtype)


def delay_body(held, last, folded, *refs):
    refs, out = refs[:-1], refs[-1]
    channels, cells = out.shape[1:]
    total = [None, None]
    if last:
        refs, before = refs[:-1], refs[-1]
        total = [before[0], before[1]]
    for i, units in enumerate(held):
        mine, other = refs[2 * i], refs[2 * i + 1]
        summed = (mine[...] + other[...].astype(jnp.float32)).astype(jnp.bfloat16)
        for j, u in enumerate(units):
            part, k = u % 2, u // 2
            both = lax.dot_general(
                folded[:, k * CHUNK : (k + 1) * CHUNK],
                summed[:, j * CHUNK : (j + 1) * CHUNK],
                (((1,), (1,)), ((), ())),
                preferred_element_type=jnp.float32,
            )
            cosine, sine = both[:channels], both[channels:]
            sine = sine if part else -sine
            for half, term in ((part, cosine), (1 - part, sine)):
                total[half] = term if total[half] is None else total[half] + term
    scale = 1.0 / math.sqrt(channels) if last else 1.0
    out[0] = total[0] * scale
    out[1] = total[1] * scale


def on_device(visibilities, kernel, weights, counts, blocks, inv_cov):
    nblocks = lax.axis_size("chan")
    groups = nblocks // MAXB
    samples, channels = visibilities.shape[1:]
    cells = kernel.shape[2]
    bf16, f32 = jnp.bfloat16, jnp.float32
    shape = jax.ShapeDtypeStruct
    hbm, anywhere = pl.BlockSpec(memory_space=pltpu.HBM), pl.BlockSpec(memory_space=pl.ANY)
    options = dict(
        compiler_params=pltpu.CompilerParams(vmem_limit_bytes=VMEM_BYTES),
        cost_estimate=pl.CostEstimate(flops=1, bytes_accessed=1, transcendentals=0),
    )
    made = {}

    def swap(values, bit):
        return lax.ppermute(values, "chan", [(i, i ^ bit) for i in range(nblocks)])

    def tied(name, *values):
        earlier = [made[other] for other in AFTER.get(name, ())]
        return lax.optimization_barrier((*values, *earlier))[: len(values)]

    listing = shape((2 * (cells + LABEL_ROWS), samples), bf16)
    operands = (visibilities, kernel, weights, counts, blocks)
    own, core, far, *chunks = pl.pallas_call(
        lambda *refs: prep_body(nblocks, *refs),
        in_specs=[hbm] * 5,
        out_specs=[pl.BlockSpec(memory_space=pltpu.VMEM)] * 3 + [anywhere] * len(PLAN),
        out_shape=[listing] * 3
        + [shape((samples, len(units) * CHUNK), bf16) for units in PLAN],
        scratch_shapes=[
            pltpu.VMEM(kernel.shape, bf16),
            pltpu.VMEM(weights.shape, jnp.int32),
            pltpu.VMEM(counts.shape, jnp.int32),
            pltpu.VMEM(blocks.shape, jnp.int32),
            pltpu.SemaphoreType.DMA((4,)),
            pltpu.SemaphoreType.DMA((2 * channels // CHUNK,)),
        ],
        name="prep",
        **options,
    )(*[pltpu.with_memory_space_constraint(x, pltpu.HBM) for x in operands])
    me = lax.axis_index("chan")
    vis_core = swap(visibilities, 1)
    core = swap(core, 1)
    far = swap(far, 2)
    vis_far = {n: swap(chunks[n], 2) for n in range(len(PLAN)) if n not in NEAR}

    made.update({f"far{n}": values for n, values in vis_far.items()})

    def grid(n, *operands):
        sources = 2 if n in NEAR else 4
        classes, lanes = 4 // sources, len(PLAN[n]) * CHUNK
        if n in DIRECT:
            out = (classes, 1, cells, lanes)
            outs = [shape(out, f32)] + [shape(out, bf16)] * (groups - 1)
        else:
            out = (classes, groups // 2, cells, lanes)
            outs = [shape(out, f32), shape(out, bf16)]
        keep, *sends = pl.pallas_call(
            lambda *refs: grid_body(groups, n, *refs),
            out_shape=outs,
            scratch_shapes=[
                pltpu.VMEM((classes * groups * cells, sources * samples), bf16),
                pltpu.VMEM((sources * samples, lanes), bf16),
            ],
            name="grid",
            **options,
        )(*operands)
        made[f"grid{n}"] = sends[0]
        sends = tied(f"first{n}", *sends)
        arrived = [swap(send, (i + 1) * MAXB) for i, send in enumerate(sends)]
        made[f"got{n}"] = arrived[0]
        return keep, arrived

    state = {n: grid(n, own, core, chunks[n], vis_core) for n in NEAR}
    (far,) = tied("relay", far)
    relay = swap(far, 1)
    for n in range(len(PLAN)):
        if n in NEAR:
            continue
        (mine,) = tied(f"relay{n}", vis_far[n])
        made[f"mine{n}"] = mine
        each = samples // PIECES
        vis_relay = [swap(mine[i * each : (i + 1) * each], 1) for i in range(PIECES)]
        state[n] = grid(n, own, core, far, relay, chunks[n], vis_core, mine, *vis_relay)

    held = {}
    for n in SECOND:
        keep, arrived = state[n]
        arrived = tied(f"second{n}", *arrived)
        bit = MAXB
        while keep.shape[1] > 1:
            bit *= 2
            summed = keep + arrived[0].astype(f32)
            summed = summed.reshape(summed.shape[0], -1, 2, *summed.shape[2:])
            upper = (me // bit) % 2 == 1
            keep = jnp.where(upper, summed[:, :, 1], summed[:, :, 0])
            send = jnp.where(upper, summed[:, :, 0], summed[:, :, 1]).astype(bf16)
            made[f"second{n}"] = send
            arrived = [swap(send, bit)]
        keep, arrived = keep[:, 0], [piece[:, 0] for piece in arrived]
        if n in NEAR or len(arrived) > 1:
            keep = keep + sum(piece.astype(f32) for piece in arrived[: None if n in NEAR else -1])
            made[f"second{n}"] = keep
        if n in NEAR:
            (send,) = tied(f"third{n}", keep[1].astype(bf16))
            arrived = [swap(send, 2)]
        held[n] = (keep[0], arrived[-1] if n in NEAR else arrived[-1][0])

    tables, early = tied("fold", delay_tables(channels), inv_cov)
    folded = pl.pallas_call(
        fold_body,
        out_shape=shape((2 * channels, channels), bf16),
        name="fold",
        **options,
    )(tables, early)

    def delayed(chosen, last, *extra):
        return pl.pallas_call(
            lambda *refs: delay_body([PLAN[n] for n in chosen], last, *refs),
            out_shape=shape((2, channels, cells), f32),
            name="delay",
            **options,
        )(folded, *[x for n in chosen for x in held[n]], *extra)

    before = delayed([n for n in range(len(PLAN)) if n not in LAST], False)
    return delayed(list(LAST), True, before)


def solution(mesh):
    placed = (
        P(None, ("obs", "chan"), None),
        P(None, ("obs", "chan"), None),
        P(("obs", "chan")),
        P(("obs", "chan")),
        P(None, ("obs", "chan")),
        P(),
    )
    return jax.shard_map(
        on_device,
        mesh=mesh,
        in_specs=placed,
        out_specs=P(None, None, ("obs", "chan")),
        check_vma=False,
    )
```

time: 38 us -> 36.5 us (0.961)
  starting transfers between devices: 20.8 us -> 18.6 us
  Pallas kernels: 4.28 us -> 5.01 us
    ppermute x19 -> x16, starting transfers between devices: 20.8 us -> 18.6 us  [swap(): return lax.ppermute(values, 'chan', [(i, i ^ bit) for i in range(nblocks)])]
    pallas_call x5 -> x7, Pallas kernels: 4.28 us -> 5.01 us  [the longest x3 1.63 us: grid(): pl.pallas_call(lambda *refs: grid_body(groups, n, *refs), out_shape=outs,...]
    ppermute x19 -> x16, waiting for transfers between devices: 12.4 us -> 12.4 us  [swap(): return lax.ppermute(values, 'chan', [(i, i ^ bit) for i in range(nblocks)])]
  transfers between devices with their start and end apart: 19 -> 16, of which waited for: 8 -> 9; matrix products, arithmetic and copies ran while one was open for 1% -> 0% of each run, Pallas kernels for 3% -> 11%
where the time goes in v3:
time: 36.5 us; the launch traced here: 36.4 us
  starting transfers between devices  18.6 us (51%)
  waiting for transfers between devices  12.4 us (34%)
  Pallas kernels  5.01 us (14%)
    ppermute x16, starting transfers between devices, swap(): return lax.ppermute(values, 'chan', [(i, i ^ bit) for i in range(nblocks)])  18.6 us
    ppermute x16, waiting for transfers between devices, swap(): return lax.ppermute(values, 'chan', [(i, i ^ bit) for i in range(nblocks)])  12.4 us
    pallas_call x3, Pallas kernels, grid(): pl.pallas_call(lambda *refs: grid_body(groups, n, *refs), out_shape=outs,...  1.63 us
    pallas_call x1, Pallas kernels, on_device(): pl.pallas_call(lambda *refs: prep_body(nblocks, *refs), in_specs=[hbm] *...  1.5 us
    pallas_call x2, Pallas kernels, delayed(): pl.pallas_call(lambda *refs: delay_body([PLAN[n] for n in chosen], last,...  1.38 us
  transfers between devices with their start and end apart: 16, of which 9 were waited for; matrix products, arithmetic and copies ran while one was open for 0% of the time, Pallas kernels for 11%

profile of v3, /device:TPU:0, one launch (start us, length us, event | category | flops | bytes accessed | tf_op | source)
XLA Modules:
  0.0 36.4 jit_solution(5053727357378579186)
XLA Ops:
  0.0 0.0 copy-start
  0.0 0.5 %collective-permute-start.2 = (bf16[2,256,384]{2,1,0:T(8,128)(2,1)}, bf16[2,256,384]{2,1,0:T(8,128)(2,1)S(1)}, u32[]{:S(2)}, u32[]{:S(2)}) collective-permute-start(bf16[2,256,384]{2,1,0:T(8,128)(2,1)} %refs_0_.1), channel_id=1, source_target_pairs={{0,1},{1,0},{2,3},{3,2},{4,5},{5,4},{6,7},{7,6},{8,9},{9,8},{10,11... | collective-permute-start | bytes 1179656 | tf_op jit(solution)/shard_map/ppermute | solution.py:183
  0.5 1.5 %prep.1 = (bf16[288,256]{1,0:T(8,128)(2,1)S(1)}, bf16[288,256]{1,0:T(8,128)(2,1)S(1)}, bf16[288,256]{1,0:T(8,128)(2,1)S(1)}, bf16[256,128]{1,0:T(8,128)(2,1)S(1)...) custom-call(bf16[2,256,384]{2,1,0:T(8,128)(2,1)} %refs_0_.1, bf16[4,256,128]{2,1,0:T(8,128)(2,1)} %refs_1_.1, ...), custom_call_target="tpu_custom_call" | custom-call | flops 1 | bytes 1 | tf_op jit(solution)/shard_map/prep/pallas_call | solution.py:191
  2.0 0.2 collective-permute-start
  2.1 2.9 %collective-permute-start.5 = (bf16[256,384]{1,0:T(8,128)(2,1)S(1)}, bf16[256,384]{1,0:T(8,128)(2,1)S(1)}, u32[]{:S(2)}, u32[]{:S(2)}) collective-permute-start(bf16[256,384]{1,0:T(8,128)(2,1)S(1)} %get-tuple-element.40.refs_4_), channel_id=1, source_target_pairs={{0,2},{1,3},{2,0},{3,1},{4,6},{5,7},{6,4},{7,5},{8,10},{9,11},{10,... | collective-permute-start | bytes 589832 | tf_op jit(solution)/shard_map/ppermute | solution.py:183
  5.1 0.0 collective-permute-start.1
  5.1 0.0 collective-permute-done.refs_1_
  5.1 0.0 collective-permute-done.2.refs_3_.refs_5_
  5.1 0.0 copy-start.1
  5.1 0.4 %grid.3 = (f32[2,1,128,128]{3,2,1,0:T(8,128)S(1)}, bf16[2,1,128,128]{3,2,1,0:T(8,128)(2,1)S(1)}, bf16[2,1,128,128]{3,2,1,0:T(8,128)(2,1)S(1)}, bf16[2,1,128,128]{3,2,1,0:T(8,128)(2,1)S(1)}) custom-call(bf16[288,256]{1,0:T(8,128)(2,1)S(1)} %get-tuple-element.33.refs_0_, bf16[288,256]{1,0:T(8,128)(2,1)S(1)} %collective-permute-done.refs_1_, ...), custom_call_target="tpu_custom_call" | custom-call | flops 1 | bytes 1 | tf_op jit(solution)/shard_map/grid/pallas_call | solution.py:225
  5.6 2.1 %collective-permute-start.10 = (bf16[2,1,128,128]{3,2,1,0:T(8,128)(2,1)S(1)}, bf16[2,1,128,128]{3,2,1,0:T(8,128)(2,1)S(1)}, u32[]{:S(2)}, u32[]{:S(2)}) collective-permute-start(bf16[2,1,128,128]{3,2,1,0:T(8,128)(2,1)S(1)} %get-tuple-element.49), channel_id=1, source_target_pairs={{0,4},{1,5},{2,6},{3,7},{4,0},{5,1},{6,2},{7,3},{8,12},{9,13},{10,... | collective-permute-start | bytes 196616 | tf_op jit(solution)/shard_map/ppermute | solution.py:183
  7.7 2.6 %collective-permute-start.11 = (bf16[2,1,128,128]{3,2,1,0:T(8,128)(2,1)S(1)}, bf16[2,1,128,128]{3,2,1,0:T(8,128)(2,1)S(1)}, u32[]{:S(2)}, u32[]{:S(2)}) collective-permute-start(bf16[2,1,128,128]{3,2,1,0:T(8,128)(2,1)S(1)} %get-tuple-element.50), channel_id=1, source_target_pairs={{0,8},{1,9},{2,10},{3,11},{4,12},{5,13},{6,14},{7,15},{8,0},{9,1},... | collective-permute-start | bytes 196616 | tf_op jit(solution)/shard_map/ppermute | solution.py:183
  10.2 0.0 collective-permute-start.12
  10.3 0.0 copy-done
  10.3 0.0 copy-done.1
  10.3 0.5 %fold.1.refs_0_ = bf16[768,384]{1,0:T(8,128)(2,1)S(1)} custom-call(bf16[768,384]{1,0:T(8,128)(2,1)S(1)} %copy-done, bf16[384,384]{1,0:T(8,128)(2,1)S(1)} %copy-done.1), custom_call_target="tpu_custom_call" | custom-call | flops 1 | bytes 1 | tf_op jit(solution)/shard_map/fold/pallas_call | solution.py:277
  10.8 2.5 %collective-permute-done.1.refs_2_ = bf16[288,256]{1,0:T(8,128)(2,1)S(1)} collective-permute-done((bf16[288,256]{1,0:T(8,128)(2,1)S(1)}, bf16[288,256]{1,0:T(8,128)(2,1)S(1)}, u32[]{:S(2)}, u32[]{:S(2)}) %collective-permute-start.1) | collective-permute-done | bytes 147488 | tf_op jit(solution)/shard_map/ppermute | solution.py:183
  13.4 1.7 %collective-permute-start.4 = (bf16[256,256]{1,0:T(8,128)(2,1)S(1)}, bf16[256,256]{1,0:T(8,128)(2,1)S(1)}, u32[]{:S(2)}, u32[]{:S(2)}) collective-permute-start(bf16[256,256]{1,0:T(8,128)(2,1)S(1)} %get-tuple-element.39.refs_4_), channel_id=1, source_target_pairs={{0,2},{1,3},{2,0},{3,1},{4,6},{5,7},{6,4},{7,5},{8,10},{9,11},{10,... | collective-permute-start | bytes 393224 | tf_op jit(solution)/shard_map/ppermute | solution.py:183
  15.1 0.0 collective-permute-done.5.refs_6_
  15.1 0.0 collective-permute-start.3
  15.1 0.0 collective-permute-done.10
  15.1 0.5 %collective-permute-start.6 = (bf16[256,384]{1,0:T(8,128)(2,1)S(1)}, bf16[256,384]{1,0:T(8,128)(2,1)S(1)}, u32[]{:S(2)}, u32[]{:S(2)}) collective-permute-start(bf16[256,384]{1,0:T(8,128)(2,1)S(1)} %collective-permute-done.5.refs_6_), channel_id=1, source_target_pairs={{0,1},{1,0},{2,3},{3,2},{4,5},{5,4},{6,7},{7,6},{8,9},{9,8},{10,11... | collective-permute-start | bytes 589832 | tf_op jit(solution)/shard_map/ppermute | solution.py:183
  15.6 0.0 collective-permute-done.11
  15.6 0.7 %collective-permute-done.12 = bf16[2,1,128,128]{3,2,1,0:T(8,128)(2,1)S(1)} collective-permute-done((bf16[2,1,128,128]{3,2,1,0:T(8,128)(2,1)S(1)}, bf16[2,1,128,128]{3,2,1,0:T(8,128)(2,1)S(1)}, u32[]{:S(2)}, u32[]{:S(2)}) %collective-permute-start.12) | collective-permute-done | bytes 65568 | tf_op jit(solution)/shard_map/ppermute | solution.py:183
  16.4 0.1 collective-permute-done.3.refs_3_
  16.5 0.3 collective-permute-done.6.refs_7_
  16.8 0.7 %grid.4 = (f32[1,2,128,384]{3,2,1,0:T(8,128)S(1)}, bf16[1,2,128,384]{3,2,1,0:T(8,128)(2,1)S(1)}) custom-call(bf16[288,256]{1,0:T(8,128)(2,1)S(1)} %get-tuple-element.33.refs_0_, bf16[288,256]{1,0:T(8,128)(2,1)S(1)} %collective-permute-done.refs_1_, bf16[288,256]{1,0:T(8,128)(2,1)S(1)} %collective-permute-done.1.refs_2_, ...), custom_call_target="tpu_custom_call" | custom-call | flops 1 | bytes 1 | tf_op jit(solution)/shard_map/grid/pallas_call | solution.py:225
  17.5 1.6 %collective-permute-start.13 = (bf16[1,2,128,384]{3,2,1,0:T(8,128)(2,1)S(1)}, bf16[1,2,128,384]{3,2,1,0:T(8,128)(2,1)S(1)}, u32[]{:S(2)}, u32[]{:S(2)}) collective-permute-start(bf16[1,2,128,384]{3,2,1,0:T(8,128)(2,1)S(1)} %get-tuple-element.42), channel_id=1, source_target_pairs={{0,4},{1,5},{2,6},{3,7},{4,0},{5,1},{6,2},{7,3},{8,12},{9,13},{10,... | collective-permute-start | bytes 589832 | tf_op jit(solution)/shard_map/ppermute | solution.py:183
  19.1 0.0 collective-permute-done.4.refs_6_
  19.1 0.0 collective-permute-start.7
  19.2 1.3 %collective-permute-done.7.refs_7_ = bf16[256,256]{1,0:T(8,128)(2,1)S(1)} collective-permute-done((bf16[256,256]{1,0:T(8,128)(2,1)S(1)}, bf16[256,256]{1,0:T(8,128)(2,1)S(1)}, u32[]{:S(2)}, u32[]{:S(2)}) %collective-permute-start.7) | collective-permute-done | bytes 131104 | tf_op jit(solution)/shard_map/ppermute | solution.py:183
  20.5 0.4 %grid.5 = (f32[1,2,128,256]{3,2,1,0:T(8,128)S(1)}, bf16[1,2,128,256]{3,2,1,0:T(8,128)(2,1)S(1)}) custom-call(bf16[288,256]{1,0:T(8,128)(2,1)S(1)} %get-tuple-element.33.refs_0_, bf16[288,256]{1,0:T(8,128)(2,1)S(1)} %collective-permute-done.refs_1_, bf16[288,256]{1,0:T(8,128)(2,1)S(1)} %collective-permute-done.1.refs_2_, ...), custom_call_target="tpu_custom_call" | custom-call | flops 1 | bytes 1 | tf_op jit(solution)/shard_map/grid/pallas_call | solution.py:225
  20.9 1.0 %collective-permute-start.8 = (bf16[1,2,128,256]{3,2,1,0:T(8,128)(2,1)S(1)}, bf16[1,2,128,256]{3,2,1,0:T(8,128)(2,1)S(1)}, u32[]{:S(2)}, u32[]{:S(2)}) collective-permute-start(bf16[1,2,128,256]{3,2,1,0:T(8,128)(2,1)S(1)} %get-tuple-element.45), channel_id=1, source_target_pairs={{0,4},{1,5},{2,6},{3,7},{4,0},{5,1},{6,2},{7,3},{8,12},{9,13},{10,... | collective-permute-start | bytes 393224 | tf_op jit(solution)/shard_map/ppermute | solution.py:183
  22.0 3.3 %collective-permute-done.13 = bf16[1,2,128,384]{3,2,1,0:T(8,128)(2,1)S(1)} collective-permute-done((bf16[1,2,128,384]{3,2,1,0:T(8,128)(2,1)S(1)}, bf16[1,2,128,384]{3,2,1,0:T(8,128)(2,1)S(1)}, u32[]{:S(2)}, u32[]{:S(2)}) %collective-permute-start.13) | collective-permute-done | bytes 196640 | tf_op jit(solution)/shard_map/ppermute | solution.py:183
  25.3 2.7 %collective-permute-start.15 = (bf16[1,1,128,384]{3,2,1,0:T(8,128)(2,1)S(1)}, bf16[1,1,128,384]{3,2,1,0:T(8,128)(2,1)S(1)}, u32[]{:S(2)}, u32[]{:S(2)}) collective-permute-start(bf16[1,1,128,384]{3,2,1,0:T(8,128)(2,1)S(1)} %fusion), channel_id=1, source_target_pairs={{0,8},{1,9},{2,10},{3,11},{4,12},{5,13},{6,14},{7,15},{8,0},{9,1},... | collective-permute-start | bytes 294920 | tf_op jit(solution)/shard_map/ppermute | solution.py:183
  28.0 0.3 collective-permute-start.14
  28.4 0.0 collective-permute-done.8
  28.4 2.4 %collective-permute-start.9 = (bf16[1,1,128,256]{3,2,1,0:T(8,128)(2,1)S(1)}, bf16[1,1,128,256]{3,2,1,0:T(8,128)(2,1)S(1)}, u32[]{:S(2)}, u32[]{:S(2)}) collective-permute-start(bf16[1,1,128,256]{3,2,1,0:T(8,128)(2,1)S(1)} %fusion.1), channel_id=1, source_target_pairs={{0,8},{1,9},{2,10},{3,11},{4,12},{5,13},{6,14},{7,15},{8,0},{9,1},... | collective-permute-start | bytes 196616 | tf_op jit(solution)/shard_map/ppermute | solution.py:183
  30.8 1.1 %collective-permute-done.14.refs_2_ = bf16[128,128]{1,0:T(8,128)(2,1)S(1)} collective-permute-done((bf16[128,128]{1,0:T(8,128)(2,1)S(1)}, bf16[128,128]{1,0:T(8,128)(2,1)S(1)}, u32[]{:S(2)}, u32[]{:S(2)}) %collective-permute-start.14) | collective-permute-done | bytes 32800 | tf_op jit(solution)/shard_map/ppermute | solution.py:183
  31.9 2.0 %collective-permute-done.15 = bf16[1,1,128,384]{3,2,1,0:T(8,128)(2,1)S(1)} collective-permute-done((bf16[1,1,128,384]{3,2,1,0:T(8,128)(2,1)S(1)}, bf16[1,1,128,384]{3,2,1,0:T(8,128)(2,1)S(1)}, u32[]{:S(2)}, u32[]{:S(2)}) %collective-permute-start.15) | collective-permute-done | bytes 98336 | tf_op jit(solution)/shard_map/ppermute | solution.py:183
  33.9 0.4 %delay.2.refs_3_ = f32[2,384,128]{2,1,0:T(8,128)S(1)} custom-call(bf16[768,384]{1,0:T(8,128)(2,1)S(1)} %fold.1.refs_0_, f32[128,128]{1,0:T(8,128)S(1)} %slice_bitcast_fusion.refs_1_, bf16[128,128]{1,0:T(8,128)(2,1)S(1)} %collective-permute-done.14.refs_2_, f32[128,384]{1,0:T(8,128)S(1)} %select_bitcast_fusion.refs_3_, bf16[128,384]{1,0:T(8,128)(2,1)S(1)} %bitcast.18), custom_call_target="tpu_custom_call" | custom-call | flops 1 | bytes 1 | tf_op jit(solution)/shard_map/delay/pallas_call | solution.py:285
  34.3 1.0 %collective-permute-done.9 = bf16[1,1,128,256]{3,2,1,0:T(8,128)(2,1)S(1)} collective-permute-done((bf16[1,1,128,256]{3,2,1,0:T(8,128)(2,1)S(1)}, bf16[1,1,128,256]{3,2,1,0:T(8,128)(2,1)S(1)}, u32[]{:S(2)}, u32[]{:S(2)}) %collective-permute-start.9) | collective-permute-done | bytes 65568 | tf_op jit(solution)/shard_map/ppermute | solution.py:183
  35.3 1.0 %delay.3 = f32[2,384,128]{2,1,0:T(8,128)} custom-call(bf16[768,384]{1,0:T(8,128)(2,1)S(1)} %fold.1.refs_0_, f32[128,256]{1,0:T(8,128)S(1)} %select_bitcast_fusion.1.refs_1_, bf16[128,256]{1,0:T(8,128)(2,1)S(1)} %bitcast.19, f32[2,384,128]{2,1,0:T(8,128)S(1)} %delay.2.refs_3_), custom_call_target="tpu_custom_call" | custom-call | flops 1 | bytes 1 | tf_op jit(solution)/shard_map/delay/pallas_call | solution.py:285
  (9 shorter events, 0.2 us)
Async XLA Ops:
  0.0 10.3 %copy-start = (bf16[768,384]{1,0:T(8,128)(2,1)S(1)}, bf16[768,384]{1,0:T(8,128)(2,1)}, u32[]{:S(2)}) copy-start(bf16[768,384]{1,0:T(8,128)(2,1)} %constant.38.clone.tables) | copy-start | bytes 1769476
  0.0 5.1 %collective-permute-start.2 = (bf16[2,256,384]{2,1,0:T(8,128)(2,1)}, bf16[2,256,384]{2,1,0:T(8,128)(2,1)S(1)}, u32[]{:S(2)}, u32[]{:S(2)}) collective-permute-start(bf16[2,256,384]{2,1,0:T(8,128)(2,1)} %refs_0_.1), channel_id=1, source_target_pairs={{0,1},{1,0},{2,3},{3,2},{4,5},{5,4},{6,7},{7,6},{8,9},{9,8},{10,11... | collective-permute-start | bytes 1179656 | tf_op jit(solution)/shard_map/ppermute | solution.py:183
  2.0 3.1 %collective-permute-start = (bf16[288,256]{1,0:T(8,128)(2,1)S(1)}, bf16[288,256]{1,0:T(8,128)(2,1)S(1)}, u32[]{:S(2)}, u32[]{:S(2)}) collective-permute-start(bf16[288,256]{1,0:T(8,128)(2,1)S(1)} %get-tuple-element.34), channel_id=1, source_target_pairs={{0,1},{1,0},{2,3},{3,2},{4,5},{5,4},{6,7},{7,6},{8,9},{9,8},{10,11... | collective-permute-start | bytes 442376 | tf_op jit(solution)/shard_map/ppermute | solution.py:183
  2.1 13.0 %collective-permute-start.5 = (bf16[256,384]{1,0:T(8,128)(2,1)S(1)}, bf16[256,384]{1,0:T(8,128)(2,1)S(1)}, u32[]{:S(2)}, u32[]{:S(2)}) collective-permute-start(bf16[256,384]{1,0:T(8,128)(2,1)S(1)} %get-tuple-element.40.refs_4_), channel_id=1, source_target_pairs={{0,2},{1,3},{2,0},{3,1},{4,6},{5,7},{6,4},{7,5},{8,10},{9,11},{10,... | collective-permute-start | bytes 589832 | tf_op jit(solution)/shard_map/ppermute | solution.py:183
  5.1 8.3 %collective-permute-start.1 = (bf16[288,256]{1,0:T(8,128)(2,1)S(1)}, bf16[288,256]{1,0:T(8,128)(2,1)S(1)}, u32[]{:S(2)}, u32[]{:S(2)}) collective-permute-start(bf16[288,256]{1,0:T(8,128)(2,1)S(1)} %get-tuple-element.35), channel_id=1, source_target_pairs={{0,2},{1,3},{2,0},{3,1},{4,6},{5,7},{6,4},{7,5},{8,10},{9,11},{10,... | collective-permute-start | bytes 442376 | tf_op jit(solution)/shard_map/ppermute | solution.py:183
  5.1 5.2 %copy-start.1 = (bf16[384,384]{1,0:T(8,128)(2,1)S(1)}, bf16[384,384]{1,0:T(8,128)(2,1)}, u32[]{:S(2)}) copy-start(bf16[384,384]{1,0:T(8,128)(2,1)} %inv_cov) | copy-start | bytes 884740
  5.6 9.6 %collective-permute-start.10 = (bf16[2,1,128,128]{3,2,1,0:T(8,128)(2,1)S(1)}, bf16[2,1,128,128]{3,2,1,0:T(8,128)(2,1)S(1)}, u32[]{:S(2)}, u32[]{:S(2)}) collective-permute-start(bf16[2,1,128,128]{3,2,1,0:T(8,128)(2,1)S(1)} %get-tuple-element.49), channel_id=1, source_target_pairs={{0,4},{1,5},{2,6},{3,7},{4,0},{5,1},{6,2},{7,3},{8,12},{9,13},{10,... | collective-permute-start | bytes 196616 | tf_op jit(solution)/shard_map/ppermute | solution.py:183
  7.7 8.0 %collective-permute-start.11 = (bf16[2,1,128,128]{3,2,1,0:T(8,128)(2,1)S(1)}, bf16[2,1,128,128]{3,2,1,0:T(8,128)(2,1)S(1)}, u32[]{:S(2)}, u32[]{:S(2)}) collective-permute-start(bf16[2,1,128,128]{3,2,1,0:T(8,128)(2,1)S(1)} %get-tuple-element.50), channel_id=1, source_target_pairs={{0,8},{1,9},{2,10},{3,11},{4,12},{5,13},{6,14},{7,15},{8,0},{9,1},... | collective-permute-start | bytes 196616 | tf_op jit(solution)/shard_map/ppermute | solution.py:183
  10.2 6.1 %collective-permute-start.12 = (bf16[2,1,128,128]{3,2,1,0:T(8,128)(2,1)S(1)}, bf16[2,1,128,128]{3,2,1,0:T(8,128)(2,1)S(1)}, u32[]{:S(2)}, u32[]{:S(2)}) collective-permute-start(bf16[2,1,128,128]{3,2,1,0:T(8,128)(2,1)S(1)} %get-tuple-element.51), channel_id=1, source_target_pairs={{0,12},{1,13},{2,14},{3,15},{4,8},{5,9},{6,10},{7,11},{8,4},{9,5},... | collective-permute-start | bytes 196616 | tf_op jit(solution)/shard_map/ppermute | solution.py:183
  13.4 5.8 %collective-permute-start.4 = (bf16[256,256]{1,0:T(8,128)(2,1)S(1)}, bf16[256,256]{1,0:T(8,128)(2,1)S(1)}, u32[]{:S(2)}, u32[]{:S(2)}) collective-permute-start(bf16[256,256]{1,0:T(8,128)(2,1)S(1)} %get-tuple-element.39.refs_4_), channel_id=1, source_target_pairs={{0,2},{1,3},{2,0},{3,1},{4,6},{5,7},{6,4},{7,5},{8,10},{9,11},{10,... | collective-permute-start | bytes 393224 | tf_op jit(solution)/shard_map/ppermute | solution.py:183
  15.1 1.4 %collective-permute-start.3 = (bf16[288,256]{1,0:T(8,128)(2,1)S(1)}, bf16[288,256]{1,0:T(8,128)(2,1)S(1)}, u32[]{:S(2)}, u32[]{:S(2)}) collective-permute-start(bf16[288,256]{1,0:T(8,128)(2,1)S(1)} %collective-permute-done.1.refs_2_), channel_id=1, source_target_pairs={{0,1},{1,0},{2,3},{3,2},{4,5},{5,4},{6,7},{7,6},{8,9},{9,8},{10,11... | collective-permute-start | bytes 442376 | tf_op jit(solution)/shard_map/ppermute | solution.py:183
  15.1 1.6 %collective-permute-start.6 = (bf16[256,384]{1,0:T(8,128)(2,1)S(1)}, bf16[256,384]{1,0:T(8,128)(2,1)S(1)}, u32[]{:S(2)}, u32[]{:S(2)}) collective-permute-start(bf16[256,384]{1,0:T(8,128)(2,1)S(1)} %collective-permute-done.5.refs_6_), channel_id=1, source_target_pairs={{0,1},{1,0},{2,3},{3,2},{4,5},{5,4},{6,7},{7,6},{8,9},{9,8},{10,11... | collective-permute-start | bytes 589832 | tf_op jit(solution)/shard_map/ppermute | solution.py:183
  17.5 7.8 %collective-permute-start.13 = (bf16[1,2,128,384]{3,2,1,0:T(8,128)(2,1)S(1)}, bf16[1,2,128,384]{3,2,1,0:T(8,128)(2,1)S(1)}, u32[]{:S(2)}, u32[]{:S(2)}) collective-permute-start(bf16[1,2,128,384]{3,2,1,0:T(8,128)(2,1)S(1)} %get-tuple-element.42), channel_id=1, source_target_pairs={{0,4},{1,5},{2,6},{3,7},{4,0},{5,1},{6,2},{7,3},{8,12},{9,13},{10,... | collective-permute-start | bytes 589832 | tf_op jit(solution)/shard_map/ppermute | solution.py:183
  19.1 1.3 %collective-permute-start.7 = (bf16[256,256]{1,0:T(8,128)(2,1)S(1)}, bf16[256,256]{1,0:T(8,128)(2,1)S(1)}, u32[]{:S(2)}, u32[]{:S(2)}) collective-permute-start(bf16[256,256]{1,0:T(8,128)(2,1)S(1)} %collective-permute-done.4.refs_6_), channel_id=1, source_target_pairs={{0,1},{1,0},{2,3},{3,2},{4,5},{5,4},{6,7},{7,6},{8,9},{9,8},{10,11... | collective-permute-start | bytes 393224 | tf_op jit(solution)/shard_map/ppermute | solution.py:183
  20.9 7.4 %collective-permute-start.8 = (bf16[1,2,128,256]{3,2,1,0:T(8,128)(2,1)S(1)}, bf16[1,2,128,256]{3,2,1,0:T(8,128)(2,1)S(1)}, u32[]{:S(2)}, u32[]{:S(2)}) collective-permute-start(bf16[1,2,128,256]{3,2,1,0:T(8,128)(2,1)S(1)} %get-tuple-element.45), channel_id=1, source_target_pairs={{0,4},{1,5},{2,6},{3,7},{4,0},{5,1},{6,2},{7,3},{8,12},{9,13},{10,... | collective-permute-start | bytes 393224 | tf_op jit(solution)/shard_map/ppermute | solution.py:183
  25.3 8.6 %collective-permute-start.15 = (bf16[1,1,128,384]{3,2,1,0:T(8,128)(2,1)S(1)}, bf16[1,1,128,384]{3,2,1,0:T(8,128)(2,1)S(1)}, u32[]{:S(2)}, u32[]{:S(2)}) collective-permute-start(bf16[1,1,128,384]{3,2,1,0:T(8,128)(2,1)S(1)} %fusion), channel_id=1, source_target_pairs={{0,8},{1,9},{2,10},{3,11},{4,12},{5,13},{6,14},{7,15},{8,0},{9,1},... | collective-permute-start | bytes 294920 | tf_op jit(solution)/shard_map/ppermute | solution.py:183
  28.0 3.9 %collective-permute-start.14 = (bf16[128,128]{1,0:T(8,128)(2,1)S(1)}, bf16[128,128]{1,0:T(8,128)(2,1)S(1)}, u32[]{:S(2)}, u32[]{:S(2)}) collective-permute-start(bf16[128,128]{1,0:T(8,128)(2,1)S(1)} %fusion.2), channel_id=1, source_target_pairs={{0,2},{1,3},{2,0},{3,1},{4,6},{5,7},{6,4},{7,5},{8,10},{9,11},{10,... | collective-permute-start | bytes 98312 | tf_op jit(solution)/shard_map/ppermute | solution.py:183
  28.4 6.9 %collective-permute-start.9 = (bf16[1,1,128,256]{3,2,1,0:T(8,128)(2,1)S(1)}, bf16[1,1,128,256]{3,2,1,0:T(8,128)(2,1)S(1)}, u32[]{:S(2)}, u32[]{:S(2)}) collective-permute-start(bf16[1,1,128,256]{3,2,1,0:T(8,128)(2,1)S(1)} %fusion.1), channel_id=1, source_target_pairs={{0,8},{1,9},{2,10},{3,11},{4,12},{5,13},{6,14},{7,15},{8,0},{9,1},... | collective-permute-start | bytes 196616 | tf_op jit(solution)/shard_map/ppermute | solution.py:183

commit v4 on v3

--- a/solution.py
+++ b/solution.py
@@ -14,11 +14,11 @@
 VMEM_BYTES = 48 * 1024 * 1024
 PLAN = ((0,), (1, 2, 3), (4, 5))
 NEAR = (0,)
-DIRECT = (0,)
-PIECES = 1
+DIRECT = ()
+PIECES = 2
 SECOND = (1, 0, 2)
 LAST = (2,)
-AFTER = {'relay': ['grid0'], 'relay1': ['grid0'], 'relay2': ['grid1'], 'third0': ['grid1', 'grid2', 'second1'], 'second2': ['second0']}
+AFTER = {'relay1': ['grid0', 'got0'], 'relay2': ['grid1'], 'third0': ['grid1', 'second1'], 'over2': ['core']}
 
 
 def delay_tables(channels):
@@ -34,7 +34,7 @@
 
 
 def prep_body(
-    nblocks, vis, kernel_in, weights_in, counts_in, blocks_in, own, core, far, *refs
+    nblocks, vis, kernel_in, weights_in, counts_in, blocks_in, own, core, *refs
 ):
     chunks, (kernel, weights, counts, blocks, sems, cut_sems) = refs[: len(PLAN)], refs[len(PLAN) :]
     copies = [
@@ -76,7 +76,7 @@
                 ).astype(jnp.bfloat16),
             )
         )
-    for out, flips in ((own, (0, 2)), (core, (1, 3)), (far, (2, 3))):
+    for out, flips in ((own, (0, 2)), (core, (1, 3))):
         for i, flip in enumerate(flips):
             out[i * cells : (i + 1) * cells, :] = picked[flip][0]
             out[2 * cells + i * LABEL_ROWS : 2 * cells + (i + 1) * LABEL_ROWS, :] = picked[flip][1]
@@ -100,8 +100,9 @@
         own, core, vis, vis_core = refs
         classes = [[listed(own, i, cells), listed(core, i, cells)] for i in range(2)]
     else:
-        own, core, far, relay, vis, vis_core, vis_far, *vis_relay = refs
-        classes = [[listed(table, int(i == 3), cells) for i, table in enumerate((own, core, far, relay))]]
+        own, core, far, vis, vis_core, vis_far, *vis_relay = refs
+        held = ((own, 0), (core, 0), (far, 0), (far, 1))
+        classes = [[listed(table, i, cells) for table, i in held]]
     samples = own.shape[1]
     rows[:samples, :] = vis[...]
     for i, u in enumerate(units):
@@ -188,11 +189,11 @@
 
     listing = shape((2 * (cells + LABEL_ROWS), samples), bf16)
     operands = (visibilities, kernel, weights, counts, blocks)
-    own, core, far, *chunks = pl.pallas_call(
+    own, core, *chunks = pl.pallas_call(
         lambda *refs: prep_body(nblocks, *refs),
         in_specs=[hbm] * 5,
-        out_specs=[pl.BlockSpec(memory_space=pltpu.VMEM)] * 3 + [anywhere] * len(PLAN),
-        out_shape=[listing] * 3
+        out_specs=[pl.BlockSpec(memory_space=pltpu.VMEM)] * 2 + [anywhere] * len(PLAN),
+        out_shape=[listing] * 2
         + [shape((samples, len(units) * CHUNK), bf16) for units in PLAN],
         scratch_shapes=[
             pltpu.VMEM(kernel.shape, bf16),
@@ -208,10 +209,12 @@
     me = lax.axis_index("chan")
     vis_core = swap(visibilities, 1)
     core = swap(core, 1)
-    far = swap(far, 2)
-    vis_far = {n: swap(chunks[n], 2) for n in range(len(PLAN)) if n not in NEAR}
-
-    made.update({f"far{n}": values for n, values in vis_far.items()})
+    tables, label = 2 * cells, 2 * cells + LABEL_ROWS
+    far = [x[a:b] for a, b in ((cells, tables), (label, None)) for x in (own, core)]
+    far = swap(jnp.concatenate(tied("far", *far)), 2)
+
+    made["far"] = far
+    made["core"] = core
 
     def grid(n, *operands):
         sources = 2 if n in NEAR else 4
@@ -239,8 +242,10 @@
         return keep, arrived
 
     state = {n: grid(n, own, core, chunks[n], vis_core) for n in NEAR}
-    (far,) = tied("relay", far)
-    relay = swap(far, 1)
+    vis_far = {
+        n: swap(tied(f"over{n}", chunks[n])[0], 2) for n in range(len(PLAN)) if n not in NEAR
+    }
+    made.update({f"far{n}": values for n, values in vis_far.items()})
     for n in range(len(PLAN)):
         if n in NEAR:
             continue
@@ -248,7 +253,7 @@
         made[f"mine{n}"] = mine
         each = samples // PIECES
         vis_relay = [swap(mine[i * each : (i + 1) * each], 1) for i in range(PIECES)]
-        state[n] = grid(n, own, core, far, relay, chunks[n], vis_core, mine, *vis_relay)
+        state[n] = grid(n, own, core, far, chunks[n], vis_core, mine, *vis_relay)
 
     held = {}
     for n in SECOND:
@@ -264,6 +269,7 @@
             send = jnp.where(upper, summed[:, :, 0], summed[:, :, 1]).astype(bf16)
             made[f"second{n}"] = send
             arrived = [swap(send, bit)]
+            made[f"mid{n}"] = arrived[0]
         keep, arrived = keep[:, 0], [piece[:, 0] for piece in arrived]
         if n in NEAR or len(arrived) > 1:
             keep = keep + sum(piece.astype(f32) for piece in arrived[: None if n in NEAR else -1])

time: 36.5 us -> 34.4 us (0.942)
  waiting for transfers between devices: 12.4 us -> 9.42 us
  starting transfers between devices: 18.6 us -> 19.3 us
    ppermute x16, waiting for transfers between devices: 12.4 us -> 9.42 us  [swap(): return lax.ppermute(values, 'chan', [(i, i ^ bit) for i in range(nblocks)])]
    ppermute x16, starting transfers between devices: 18.6 us -> 19.3 us  [swap(): return lax.ppermute(values, 'chan', [(i, i ^ bit) for i in range(nblocks)])]
  transfers between devices with their start and end apart: 16 -> 16, of which waited for: 9 -> 8; matrix products, arithmetic and copies ran while one was open for 0% -> 1% of each run, Pallas kernels for 11% -> 12%
where the time goes in v4:
time: 34.4 us; the launch traced here: 34.2 us
  starting transfers between devices  19.3 us (56%)
  waiting for transfers between devices  9.42 us (27%)
  Pallas kernels  5 us (15%)
    ppermute x16, starting transfers between devices, swap(): return lax.ppermute(values, 'chan', [(i, i ^ bit) for i in range(nblocks)])  19.3 us
    ppermute x16, waiting for transfers between devices, swap(): return lax.ppermute(values, 'chan', [(i, i ^ bit) for i in range(nblocks)])  9.42 us
    pallas_call x3, Pallas kernels, grid(): pl.pallas_call(lambda *refs: grid_body(groups, n, *refs), out_shape=outs,...  1.62 us
    pallas_call x1, Pallas kernels, on_device(): pl.pallas_call(lambda *refs: prep_body(nblocks, *refs), in_specs=[hbm] *...  1.5 us
    pallas_call x2, Pallas kernels, delayed(): pl.pallas_call(lambda *refs: delay_body([PLAN[n] for n in chosen], last,...  1.38 us
  transfers between devices with their start and end apart: 16, of which 8 were waited for; matrix products, arithmetic and copies ran while one was open for 1% of the time, Pallas kernels for 12%

profile of v4, /device:TPU:0, one launch (start us, length us, event | category | flops | bytes accessed | tf_op | source)
XLA Modules:
  0.0 34.2 jit_solution(14153645056781323381)
XLA Ops:
  0.0 0.5 %collective-permute-start.2 = (bf16[2,256,384]{2,1,0:T(8,128)(2,1)}, bf16[2,256,384]{2,1,0:T(8,128)(2,1)S(1)}, u32[]{:S(2)}, u32[]{:S(2)}) collective-permute-start(bf16[2,256,384]{2,1,0:T(8,128)(2,1)} %refs_0_.1), channel_id=1, source_target_pairs={{0,1},{1,0},{2,3},{3,2},{4,5},{5,4},{6,7},{7,6},{8,9},{9,8},{10,11... | collective-permute-start | bytes 1179656 | tf_op jit(solution)/shard_map/ppermute | solution.py:184
  0.5 1.5 %prep.1 = (bf16[288,256]{1,0:T(8,128)(2,1)S(1)}, bf16[288,256]{1,0:T(8,128)(2,1)S(1)}, bf16[256,128]{1,0:T(8,128)(2,1)S(1)}, bf16[256,384]{1,0:T(8,128)(2,1)S(1)}, bf16[256,256]{1,0:T(8,128)(2,1)S(1)}) custom-call(bf16[2,256,384]{2,1,0:T(8,128)(2,1)} %refs_0_.1, bf16[4,256,128]{2,1,0:T(8,128)(2,1)} %refs_1_.1, s32[256]{0:T(256)} %refs_2_.1, s32[256]{0:T(256)} %refs_3_.1, ...), custom_call_target="tpu_custom_call" | custom-call | flops 1 | bytes 1 | tf_op jit(solution)/shard_map/prep/pallas_call | solution.py:192
  2.0 0.0 copy-start
  2.0 0.1 collective-permute-start
  2.1 3.0 %collective-permute-start.4 = (bf16[256,384]{1,0:T(8,128)(2,1)S(1)}, bf16[256,384]{1,0:T(8,128)(2,1)S(1)}, u32[]{:S(2)}, u32[]{:S(2)}) collective-permute-start(bf16[256,384]{1,0:T(8,128)(2,1)S(1)} %get-tuple-element.36.refs_3_), channel_id=1, source_target_pairs={{0,2},{1,3},{2,0},{3,1},{4,6},{5,7},{6,4},{7,5},{8,10},{9,11},{10,... | collective-permute-start | bytes 589832 | tf_op jit(solution)/shard_map/ppermute | solution.py:184
  5.1 0.0 collective-permute-done.refs_1_
  5.1 0.0 collective-permute-done.2.refs_3_.refs_4_
  5.1 0.0 copy-start.1
  5.1 0.4 %grid.3 = (f32[2,2,128,128]{3,2,1,0:T(8,128)S(1)}, bf16[2,2,128,128]{3,2,1,0:T(8,128)(2,1)S(1)}) custom-call(bf16[288,256]{1,0:T(8,128)(2,1)S(1)} %get-tuple-element.28.refs_0_, bf16[288,256]{1,0:T(8,128)(2,1)S(1)} %collective-permute-done.refs_1_, bf16[256,128]{1,0:T(8,128)(2,1)S(1)} %get-tuple-element.37.refs_2_, ...), custom_call_target="tpu_custom_call" | custom-call | flops 1 | bytes 1 | tf_op jit(solution)/shard_map/grid/pallas_call | solution.py:228
  5.5 1.6 %collective-permute-start.5 = (bf16[2,2,128,128]{3,2,0,1:T(8,128)(2,1)S(1)}, bf16[2,2,128,128]{3,2,0,1:T(8,128)(2,1)S(1)}, u32[]{:S(2)}, u32[]{:S(2)}) collective-permute-start(bf16[2,2,128,128]{3,2,0,1:T(8,128)(2,1)S(1)} %copy.8), channel_id=1, source_target_pairs={{0,4},{1,5},{2,6},{3,7},{4,0},{5,1},{6,2},{7,3},{8,12},{9,13},{10,... | collective-permute-start | bytes 393224 | tf_op jit(solution)/shard_map/ppermute | solution.py:184
  7.2 0.0 copy-done
  7.2 0.0 copy-done.1
  7.2 0.5 %fold.1.refs_0_ = bf16[768,384]{1,0:T(8,128)(2,1)S(1)} custom-call(bf16[768,384]{1,0:T(8,128)(2,1)S(1)} %copy-done, bf16[384,384]{1,0:T(8,128)(2,1)S(1)} %copy-done.1), custom_call_target="tpu_custom_call" | custom-call | flops 1 | bytes 1 | tf_op jit(solution)/shard_map/fold/pallas_call | solution.py:283
  7.8 1.1 %collective-permute-start.1 = (bf16[288,256]{1,0:T(8,128)(2,1)S(1)}, bf16[288,256]{1,0:T(8,128)(2,1)S(1)}, u32[]{:S(2)}, u32[]{:S(2)}) collective-permute-start(bf16[288,256]{1,0:T(8,128)(2,1)S(1)} %pad_maximum_fusion), channel_id=1, source_target_pairs={{0,2},{1,3},{2,0},{3,1},{4,6},{5,7},{6,4},{7,5},{8,10},{9,11},{10,... | collective-permute-start | bytes 442376 | tf_op jit(solution)/shard_map/ppermute | solution.py:184
  8.9 1.0 %collective-permute-start.3 = (bf16[256,256]{1,0:T(8,128)(2,1)S(1)}, bf16[256,256]{1,0:T(8,128)(2,1)S(1)}, u32[]{:S(2)}, u32[]{:S(2)}) collective-permute-start(bf16[256,256]{1,0:T(8,128)(2,1)S(1)} %get-tuple-element.35.refs_3_), channel_id=1, source_target_pairs={{0,2},{1,3},{2,0},{3,1},{4,6},{5,7},{6,4},{7,5},{8,10},{9,11},{10,... | collective-permute-start | bytes 393224 | tf_op jit(solution)/shard_map/ppermute | solution.py:184
  9.9 0.4 %collective-permute-done.4.refs_5_ = bf16[256,384]{1,0:T(8,128)(2,1)S(1)} collective-permute-done((bf16[256,384]{1,0:T(8,128)(2,1)S(1)}, bf16[256,384]{1,0:T(8,128)(2,1)S(1)}, u32[]{:S(2)}, u32[]{:S(2)}) %collective-permute-start.4) | collective-permute-done | bytes 196640 | tf_op jit(solution)/shard_map/ppermute | solution.py:184
  10.3 0.5 %collective-permute-done.5 = bf16[2,2,128,128]{3,2,0,1:T(8,128)(2,1)S(1)} collective-permute-done((bf16[2,2,128,128]{3,2,0,1:T(8,128)(2,1)S(1)}, bf16[2,2,128,128]{3,2,0,1:T(8,128)(2,1)S(1)}, u32[]{:S(2)}, u32[]{:S(2)}) %collective-permute-start.5) | collective-permute-done | bytes 131104 | tf_op jit(solution)/shard_map/ppermute | solution.py:184
  10.9 2.7 %collective-permute-start.12 = (bf16[2,1,128,128]{3,2,0,1:T(8,128)(2,1)S(1)}, bf16[2,1,128,128]{3,2,0,1:T(8,128)(2,1)S(1)}, u32[]{:S(2)}, u32[]{:S(2)}) collective-permute-start(bf16[2,1,128,128]{3,2,0,1:T(8,128)(2,1)S(1)} %fusion.3), channel_id=1, source_target_pairs={{0,8},{1,9},{2,10},{3,11},{4,12},{5,13},{6,14},{7,15},{8,0},{9,1},... | collective-permute-start | bytes 196616 | tf_op jit(solution)/shard_map/ppermute | solution.py:184
  13.6 0.1 collective-permute-start.6
  13.7 0.5 %collective-permute-start.7 = (bf16[128,384]{1,0:T(8,128)(2,1)S(1)}, bf16[128,384]{1,0:T(8,128)(2,1)S(1)}, u32[]{:S(2)}, u32[]{:S(2)}) collective-permute-start(bf16[128,384]{1,0:T(8,128)(2,1)S(1)} %get-tuple-element.47), channel_id=1, source_target_pairs={{0,1},{1,0},{2,3},{3,2},{4,5},{5,4},{6,7},{7,6},{8,9},{9,8},{10,11... | collective-permute-start | bytes 294920 | tf_op jit(solution)/shard_map/ppermute | solution.py:184
  14.2 1.9 %collective-permute-done.12 = bf16[2,1,128,128]{3,2,0,1:T(8,128)(2,1)S(1)} collective-permute-done((bf16[2,1,128,128]{3,2,0,1:T(8,128)(2,1)S(1)}, bf16[2,1,128,128]{3,2,0,1:T(8,128)(2,1)S(1)}, u32[]{:S(2)}, u32[]{:S(2)}) %collective-permute-start.12) | collective-permute-done | bytes 65568 | tf_op jit(solution)/shard_map/ppermute | solution.py:184
  16.1 0.0 collective-permute-done.1.refs_2_
  16.1 0.0 collective-permute-done.6.refs_6_
  16.1 0.0 collective-permute-done.7.refs_7_
  16.2 0.7 %grid.4 = (f32[1,2,128,384]{3,2,1,0:T(8,128)S(1)}, bf16[1,2,128,384]{3,2,1,0:T(8,128)(2,1)S(1)}) custom-call(bf16[288,256]{1,0:T(8,128)(2,1)S(1)} %get-tuple-element.28.refs_0_, bf16[288,256]{1,0:T(8,128)(2,1)S(1)} %collective-permute-done.refs_1_, bf16[288,256]{1,0:T(8,128)(2,1)S(1)} %collective-permute-done.1.refs_2_, ...), custom_call_target="tpu_custom_call" | custom-call | flops 1 | bytes 1 | tf_op jit(solution)/shard_map/grid/pallas_call | solution.py:228
  16.9 2.1 %collective-permute-start.13 = (bf16[1,2,128,384]{3,2,1,0:T(8,128)(2,1)S(1)}, bf16[1,2,128,384]{3,2,1,0:T(8,128)(2,1)S(1)}, u32[]{:S(2)}, u32[]{:S(2)}) collective-permute-start(bf16[1,2,128,384]{3,2,1,0:T(8,128)(2,1)S(1)} %get-tuple-element.40), channel_id=1, source_target_pairs={{0,4},{1,5},{2,6},{3,7},{4,0},{5,1},{6,2},{7,3},{8,12},{9,13},{10,... | collective-permute-start | bytes 589832 | tf_op jit(solution)/shard_map/ppermute | solution.py:184
  19.0 0.0 collective-permute-done.3.refs_5_
  19.1 0.1 collective-permute-start.8
  19.1 0.5 %collective-permute-start.9 = (bf16[128,256]{1,0:T(8,128)(2,1)S(1)}, bf16[128,256]{1,0:T(8,128)(2,1)S(1)}, u32[]{:S(2)}, u32[]{:S(2)}) collective-permute-start(bf16[128,256]{1,0:T(8,128)(2,1)S(1)} %get-tuple-element.49), channel_id=1, source_target_pairs={{0,1},{1,0},{2,3},{3,2},{4,5},{5,4},{6,7},{7,6},{8,9},{9,8},{10,11... | collective-permute-start | bytes 196616 | tf_op jit(solution)/shard_map/ppermute | solution.py:184
  19.6 0.7 %collective-permute-done.8.refs_6_ = bf16[128,256]{1,0:T(8,128)(2,1)S(1)} collective-permute-done((bf16[128,256]{1,0:T(8,128)(2,1)S(1)}, bf16[128,256]{1,0:T(8,128)(2,1)S(1)}, u32[]{:S(2)}, u32[]{:S(2)}) %collective-permute-start.8) | collective-permute-done | bytes 65568 | tf_op jit(solution)/shard_map/ppermute | solution.py:184
  20.4 0.2 collective-permute-done.9.refs_7_
  20.5 0.4 %grid.5 = (f32[1,2,128,256]{3,2,1,0:T(8,128)S(1)}, bf16[1,2,128,256]{3,2,1,0:T(8,128)(2,1)S(1)}) custom-call(bf16[288,256]{1,0:T(8,128)(2,1)S(1)} %get-tuple-element.28.refs_0_, bf16[288,256]{1,0:T(8,128)(2,1)S(1)} %collective-permute-done.refs_1_, bf16[288,256]{1,0:T(8,128)(2,1)S(1)} %collective-permute-done.1.refs_2_, ...), custom_call_target="tpu_custom_call" | custom-call | flops 1 | bytes 1 | tf_op jit(solution)/shard_map/grid/pallas_call | solution.py:228
  21.0 0.1 collective-permute-start.10
  21.1 2.3 %collective-permute-done.13 = bf16[1,2,128,384]{3,2,1,0:T(8,128)(2,1)S(1)} collective-permute-done((bf16[1,2,128,384]{3,2,1,0:T(8,128)(2,1)S(1)}, bf16[1,2,128,384]{3,2,1,0:T(8,128)(2,1)S(1)}, u32[]{:S(2)}, u32[]{:S(2)}) %collective-permute-start.13) | collective-permute-done | bytes 196640 | tf_op jit(solution)/shard_map/ppermute | solution.py:184
  23.4 2.1 %collective-permute-start.15 = (bf16[1,1,128,384]{3,2,1,0:T(8,128)(2,1)S(1)}, bf16[1,1,128,384]{3,2,1,0:T(8,128)(2,1)S(1)}, u32[]{:S(2)}, u32[]{:S(2)}) collective-permute-start(bf16[1,1,128,384]{3,2,1,0:T(8,128)(2,1)S(1)} %fusion.1), channel_id=1, source_target_pairs={{0,8},{1,9},{2,10},{3,11},{4,12},{5,13},{6,14},{7,15},{8,0},{9,1},... | collective-permute-start | bytes 294920 | tf_op jit(solution)/shard_map/ppermute | solution.py:184
  25.5 1.5 %collective-permute-start.14 = (bf16[128,128]{1,0:T(8,128)(2,1)S(1)}, bf16[128,128]{1,0:T(8,128)(2,1)S(1)}, u32[]{:S(2)}, u32[]{:S(2)}) collective-permute-start(bf16[128,128]{1,0:T(8,128)(2,1)S(1)} %fusion.4), channel_id=1, source_target_pairs={{0,2},{1,3},{2,0},{3,1},{4,6},{5,7},{6,4},{7,5},{8,10},{9,11},{10,... | collective-permute-start | bytes 98312 | tf_op jit(solution)/shard_map/ppermute | solution.py:184
  27.1 0.8 %collective-permute-done.10 = bf16[1,2,128,256]{3,2,1,0:T(8,128)(2,1)S(1)} collective-permute-done((bf16[1,2,128,256]{3,2,1,0:T(8,128)(2,1)S(1)}, bf16[1,2,128,256]{3,2,1,0:T(8,128)(2,1)S(1)}, u32[]{:S(2)}, u32[]{:S(2)}) %collective-permute-start.10) | collective-permute-done | bytes 131104 | tf_op jit(solution)/shard_map/ppermute | solution.py:184
  27.9 2.3 %collective-permute-start.11 = (bf16[1,1,128,256]{3,2,1,0:T(8,128)(2,1)S(1)}, bf16[1,1,128,256]{3,2,1,0:T(8,128)(2,1)S(1)}, u32[]{:S(2)}, u32[]{:S(2)}) collective-permute-start(bf16[1,1,128,256]{3,2,1,0:T(8,128)(2,1)S(1)} %fusion.2), channel_id=1, source_target_pairs={{0,8},{1,9},{2,10},{3,11},{4,12},{5,13},{6,14},{7,15},{8,0},{9,1},... | collective-permute-start | bytes 196616 | tf_op jit(solution)/shard_map/ppermute | solution.py:184
  30.2 0.0 collective-permute-done.14.refs_2_
  30.2 0.0 collective-permute-done.15
  30.2 0.4 %delay.2.refs_3_ = f32[2,384,128]{2,1,0:T(8,128)S(1)} custom-call(bf16[768,384]{1,0:T(8,128)(2,1)S(1)} %fold.1.refs_0_, f32[128,128]{1,0:T(8,128)S(1)} %slice_bitcast_fusion.refs_1_, bf16[128,128]{1,0:T(8,128)(2,1)S(1)} %collective-permute-done.14.refs_2_, f32[128,384]{1,0:T(8,128)S(1)} %select_bitcast_fusion.refs_3_, bf16[128,384]{1,0:T(8,128)(2,1)S(1)} %bitcast.27), custom_call_target="tpu_custom_call" | custom-call | flops 1 | bytes 1 | tf_op jit(solution)/shard_map/delay/pallas_call | solution.py:291
  30.6 2.6 %collective-permute-done.11 = bf16[1,1,128,256]{3,2,1,0:T(8,128)(2,1)S(1)} collective-permute-done((bf16[1,1,128,256]{3,2,1,0:T(8,128)(2,1)S(1)}, bf16[1,1,128,256]{3,2,1,0:T(8,128)(2,1)S(1)}, u32[]{:S(2)}, u32[]{:S(2)}) %collective-permute-start.11) | collective-permute-done | bytes 65568 | tf_op jit(solution)/shard_map/ppermute | solution.py:184
  33.2 1.0 %delay.3 = f32[2,384,128]{2,1,0:T(8,128)} custom-call(bf16[768,384]{1,0:T(8,128)(2,1)S(1)} %fold.1.refs_0_, f32[128,256]{1,0:T(8,128)S(1)} %select_bitcast_fusion.1.refs_1_, bf16[128,256]{1,0:T(8,128)(2,1)S(1)} %bitcast.28, f32[2,384,128]{2,1,0:T(8,128)S(1)} %delay.2.refs_3_), custom_call_target="tpu_custom_call" | custom-call | flops 1 | bytes 1 | tf_op jit(solution)/shard_map/delay/pallas_call | solution.py:291
  (19 shorter events, 0.3 us)
Async XLA Ops:
  0.0 5.1 %collective-permute-start.2 = (bf16[2,256,384]{2,1,0:T(8,128)(2,1)}, bf16[2,256,384]{2,1,0:T(8,128)(2,1)S(1)}, u32[]{:S(2)}, u32[]{:S(2)}) collective-permute-start(bf16[2,256,384]{2,1,0:T(8,128)(2,1)} %refs_0_.1), channel_id=1, source_target_pairs={{0,1},{1,0},{2,3},{3,2},{4,5},{5,4},{6,7},{7,6},{8,9},{9,8},{10,11... | collective-permute-start | bytes 1179656 | tf_op jit(solution)/shard_map/ppermute | solution.py:184
  2.0 5.2 %copy-start = (bf16[768,384]{1,0:T(8,128)(2,1)S(1)}, bf16[768,384]{1,0:T(8,128)(2,1)}, u32[]{:S(2)}) copy-start(bf16[768,384]{1,0:T(8,128)(2,1)} %constant.42.clone.tables) | copy-start | bytes 1769476
  2.0 3.1 %collective-permute-start = (bf16[288,256]{1,0:T(8,128)(2,1)S(1)}, bf16[288,256]{1,0:T(8,128)(2,1)S(1)}, u32[]{:S(2)}, u32[]{:S(2)}) collective-permute-start(bf16[288,256]{1,0:T(8,128)(2,1)S(1)} %get-tuple-element.29), channel_id=1, source_target_pairs={{0,1},{1,0},{2,3},{3,2},{4,5},{5,4},{6,7},{7,6},{8,9},{9,8},{10,11... | collective-permute-start | bytes 442376 | tf_op jit(solution)/shard_map/ppermute | solution.py:184
  2.1 8.2 %collective-permute-start.4 = (bf16[256,384]{1,0:T(8,128)(2,1)S(1)}, bf16[256,384]{1,0:T(8,128)(2,1)S(1)}, u32[]{:S(2)}, u32[]{:S(2)}) collective-permute-start(bf16[256,384]{1,0:T(8,128)(2,1)S(1)} %get-tuple-element.36.refs_3_), channel_id=1, source_target_pairs={{0,2},{1,3},{2,0},{3,1},{4,6},{5,7},{6,4},{7,5},{8,10},{9,11},{10,... | collective-permute-start | bytes 589832 | tf_op jit(solution)/shard_map/ppermute | solution.py:184
  5.1 2.1 %copy-start.1 = (bf16[384,384]{1,0:T(8,128)(2,1)S(1)}, bf16[384,384]{1,0:T(8,128)(2,1)}, u32[]{:S(2)}) copy-start(bf16[384,384]{1,0:T(8,128)(2,1)} %inv_cov) | copy-start | bytes 884740
  5.5 5.3 %collective-permute-start.5 = (bf16[2,2,128,128]{3,2,0,1:T(8,128)(2,1)S(1)}, bf16[2,2,128,128]{3,2,0,1:T(8,128)(2,1)S(1)}, u32[]{:S(2)}, u32[]{:S(2)}) collective-permute-start(bf16[2,2,128,128]{3,2,0,1:T(8,128)(2,1)S(1)} %copy.8), channel_id=1, source_target_pairs={{0,4},{1,5},{2,6},{3,7},{4,0},{5,1},{6,2},{7,3},{8,12},{9,13},{10,... | collective-permute-start | bytes 393224 | tf_op jit(solution)/shard_map/ppermute | solution.py:184
  7.8 8.3 %collective-permute-start.1 = (bf16[288,256]{1,0:T(8,128)(2,1)S(1)}, bf16[288,256]{1,0:T(8,128)(2,1)S(1)}, u32[]{:S(2)}, u32[]{:S(2)}) collective-permute-start(bf16[288,256]{1,0:T(8,128)(2,1)S(1)} %pad_maximum_fusion), channel_id=1, source_target_pairs={{0,2},{1,3},{2,0},{3,1},{4,6},{5,7},{6,4},{7,5},{8,10},{9,11},{10,... | collective-permute-start | bytes 442376 | tf_op jit(solution)/shard_map/ppermute | solution.py:184
  8.9 10.2 %collective-permute-start.3 = (bf16[256,256]{1,0:T(8,128)(2,1)S(1)}, bf16[256,256]{1,0:T(8,128)(2,1)S(1)}, u32[]{:S(2)}, u32[]{:S(2)}) collective-permute-start(bf16[256,256]{1,0:T(8,128)(2,1)S(1)} %get-tuple-element.35.refs_3_), channel_id=1, source_target_pairs={{0,2},{1,3},{2,0},{3,1},{4,6},{5,7},{6,4},{7,5},{8,10},{9,11},{10,... | collective-permute-start | bytes 393224 | tf_op jit(solution)/shard_map/ppermute | solution.py:184
  10.9 5.2 %collective-permute-start.12 = (bf16[2,1,128,128]{3,2,0,1:T(8,128)(2,1)S(1)}, bf16[2,1,128,128]{3,2,0,1:T(8,128)(2,1)S(1)}, u32[]{:S(2)}, u32[]{:S(2)}) collective-permute-start(bf16[2,1,128,128]{3,2,0,1:T(8,128)(2,1)S(1)} %fusion.3), channel_id=1, source_target_pairs={{0,8},{1,9},{2,10},{3,11},{4,12},{5,13},{6,14},{7,15},{8,0},{9,1},... | collective-permute-start | bytes 196616 | tf_op jit(solution)/shard_map/ppermute | solution.py:184
  13.6 2.6 %collective-permute-start.6 = (bf16[128,384]{1,0:T(8,128)(2,1)S(1)}, bf16[128,384]{1,0:T(8,128)(2,1)S(1)}, u32[]{:S(2)}, u32[]{:S(2)}) collective-permute-start(bf16[128,384]{1,0:T(8,128)(2,1)S(1)} %get-tuple-element.48), channel_id=1, source_target_pairs={{0,1},{1,0},{2,3},{3,2},{4,5},{5,4},{6,7},{7,6},{8,9},{9,8},{10,11... | collective-permute-start | bytes 294920 | tf_op jit(solution)/shard_map/ppermute | solution.py:184
  13.7 2.5 %collective-permute-start.7 = (bf16[128,384]{1,0:T(8,128)(2,1)S(1)}, bf16[128,384]{1,0:T(8,128)(2,1)S(1)}, u32[]{:S(2)}, u32[]{:S(2)}) collective-permute-start(bf16[128,384]{1,0:T(8,128)(2,1)S(1)} %get-tuple-element.47), channel_id=1, source_target_pairs={{0,1},{1,0},{2,3},{3,2},{4,5},{5,4},{6,7},{7,6},{8,9},{9,8},{10,11... | collective-permute-start | bytes 294920 | tf_op jit(solution)/shard_map/ppermute | solution.py:184
  16.9 6.5 %collective-permute-start.13 = (bf16[1,2,128,384]{3,2,1,0:T(8,128)(2,1)S(1)}, bf16[1,2,128,384]{3,2,1,0:T(8,128)(2,1)S(1)}, u32[]{:S(2)}, u32[]{:S(2)}) collective-permute-start(bf16[1,2,128,384]{3,2,1,0:T(8,128)(2,1)S(1)} %get-tuple-element.40), channel_id=1, source_target_pairs={{0,4},{1,5},{2,6},{3,7},{4,0},{5,1},{6,2},{7,3},{8,12},{9,13},{10,... | collective-permute-start | bytes 589832 | tf_op jit(solution)/shard_map/ppermute | solution.py:184
  19.1 1.3 %collective-permute-start.8 = (bf16[128,256]{1,0:T(8,128)(2,1)S(1)}, bf16[128,256]{1,0:T(8,128)(2,1)S(1)}, u32[]{:S(2)}, u32[]{:S(2)}) collective-permute-start(bf16[128,256]{1,0:T(8,128)(2,1)S(1)} %get-tuple-element.50), channel_id=1, source_target_pairs={{0,1},{1,0},{2,3},{3,2},{4,5},{5,4},{6,7},{7,6},{8,9},{9,8},{10,11... | collective-permute-start | bytes 196616 | tf_op jit(solution)/shard_map/ppermute | solution.py:184
  19.1 1.4 %collective-permute-start.9 = (bf16[128,256]{1,0:T(8,128)(2,1)S(1)}, bf16[128,256]{1,0:T(8,128)(2,1)S(1)}, u32[]{:S(2)}, u32[]{:S(2)}) collective-permute-start(bf16[128,256]{1,0:T(8,128)(2,1)S(1)} %get-tuple-element.49), channel_id=1, source_target_pairs={{0,1},{1,0},{2,3},{3,2},{4,5},{5,4},{6,7},{7,6},{8,9},{9,8},{10,11... | collective-permute-start | bytes 196616 | tf_op jit(solution)/shard_map/ppermute | solution.py:184
  21.0 6.9 %collective-permute-start.10 = (bf16[1,2,128,256]{3,2,1,0:T(8,128)(2,1)S(1)}, bf16[1,2,128,256]{3,2,1,0:T(8,128)(2,1)S(1)}, u32[]{:S(2)}, u32[]{:S(2)}) collective-permute-start(bf16[1,2,128,256]{3,2,1,0:T(8,128)(2,1)S(1)} %get-tuple-element.43), channel_id=1, source_target_pairs={{0,4},{1,5},{2,6},{3,7},{4,0},{5,1},{6,2},{7,3},{8,12},{9,13},{10,... | collective-permute-start | bytes 393224 | tf_op jit(solution)/shard_map/ppermute | solution.py:184
  23.4 6.8 %collective-permute-start.15 = (bf16[1,1,128,384]{3,2,1,0:T(8,128)(2,1)S(1)}, bf16[1,1,128,384]{3,2,1,0:T(8,128)(2,1)S(1)}, u32[]{:S(2)}, u32[]{:S(2)}) collective-permute-start(bf16[1,1,128,384]{3,2,1,0:T(8,128)(2,1)S(1)} %fusion.1), channel_id=1, source_target_pairs={{0,8},{1,9},{2,10},{3,11},{4,12},{5,13},{6,14},{7,15},{8,0},{9,1},... | collective-permute-start | bytes 294920 | tf_op jit(solution)/shard_map/ppermute | solution.py:184
  25.5 4.7 %collective-permute-start.14 = (bf16[128,128]{1,0:T(8,128)(2,1)S(1)}, bf16[128,128]{1,0:T(8,128)(2,1)S(1)}, u32[]{:S(2)}, u32[]{:S(2)}) collective-permute-start(bf16[128,128]{1,0:T(8,128)(2,1)S(1)} %fusion.4), channel_id=1, source_target_pairs={{0,2},{1,3},{2,0},{3,1},{4,6},{5,7},{6,4},{7,5},{8,10},{9,11},{10,... | collective-permute-start | bytes 98312 | tf_op jit(solution)/shard_map/ppermute | solution.py:184
  27.9 5.3 %collective-permute-start.11 = (bf16[1,1,128,256]{3,2,1,0:T(8,128)(2,1)S(1)}, bf16[1,1,128,256]{3,2,1,0:T(8,128)(2,1)S(1)}, u32[]{:S(2)}, u32[]{:S(2)}) collective-permute-start(bf16[1,1,128,256]{3,2,1,0:T(8,128)(2,1)S(1)} %fusion.2), channel_id=1, source_target_pairs={{0,8},{1,9},{2,10},{3,11},{4,12},{5,13},{6,14},{7,15},{8,0},{9,1},... | collective-permute-start | bytes 196616 | tf_op jit(solution)/shard_map/ppermute | solution.py:184

commit v5 on v4

--- a/solution.py
+++ b/solution.py
@@ -18,7 +18,8 @@
 PIECES = 2
 SECOND = (1, 0, 2)
 LAST = (2,)
-AFTER = {'relay1': ['grid0', 'got0'], 'relay2': ['grid1'], 'third0': ['grid1', 'second1'], 'over2': ['core']}
+HALVED = (1,)
+AFTER = {'relay1': ['grid0', 'got0'], 'relay2': ['grid1'], 'third0': ['grid1', 'second1'], 'over2': ['core'], 'sum0': ['grid1']}
 
 
 def delay_tables(channels):
@@ -209,6 +210,15 @@
     me = lax.axis_index("chan")
     vis_core = swap(visibilities, 1)
     core = swap(core, 1)
+    made["core"] = core
+    angles, early = tied("fold", delay_tables(channels), inv_cov)
+    folded = pl.pallas_call(
+        fold_body,
+        out_shape=shape((2 * channels, channels), bf16),
+        name="fold",
+        **options,
+    )(angles, early)
+    made["fold"] = folded
     tables, label = 2 * cells, 2 * cells + LABEL_ROWS
     far = [x[a:b] for a, b in ((cells, tables), (label, None)) for x in (own, core)]
     far = swap(jnp.concatenate(tied("far", *far)), 2)
@@ -237,7 +247,11 @@
         )(*operands)
         made[f"grid{n}"] = sends[0]
         sends = tied(f"first{n}", *sends)
-        arrived = [swap(send, (i + 1) * MAXB) for i, send in enumerate(sends)]
+        if n in HALVED:
+            halves = jnp.split(sends[0], 2, axis=1)
+            arrived = [jnp.concatenate([swap(half, MAXB) for half in halves], axis=1)]
+        else:
+            arrived = [swap(send, (i + 1) * MAXB) for i, send in enumerate(sends)]
         made[f"got{n}"] = arrived[0]
         return keep, arrived
 
@@ -270,6 +284,7 @@
             made[f"second{n}"] = send
             arrived = [swap(send, bit)]
             made[f"mid{n}"] = arrived[0]
+        arrived = tied(f"sum{n}", *arrived)
         keep, arrived = keep[:, 0], [piece[:, 0] for piece in arrived]
         if n in NEAR or len(arrived) > 1:
             keep = keep + sum(piece.astype(f32) for piece in arrived[: None if n in NEAR else -1])
@@ -277,15 +292,8 @@
         if n in NEAR:
             (send,) = tied(f"third{n}", keep[1].astype(bf16))
             arrived = [swap(send, 2)]
+            made[f"third{n}"] = arrived[0]
         held[n] = (keep[0], arrived[-1] if n in NEAR else arrived[-1][0])
-
-    tables, early = tied("fold", delay_tables(channels), inv_cov)
-    folded = pl.pallas_call(
-        fold_body,
-        out_shape=shape((2 * channels, channels), bf16),
-        name="fold",
-        **options,
-    )(tables, early)
 
     def delayed(chosen, last, *extra):
         return pl.pallas_call(

time: 34.4 us -> 34 us (0.988)
  waiting for transfers between devices: 9.42 us -> 7.24 us
  starting transfers between devices: 19.3 us -> 21 us
    ppermute x16 -> x17, waiting for transfers between devices: 9.42 us -> 7.24 us  [swap(): return lax.ppermute(values, 'chan', [(i, i ^ bit) for i in range(nblocks)])]
    ppermute x16 -> x17, starting transfers between devices: 19.3 us -> 21 us  [swap(): return lax.ppermute(values, 'chan', [(i, i ^ bit) for i in range(nblocks)])]
  transfers between devices with their start and end apart: 16 -> 17, of which waited for: 8 -> 8; matrix products, arithmetic and copies ran while one was open for 1% -> 1% of each run, Pallas kernels for 12% -> 12%
where the time goes in v5:
time: 34 us; the launch traced here: 33.8 us
  starting transfers between devices  21 us (62%)
  waiting for transfers between devices  7.24 us (21%)
  Pallas kernels  5.01 us (15%)
    ppermute x17, starting transfers between devices, swap(): return lax.ppermute(values, 'chan', [(i, i ^ bit) for i in range(nblocks)])  21 us
    ppermute x17, waiting for transfers between devices, swap(): return lax.ppermute(values, 'chan', [(i, i ^ bit) for i in range(nblocks)])  7.24 us
    pallas_call x3, Pallas kernels, grid(): pl.pallas_call(lambda *refs: grid_body(groups, n, *refs), out_shape=outs,...  1.62 us
    pallas_call x1, Pallas kernels, on_device(): pl.pallas_call(lambda *refs: prep_body(nblocks, *refs), in_specs=[hbm] *...  1.5 us
    pallas_call x2, Pallas kernels, delayed(): pl.pallas_call(lambda *refs: delay_body([PLAN[n] for n in chosen], last,...  1.39 us
  transfers between devices with their start and end apart: 17, of which 8 were waited for; matrix products, arithmetic and copies ran while one was open for 1% of the time, Pallas kernels for 12%

profile of v5, /device:TPU:0, one launch (start us, length us, event | category | flops | bytes accessed | tf_op | source)
XLA Modules:
  0.0 33.8 jit_solution(7836680101202196763)
XLA Ops:
  0.0 0.5 %collective-permute-start.2 = (bf16[2,256,384]{2,1,0:T(8,128)(2,1)}, bf16[2,256,384]{2,1,0:T(8,128)(2,1)S(1)}, u32[]{:S(2)}, u32[]{:S(2)}) collective-permute-start(bf16[2,256,384]{2,1,0:T(8,128)(2,1)} %refs_0_.1), channel_id=1, source_target_pairs={{0,1},{1,0},{2,3},{3,2},{4,5},{5,4},{6,7},{7,6},{8,9},{9,8},{10,11... | collective-permute-start | bytes 1179656 | tf_op jit(solution)/shard_map/ppermute | solution.py:185
  0.5 1.5 %prep.1 = (bf16[288,256]{1,0:T(8,128)(2,1)S(1)}, bf16[288,256]{1,0:T(8,128)(2,1)S(1)}, bf16[256,128]{1,0:T(8,128)(2,1)S(1)}, bf16[256,384]{1,0:T(8,128)(2,1)S(1)}, bf16[256,256]{1,0:T(8,128)(2,1)S(1)}) custom-call(bf16[2,256,384]{2,1,0:T(8,128)(2,1)} %refs_0_.1, bf16[4,256,128]{2,1,0:T(8,128)(2,1)} %refs_1_.1, s32[256]{0:T(256)} %refs_2_.1, s32[256]{0:T(256)} %refs_3_.1, ...), custom_call_target="tpu_custom_call" | custom-call | flops 1 | bytes 1 | tf_op jit(solution)/shard_map/prep/pallas_call | solution.py:193
  2.0 0.0 copy-start
  2.0 0.1 collective-permute-start
  2.1 3.0 %collective-permute-start.4 = (bf16[256,384]{1,0:T(8,128)(2,1)S(1)}, bf16[256,384]{1,0:T(8,128)(2,1)S(1)}, u32[]{:S(2)}, u32[]{:S(2)}) collective-permute-start(bf16[256,384]{1,0:T(8,128)(2,1)S(1)} %get-tuple-element.37.refs_3_), channel_id=1, source_target_pairs={{0,2},{1,3},{2,0},{3,1},{4,6},{5,7},{6,4},{7,5},{8,10},{9,11},{10,... | collective-permute-start | bytes 589832 | tf_op jit(solution)/shard_map/ppermute | solution.py:185
  5.1 0.0 collective-permute-done.refs_1_
  5.1 0.0 collective-permute-done.2.refs_3_.refs_4_
  5.1 0.0 copy-start.1
  5.1 0.4 %grid.3 = (f32[2,2,128,128]{3,2,1,0:T(8,128)S(1)}, bf16[2,2,128,128]{3,2,1,0:T(8,128)(2,1)S(1)}) custom-call(bf16[288,256]{1,0:T(8,128)(2,1)S(1)} %get-tuple-element.29.refs_0_, bf16[288,256]{1,0:T(8,128)(2,1)S(1)} %collective-permute-done.refs_1_, bf16[256,128]{1,0:T(8,128)(2,1)S(1)} %get-tuple-element.38.refs_2_, ...), custom_call_target="tpu_custom_call" | custom-call | flops 1 | bytes 1 | tf_op jit(solution)/shard_map/grid/pallas_call | solution.py:238
  5.5 1.6 %collective-permute-start.5 = (bf16[2,2,128,128]{3,2,0,1:T(8,128)(2,1)S(1)}, bf16[2,2,128,128]{3,2,0,1:T(8,128)(2,1)S(1)}, u32[]{:S(2)}, u32[]{:S(2)}) collective-permute-start(bf16[2,2,128,128]{3,2,0,1:T(8,128)(2,1)S(1)} %copy.8), channel_id=1, source_target_pairs={{0,4},{1,5},{2,6},{3,7},{4,0},{5,1},{6,2},{7,3},{8,12},{9,13},{10,... | collective-permute-start | bytes 393224 | tf_op jit(solution)/shard_map/ppermute | solution.py:185
  7.2 0.0 copy-done
  7.2 0.0 copy-done.1
  7.2 0.5 %fold.1.refs_0_ = bf16[768,384]{1,0:T(8,128)(2,1)S(1)} custom-call(bf16[768,384]{1,0:T(8,128)(2,1)S(1)} %copy-done, bf16[384,384]{1,0:T(8,128)(2,1)S(1)} %copy-done.1), custom_call_target="tpu_custom_call" | custom-call | flops 1 | bytes 1 | tf_op jit(solution)/shard_map/fold/pallas_call | solution.py:215
  7.8 1.1 %collective-permute-start.1 = (bf16[288,256]{1,0:T(8,128)(2,1)S(1)}, bf16[288,256]{1,0:T(8,128)(2,1)S(1)}, u32[]{:S(2)}, u32[]{:S(2)}) collective-permute-start(bf16[288,256]{1,0:T(8,128)(2,1)S(1)} %pad_maximum_fusion.1), channel_id=1, source_target_pairs={{0,2},{1,3},{2,0},{3,1},{4,6},{5,7},{6,4},{7,5},{8,10},{9,11},{10,... | collective-permute-start | bytes 442376 | tf_op jit(solution)/shard_map/ppermute | solution.py:185
  8.9 1.0 %collective-permute-start.3 = (bf16[256,256]{1,0:T(8,128)(2,1)S(1)}, bf16[256,256]{1,0:T(8,128)(2,1)S(1)}, u32[]{:S(2)}, u32[]{:S(2)}) collective-permute-start(bf16[256,256]{1,0:T(8,128)(2,1)S(1)} %get-tuple-element.36.refs_3_), channel_id=1, source_target_pairs={{0,2},{1,3},{2,0},{3,1},{4,6},{5,7},{6,4},{7,5},{8,10},{9,11},{10,... | collective-permute-start | bytes 393224 | tf_op jit(solution)/shard_map/ppermute | solution.py:185
  9.9 0.4 %collective-permute-done.4.refs_5_ = bf16[256,384]{1,0:T(8,128)(2,1)S(1)} collective-permute-done((bf16[256,384]{1,0:T(8,128)(2,1)S(1)}, bf16[256,384]{1,0:T(8,128)(2,1)S(1)}, u32[]{:S(2)}, u32[]{:S(2)}) %collective-permute-start.4) | collective-permute-done | bytes 196640 | tf_op jit(solution)/shard_map/ppermute | solution.py:185
  10.3 0.5 %collective-permute-done.5 = bf16[2,2,128,128]{3,2,0,1:T(8,128)(2,1)S(1)} collective-permute-done((bf16[2,2,128,128]{3,2,0,1:T(8,128)(2,1)S(1)}, bf16[2,2,128,128]{3,2,0,1:T(8,128)(2,1)S(1)}, u32[]{:S(2)}, u32[]{:S(2)}) %collective-permute-start.5) | collective-permute-done | bytes 131104 | tf_op jit(solution)/shard_map/ppermute | solution.py:185
  10.8 0.1 collective-permute-start.6
  10.9 0.5 %collective-permute-start.7 = (bf16[128,384]{1,0:T(8,128)(2,1)S(1)}, bf16[128,384]{1,0:T(8,128)(2,1)S(1)}, u32[]{:S(2)}, u32[]{:S(2)}) collective-permute-start(bf16[128,384]{1,0:T(8,128)(2,1)S(1)} %get-tuple-element.51), channel_id=1, source_target_pairs={{0,1},{1,0},{2,3},{3,2},{4,5},{5,4},{6,7},{7,6},{8,9},{9,8},{10,11... | collective-permute-start | bytes 294920 | tf_op jit(solution)/shard_map/ppermute | solution.py:185
  11.5 2.7 %collective-permute-start.12 = (bf16[2,1,128,128]{3,2,0,1:T(8,128)(2,1)S(1)}, bf16[2,1,128,128]{3,2,0,1:T(8,128)(2,1)S(1)}, u32[]{:S(2)}, u32[]{:S(2)}) collective-permute-start(bf16[2,1,128,128]{3,2,0,1:T(8,128)(2,1)S(1)} %fusion.3), channel_id=1, source_target_pairs={{0,8},{1,9},{2,10},{3,11},{4,12},{5,13},{6,14},{7,15},{8,0},{9,1},... | collective-permute-start | bytes 196616 | tf_op jit(solution)/shard_map/ppermute | solution.py:185
  14.2 0.5 %collective-permute-done.1.refs_2_ = bf16[288,256]{1,0:T(8,128)(2,1)S(1)} collective-permute-done((bf16[288,256]{1,0:T(8,128)(2,1)S(1)}, bf16[288,256]{1,0:T(8,128)(2,1)S(1)}, u32[]{:S(2)}, u32[]{:S(2)}) %collective-permute-start.1) | collective-permute-done | bytes 147488 | tf_op jit(solution)/shard_map/ppermute | solution.py:185
  14.6 0.0 collective-permute-done.6.refs_6_
  14.6 0.0 collective-permute-done.7.refs_7_
  14.6 0.7 %grid.4 = (f32[1,2,128,384]{3,2,1,0:T(8,128)S(1)}, bf16[1,2,128,384]{3,2,1,0:T(8,128)(2,1)S(1)}) custom-call(bf16[288,256]{1,0:T(8,128)(2,1)S(1)} %get-tuple-element.29.refs_0_, bf16[288,256]{1,0:T(8,128)(2,1)S(1)} %collective-permute-done.refs_1_, bf16[288,256]{1,0:T(8,128)(2,1)S(1)} %collective-permute-done.1.refs_2_, ...), custom_call_target="tpu_custom_call" | custom-call | flops 1 | bytes 1 | tf_op jit(solution)/shard_map/grid/pallas_call | solution.py:238
  15.4 1.6 %collective-permute-start.13 = (bf16[1,1,128,384]{3,2,1,0:T(8,128)(2,1)S(1)}, bf16[1,1,128,384]{3,2,1,0:T(8,128)(2,1)S(1)}, u32[]{:S(2)}, u32[]{:S(2)}) collective-permute-start(bf16[1,1,128,384]{3,2,1,0:T(8,128)(2,1)S(1)} %get-tuple-element.49), channel_id=1, source_target_pairs={{0,4},{1,5},{2,6},{3,7},{4,0},{5,1},{6,2},{7,3},{8,12},{9,13},{10,... | collective-permute-start | bytes 294920 | tf_op jit(solution)/shard_map/ppermute | solution.py:185
  17.0 0.5 %collective-permute-start.14 = (bf16[1,1,128,384]{3,2,1,0:T(8,128)(2,1)S(1)}, bf16[1,1,128,384]{3,2,1,0:T(8,128)(2,1)S(1)}, u32[]{:S(2)}, u32[]{:S(2)}) collective-permute-start(bf16[1,1,128,384]{3,2,1,0:T(8,128)(2,1)S(1)} %get-tuple-element.50), channel_id=1, source_target_pairs={{0,4},{1,5},{2,6},{3,7},{4,0},{5,1},{6,2},{7,3},{8,12},{9,13},{10,... | collective-permute-start | bytes 294920 | tf_op jit(solution)/shard_map/ppermute | solution.py:185
  17.5 0.0 collective-permute-done.12
  17.6 0.0 collective-permute-done.3.refs_5_
  17.6 0.1 collective-permute-start.8
  17.7 0.5 %collective-permute-start.9 = (bf16[128,256]{1,0:T(8,128)(2,1)S(1)}, bf16[128,256]{1,0:T(8,128)(2,1)S(1)}, u32[]{:S(2)}, u32[]{:S(2)}) collective-permute-start(bf16[128,256]{1,0:T(8,128)(2,1)S(1)} %get-tuple-element.53), channel_id=1, source_target_pairs={{0,1},{1,0},{2,3},{3,2},{4,5},{5,4},{6,7},{7,6},{8,9},{9,8},{10,11... | collective-permute-start | bytes 196616 | tf_op jit(solution)/shard_map/ppermute | solution.py:185
  18.2 0.7 %collective-permute-done.8.refs_6_ = bf16[128,256]{1,0:T(8,128)(2,1)S(1)} collective-permute-done((bf16[128,256]{1,0:T(8,128)(2,1)S(1)}, bf16[128,256]{1,0:T(8,128)(2,1)S(1)}, u32[]{:S(2)}, u32[]{:S(2)}) %collective-permute-start.8) | collective-permute-done | bytes 65568 | tf_op jit(solution)/shard_map/ppermute | solution.py:185
  18.9 0.2 collective-permute-done.9.refs_7_
  19.1 0.4 %grid.5 = (f32[1,2,128,256]{3,2,1,0:T(8,128)S(1)}, bf16[1,2,128,256]{3,2,1,0:T(8,128)(2,1)S(1)}) custom-call(bf16[288,256]{1,0:T(8,128)(2,1)S(1)} %get-tuple-element.29.refs_0_, bf16[288,256]{1,0:T(8,128)(2,1)S(1)} %collective-permute-done.refs_1_, bf16[288,256]{1,0:T(8,128)(2,1)S(1)} %collective-permute-done.1.refs_2_, ...), custom_call_target="tpu_custom_call" | custom-call | flops 1 | bytes 1 | tf_op jit(solution)/shard_map/grid/pallas_call | solution.py:238
  19.5 1.6 %collective-permute-start.10 = (bf16[1,2,128,256]{3,2,1,0:T(8,128)(2,1)S(1)}, bf16[1,2,128,256]{3,2,1,0:T(8,128)(2,1)S(1)}, u32[]{:S(2)}, u32[]{:S(2)}) collective-permute-start(bf16[1,2,128,256]{3,2,1,0:T(8,128)(2,1)S(1)} %get-tuple-element.44), channel_id=1, source_target_pairs={{0,4},{1,5},{2,6},{3,7},{4,0},{5,1},{6,2},{7,3},{8,12},{9,13},{10,... | collective-permute-start | bytes 393224 | tf_op jit(solution)/shard_map/ppermute | solution.py:185
  21.1 0.0 collective-permute-done.13
  21.1 1.1 %collective-permute-done.14 = bf16[1,1,128,384]{3,2,1,0:T(8,128)(2,1)S(1)} collective-permute-done((bf16[1,1,128,384]{3,2,1,0:T(8,128)(2,1)S(1)}, bf16[1,1,128,384]{3,2,1,0:T(8,128)(2,1)S(1)}, u32[]{:S(2)}, u32[]{:S(2)}) %collective-permute-start.14) | collective-permute-done | bytes 98336 | tf_op jit(solution)/shard_map/ppermute | solution.py:185
  22.3 2.0 %collective-permute-start.16 = (bf16[1,1,128,384]{3,2,1,0:T(8,128)(2,1)S(1)}, bf16[1,1,128,384]{3,2,1,0:T(8,128)(2,1)S(1)}, u32[]{:S(2)}, u32[]{:S(2)}) collective-permute-start(bf16[1,1,128,384]{3,2,1,0:T(8,128)(2,1)S(1)} %fusion.1), channel_id=1, source_target_pairs={{0,8},{1,9},{2,10},{3,11},{4,12},{5,13},{6,14},{7,15},{8,0},{9,1},... | collective-permute-start | bytes 294920 | tf_op jit(solution)/shard_map/ppermute | solution.py:185
  24.3 1.5 %collective-permute-start.15 = (bf16[128,128]{1,0:T(8,128)(2,1)S(1)}, bf16[128,128]{1,0:T(8,128)(2,1)S(1)}, u32[]{:S(2)}, u32[]{:S(2)}) collective-permute-start(bf16[128,128]{1,0:T(8,128)(2,1)S(1)} %fusion.4), channel_id=1, source_target_pairs={{0,2},{1,3},{2,0},{3,1},{4,6},{5,7},{6,4},{7,5},{8,10},{9,11},{10,... | collective-permute-start | bytes 98312 | tf_op jit(solution)/shard_map/ppermute | solution.py:185
  25.9 0.0 collective-permute-done.10
  26.0 2.6 %collective-permute-start.11 = (bf16[1,1,128,256]{3,2,1,0:T(8,128)(2,1)S(1)}, bf16[1,1,128,256]{3,2,1,0:T(8,128)(2,1)S(1)}, u32[]{:S(2)}, u32[]{:S(2)}) collective-permute-start(bf16[1,1,128,256]{3,2,1,0:T(8,128)(2,1)S(1)} %fusion.2), channel_id=1, source_target_pairs={{0,8},{1,9},{2,10},{3,11},{4,12},{5,13},{6,14},{7,15},{8,0},{9,1},... | collective-permute-start | bytes 196616 | tf_op jit(solution)/shard_map/ppermute | solution.py:185
  28.6 1.5 %collective-permute-done.16 = bf16[1,1,128,384]{3,2,1,0:T(8,128)(2,1)S(1)} collective-permute-done((bf16[1,1,128,384]{3,2,1,0:T(8,128)(2,1)S(1)}, bf16[1,1,128,384]{3,2,1,0:T(8,128)(2,1)S(1)}, u32[]{:S(2)}, u32[]{:S(2)}) %collective-permute-start.16) | collective-permute-done | bytes 98336 | tf_op jit(solution)/shard_map/ppermute | solution.py:185
  30.1 0.0 collective-permute-done.15.refs_2_
  30.1 0.4 %delay.2.refs_3_ = f32[2,384,128]{2,1,0:T(8,128)S(1)} custom-call(bf16[768,384]{1,0:T(8,128)(2,1)S(1)} %fold.1.refs_0_, f32[128,128]{1,0:T(8,128)S(1)} %slice_bitcast_fusion.refs_1_, bf16[128,128]{1,0:T(8,128)(2,1)S(1)} %collective-permute-done.15.refs_2_, f32[128,384]{1,0:T(8,128)S(1)} %select_bitcast_fusion.refs_3_, bf16[128,384]{1,0:T(8,128)(2,1)S(1)} %bitcast.27), custom_call_target="tpu_custom_call" | custom-call | flops 1 | bytes 1 | tf_op jit(solution)/shard_map/delay/pallas_call | solution.py:299
  30.5 2.3 %collective-permute-done.11 = bf16[1,1,128,256]{3,2,1,0:T(8,128)(2,1)S(1)} collective-permute-done((bf16[1,1,128,256]{3,2,1,0:T(8,128)(2,1)S(1)}, bf16[1,1,128,256]{3,2,1,0:T(8,128)(2,1)S(1)}, u32[]{:S(2)}, u32[]{:S(2)}) %collective-permute-start.11) | collective-permute-done | bytes 65568 | tf_op jit(solution)/shard_map/ppermute | solution.py:185
  32.8 1.0 %delay.3 = f32[2,384,128]{2,1,0:T(8,128)} custom-call(bf16[768,384]{1,0:T(8,128)(2,1)S(1)} %fold.1.refs_0_, f32[128,256]{1,0:T(8,128)S(1)} %select_bitcast_fusion.1.refs_1_, bf16[128,256]{1,0:T(8,128)(2,1)S(1)} %bitcast.28, f32[2,384,128]{2,1,0:T(8,128)S(1)} %delay.2.refs_3_), custom_call_target="tpu_custom_call" | custom-call | flops 1 | bytes 1 | tf_op jit(solution)/shard_map/delay/pallas_call | solution.py:299
  (21 shorter events, 0.3 us)
Async XLA Ops:
  0.0 5.1 %collective-permute-start.2 = (bf16[2,256,384]{2,1,0:T(8,128)(2,1)}, bf16[2,256,384]{2,1,0:T(8,128)(2,1)S(1)}, u32[]{:S(2)}, u32[]{:S(2)}) collective-permute-start(bf16[2,256,384]{2,1,0:T(8,128)(2,1)} %refs_0_.1), channel_id=1, source_target_pairs={{0,1},{1,0},{2,3},{3,2},{4,5},{5,4},{6,7},{7,6},{8,9},{9,8},{10,11... | collective-permute-start | bytes 1179656 | tf_op jit(solution)/shard_map/ppermute | solution.py:185
  2.0 5.2 %copy-start = (bf16[768,384]{1,0:T(8,128)(2,1)S(1)}, bf16[768,384]{1,0:T(8,128)(2,1)}, u32[]{:S(2)}) copy-start(bf16[768,384]{1,0:T(8,128)(2,1)} %constant.42.clone.tables) | copy-start | bytes 1769476
  2.0 3.1 %collective-permute-start = (bf16[288,256]{1,0:T(8,128)(2,1)S(1)}, bf16[288,256]{1,0:T(8,128)(2,1)S(1)}, u32[]{:S(2)}, u32[]{:S(2)}) collective-permute-start(bf16[288,256]{1,0:T(8,128)(2,1)S(1)} %get-tuple-element.30), channel_id=1, source_target_pairs={{0,1},{1,0},{2,3},{3,2},{4,5},{5,4},{6,7},{7,6},{8,9},{9,8},{10,11... | collective-permute-start | bytes 442376 | tf_op jit(solution)/shard_map/ppermute | solution.py:185
  2.1 8.2 %collective-permute-start.4 = (bf16[256,384]{1,0:T(8,128)(2,1)S(1)}, bf16[256,384]{1,0:T(8,128)(2,1)S(1)}, u32[]{:S(2)}, u32[]{:S(2)}) collective-permute-start(bf16[256,384]{1,0:T(8,128)(2,1)S(1)} %get-tuple-element.37.refs_3_), channel_id=1, source_target_pairs={{0,2},{1,3},{2,0},{3,1},{4,6},{5,7},{6,4},{7,5},{8,10},{9,11},{10,... | collective-permute-start | bytes 589832 | tf_op jit(solution)/shard_map/ppermute | solution.py:185
  5.1 2.1 %copy-start.1 = (bf16[384,384]{1,0:T(8,128)(2,1)S(1)}, bf16[384,384]{1,0:T(8,128)(2,1)}, u32[]{:S(2)}) copy-start(bf16[384,384]{1,0:T(8,128)(2,1)} %inv_cov) | copy-start | bytes 884740
  5.5 5.3 %collective-permute-start.5 = (bf16[2,2,128,128]{3,2,0,1:T(8,128)(2,1)S(1)}, bf16[2,2,128,128]{3,2,0,1:T(8,128)(2,1)S(1)}, u32[]{:S(2)}, u32[]{:S(2)}) collective-permute-start(bf16[2,2,128,128]{3,2,0,1:T(8,128)(2,1)S(1)} %copy.8), channel_id=1, source_target_pairs={{0,4},{1,5},{2,6},{3,7},{4,0},{5,1},{6,2},{7,3},{8,12},{9,13},{10,... | collective-permute-start | bytes 393224 | tf_op jit(solution)/shard_map/ppermute | solution.py:185
  7.8 6.8 %collective-permute-start.1 = (bf16[288,256]{1,0:T(8,128)(2,1)S(1)}, bf16[288,256]{1,0:T(8,128)(2,1)S(1)}, u32[]{:S(2)}, u32[]{:S(2)}) collective-permute-start(bf16[288,256]{1,0:T(8,128)(2,1)S(1)} %pad_maximum_fusion.1), channel_id=1, source_target_pairs={{0,2},{1,3},{2,0},{3,1},{4,6},{5,7},{6,4},{7,5},{8,10},{9,11},{10,... | collective-permute-start | bytes 442376 | tf_op jit(solution)/shard_map/ppermute | solution.py:185
  8.9 8.7 %collective-permute-start.3 = (bf16[256,256]{1,0:T(8,128)(2,1)S(1)}, bf16[256,256]{1,0:T(8,128)(2,1)S(1)}, u32[]{:S(2)}, u32[]{:S(2)}) collective-permute-start(bf16[256,256]{1,0:T(8,128)(2,1)S(1)} %get-tuple-element.36.refs_3_), channel_id=1, source_target_pairs={{0,2},{1,3},{2,0},{3,1},{4,6},{5,7},{6,4},{7,5},{8,10},{9,11},{10,... | collective-permute-start | bytes 393224 | tf_op jit(solution)/shard_map/ppermute | solution.py:185
  10.8 3.8 %collective-permute-start.6 = (bf16[128,384]{1,0:T(8,128)(2,1)S(1)}, bf16[128,384]{1,0:T(8,128)(2,1)S(1)}, u32[]{:S(2)}, u32[]{:S(2)}) collective-permute-start(bf16[128,384]{1,0:T(8,128)(2,1)S(1)} %get-tuple-element.52), channel_id=1, source_target_pairs={{0,1},{1,0},{2,3},{3,2},{4,5},{5,4},{6,7},{7,6},{8,9},{9,8},{10,11... | collective-permute-start | bytes 294920 | tf_op jit(solution)/shard_map/ppermute | solution.py:185
  10.9 3.7 %collective-permute-start.7 = (bf16[128,384]{1,0:T(8,128)(2,1)S(1)}, bf16[128,384]{1,0:T(8,128)(2,1)S(1)}, u32[]{:S(2)}, u32[]{:S(2)}) collective-permute-start(bf16[128,384]{1,0:T(8,128)(2,1)S(1)} %get-tuple-element.51), channel_id=1, source_target_pairs={{0,1},{1,0},{2,3},{3,2},{4,5},{5,4},{6,7},{7,6},{8,9},{9,8},{10,11... | collective-permute-start | bytes 294920 | tf_op jit(solution)/shard_map/ppermute | solution.py:185
  11.5 6.1 %collective-permute-start.12 = (bf16[2,1,128,128]{3,2,0,1:T(8,128)(2,1)S(1)}, bf16[2,1,128,128]{3,2,0,1:T(8,128)(2,1)S(1)}, u32[]{:S(2)}, u32[]{:S(2)}) collective-permute-start(bf16[2,1,128,128]{3,2,0,1:T(8,128)(2,1)S(1)} %fusion.3), channel_id=1, source_target_pairs={{0,8},{1,9},{2,10},{3,11},{4,12},{5,13},{6,14},{7,15},{8,0},{9,1},... | collective-permute-start | bytes 196616 | tf_op jit(solution)/shard_map/ppermute | solution.py:185
  15.4 5.7 %collective-permute-start.13 = (bf16[1,1,128,384]{3,2,1,0:T(8,128)(2,1)S(1)}, bf16[1,1,128,384]{3,2,1,0:T(8,128)(2,1)S(1)}, u32[]{:S(2)}, u32[]{:S(2)}) collective-permute-start(bf16[1,1,128,384]{3,2,1,0:T(8,128)(2,1)S(1)} %get-tuple-element.49), channel_id=1, source_target_pairs={{0,4},{1,5},{2,6},{3,7},{4,0},{5,1},{6,2},{7,3},{8,12},{9,13},{10,... | collective-permute-start | bytes 294920 | tf_op jit(solution)/shard_map/ppermute | solution.py:185
  17.0 5.2 %collective-permute-start.14 = (bf16[1,1,128,384]{3,2,1,0:T(8,128)(2,1)S(1)}, bf16[1,1,128,384]{3,2,1,0:T(8,128)(2,1)S(1)}, u32[]{:S(2)}, u32[]{:S(2)}) collective-permute-start(bf16[1,1,128,384]{3,2,1,0:T(8,128)(2,1)S(1)} %get-tuple-element.50), channel_id=1, source_target_pairs={{0,4},{1,5},{2,6},{3,7},{4,0},{5,1},{6,2},{7,3},{8,12},{9,13},{10,... | collective-permute-start | bytes 294920 | tf_op jit(solution)/shard_map/ppermute | solution.py:185
  17.6 1.3 %collective-permute-start.8 = (bf16[128,256]{1,0:T(8,128)(2,1)S(1)}, bf16[128,256]{1,0:T(8,128)(2,1)S(1)}, u32[]{:S(2)}, u32[]{:S(2)}) collective-permute-start(bf16[128,256]{1,0:T(8,128)(2,1)S(1)} %get-tuple-element.54), channel_id=1, source_target_pairs={{0,1},{1,0},{2,3},{3,2},{4,5},{5,4},{6,7},{7,6},{8,9},{9,8},{10,11... | collective-permute-start | bytes 196616 | tf_op jit(solution)/shard_map/ppermute | solution.py:185
  17.7 1.4 %collective-permute-start.9 = (bf16[128,256]{1,0:T(8,128)(2,1)S(1)}, bf16[128,256]{1,0:T(8,128)(2,1)S(1)}, u32[]{:S(2)}, u32[]{:S(2)}) collective-permute-start(bf16[128,256]{1,0:T(8,128)(2,1)S(1)} %get-tuple-element.53), channel_id=1, source_target_pairs={{0,1},{1,0},{2,3},{3,2},{4,5},{5,4},{6,7},{7,6},{8,9},{9,8},{10,11... | collective-permute-start | bytes 196616 | tf_op jit(solution)/shard_map/ppermute | solution.py:185
  19.5 6.4 %collective-permute-start.10 = (bf16[1,2,128,256]{3,2,1,0:T(8,128)(2,1)S(1)}, bf16[1,2,128,256]{3,2,1,0:T(8,128)(2,1)S(1)}, u32[]{:S(2)}, u32[]{:S(2)}) collective-permute-start(bf16[1,2,128,256]{3,2,1,0:T(8,128)(2,1)S(1)} %get-tuple-element.44), channel_id=1, source_target_pairs={{0,4},{1,5},{2,6},{3,7},{4,0},{5,1},{6,2},{7,3},{8,12},{9,13},{10,... | collective-permute-start | bytes 393224 | tf_op jit(solution)/shard_map/ppermute | solution.py:185
  22.3 7.8 %collective-permute-start.16 = (bf16[1,1,128,384]{3,2,1,0:T(8,128)(2,1)S(1)}, bf16[1,1,128,384]{3,2,1,0:T(8,128)(2,1)S(1)}, u32[]{:S(2)}, u32[]{:S(2)}) collective-permute-start(bf16[1,1,128,384]{3,2,1,0:T(8,128)(2,1)S(1)} %fusion.1), channel_id=1, source_target_pairs={{0,8},{1,9},{2,10},{3,11},{4,12},{5,13},{6,14},{7,15},{8,0},{9,1},... | collective-permute-start | bytes 294920 | tf_op jit(solution)/shard_map/ppermute | solution.py:185
  24.3 5.8 %collective-permute-start.15 = (bf16[128,128]{1,0:T(8,128)(2,1)S(1)}, bf16[128,128]{1,0:T(8,128)(2,1)S(1)}, u32[]{:S(2)}, u32[]{:S(2)}) collective-permute-start(bf16[128,128]{1,0:T(8,128)(2,1)S(1)} %fusion.4), channel_id=1, source_target_pairs={{0,2},{1,3},{2,0},{3,1},{4,6},{5,7},{6,4},{7,5},{8,10},{9,11},{10,... | collective-permute-start | bytes 98312 | tf_op jit(solution)/shard_map/ppermute | solution.py:185
  26.0 6.8 %collective-permute-start.11 = (bf16[1,1,128,256]{3,2,1,0:T(8,128)(2,1)S(1)}, bf16[1,1,128,256]{3,2,1,0:T(8,128)(2,1)S(1)}, u32[]{:S(2)}, u32[]{:S(2)}) collective-permute-start(bf16[1,1,128,256]{3,2,1,0:T(8,128)(2,1)S(1)} %fusion.2), channel_id=1, source_target_pairs={{0,8},{1,9},{2,10},{3,11},{4,12},{5,13},{6,14},{7,15},{8,0},{9,1},... | collective-permute-start | bytes 196616 | tf_op jit(solution)/shard_map/ppermute | solution.py:185
